TPU v7x, 512 devices: a whole 4x4x16 slice. The times are simulated.
512 devices in a mesh: expert: 64 (over z_hi, y, x), tensor: 8 (over z_lo, core).
Axes of the slice: x: 4, y: 4, z: 16 (z_hi: 4, z_lo: 4; z = z_hi * 4 + z_lo), core: 2. Of those that a mesh axis runs over, the one named last changes fastest.
Arguments:
- grad_out: bfloat16 [32768, 3072], P('expert', 'tensor'), may hold values from -6 to 6
- hidden_in: bfloat16 [32768, 4096], P('expert', 'tensor')
- gate_prob: float32 [32768], P('expert'), may hold values from 0.1 to 1
- expert_ids: int32 [32768, 1], P('expert'), may hold values from 0 to 63; in each aligned block of 512 rows (0 to 511, 512 to 1023, ...) at most 16 rows name the same one
- w_down: bfloat16 [64, 4096, 3072], P('expert', 'tensor'), may hold values from -0.09375 to 0.09375
Outputs:
- grad_hidden: bfloat16 [32768, 4096], P('expert', 'tensor')
- grad_gate: float32 [32768], P('expert')
Inputs may be any that keep to these rules, and one draw needn't show every extreme that they name: `expert_ids`: in each aligned block of 512 tokens no expert is named more than 16 times, a bound that some block reaches.
All inputs are finite; a program needn't handle non-finite values.
Results may differ from a plain program's by a relative error of at most 0.0049.
Values may be sent and summed in bfloat16 or wider, within the bound.
No kernel may reach another device: no remote copies, remote signals or barrier semaphores. Data moves between devices by JAX's collectives and lax.ppermute only.
A program may use at most 64 MiB of HBM per device.

v0:
```python
import jax
import jax.numpy as jnp
from jax import lax
from jax.sharding import PartitionSpec as P


def token_slots(expert_ids, experts, capacity):
    chosen = expert_ids[:, 0]
    onehot = (chosen[:, None] == jnp.arange(experts, dtype=jnp.int32)[None, :]).astype(jnp.int32)
    earlier = jnp.sum((jnp.cumsum(onehot, axis=0) - 1) * onehot, axis=1)
    return chosen * capacity + earlier


def body(grad_out, hidden_in, gate_prob, expert_ids, w_down):
    tokens = grad_out.shape[0]
    groups = lax.axis_size("expert")
    local = w_down.shape[0]
    experts = local * groups
    capacity = 2 * tokens // experts
    target = token_slots(expert_ids, experts, capacity)
    source = (
        jnp.full((experts * capacity,), tokens, jnp.int32)
        .at[target]
        .set(jnp.arange(tokens, dtype=jnp.int32))
    )
    outgoing = lax.all_gather(grad_out, "tensor", axis=1, tiled=True)
    padded = jnp.concatenate([outgoing, jnp.zeros((1, outgoing.shape[1]), outgoing.dtype)], axis=0)
    send = padded[source].reshape(experts, capacity, outgoing.shape[1])
    received = lax.all_to_all(send, "expert", split_axis=0, concat_axis=0, tiled=True)
    slots = received.shape[1]
    shaped = received.reshape(groups, local, slots, received.shape[2])
    product = jnp.einsum("sxcd,xfd->sxcf", shaped, w_down, preferred_element_type=jnp.float32)
    returned_rows = lax.all_to_all(
        product.astype(jnp.bfloat16).reshape(experts, slots, w_down.shape[1]),
        "expert",
        split_axis=0,
        concat_axis=0,
        tiled=True,
    )
    flat = returned_rows.reshape(experts * capacity, returned_rows.shape[2])
    returned = flat[target].astype(jnp.float32)
    grad_hidden = (gate_prob[:, None] * returned).astype(jnp.bfloat16)
    partial_sum = jnp.sum(hidden_in.astype(jnp.float32) * returned, axis=1)
    grad_gate = lax.psum(partial_sum, "tensor")
    return (grad_hidden, grad_gate)


def solution(mesh):
    return jax.shard_map(
        body,
        mesh=mesh,
        in_specs=(
            P("expert", "tensor"),
            P("expert", "tensor"),
            P("expert"),
            P("expert", None),
            P("expert", "tensor", None),
        ),
        out_specs=(P("expert", "tensor"), P("expert")),
        check_vma=False,
    )
```

profile of v0, /device:TPU:1, one launch (start us, length us, event | category | flops | bytes accessed | tf_op | source)
XLA Modules:
  0.0 475.2 jit_solution(18276313659422710938)
XLA Ops:
  7.2 0.0 copy-start
  7.2 0.0 all-gather.2.cloned.1.call-start
  7.2 0.7 all-gather.2.cloned.1.call-update
  7.9 0.9 fusion.9
  8.8 1.2 reduce-window.6
  10.0 0.2 slice_reduce_fusion
  10.3 0.8 fusion.8
  11.1 0.7 compare_select_fusion
  11.8 2.4 scatter_custom_fusion
  14.3 48.8 %all-gather.2.cloned.1.call-done = bf16[512,3072]{1,0:T(8,128)(2,1)} async-done(((bf16[512,384]{1,0:T(8,128)(2,1)}), bf16[512,3072]{1,0:T(8,128)(2,1)}) %all-gather.2.cloned.1.call-update) | async-done | bytes 3145744 | tf_op jit(solution)/shard_map/all_gather | solution.py:26
  63.1 3.9 concatenate.3
  66.9 14.5 %gather_fusion = bf16[1024,3072]{1,0:T(8,128)(2,1)} fusion(bf16[513,3072]{1,0:T(8,128)(2,1)} %concatenate.3, s32[1024]{0:T(1024)S(1)} %fusion.10), kind=kCustom, calls=%fused_computation | custom fusion | bytes 12587008 | tf_op jit(solution)/shard_map/gather | solution.py:28
  81.5 296.3 %all_to_all.10 = bf16[64,16,3072]{2,1,0:T(8,128)(2,1)S(1)} all-to-all(bf16[64,16,3072]{2,1,0:T(8,128)(2,1)} %bitcast.28), channel_id=1, replica_groups=mesh['expert'=64,'tensor'=8] {'expert'}, dimensions={0} | all-to-all | bytes 12582912 | tf_op jit(solution)/shard_map/all_to_all | solution.py:29
  377.8 0.0 copy-done
  377.8 4.5 fusion.2
  382.3 0.0 copy-start.1
  382.3 14.7 %all-to-all-start.1 = ((bf16[64,16,512]{2,1,0:T(8,128)(2,1)}), bf16[64,16,512]{2,1,0:T(8,128)(2,1)}, u32[]{:S(2)}, u32[]{:S(2)}) async-start(bf16[64,16,512]{2,1,0:T(8,128)(2,1)} %fusion.2), calls=%async_computation.1 | async-start | bytes 2097152 | tf_op jit(solution)/shard_map/all_to_all | solution.py:33
  397.0 45.4 %all-to-all-done.1 = bf16[64,16,512]{2,1,0:T(8,128)(2,1)} async-done(((bf16[64,16,512]{2,1,0:T(8,128)(2,1)}), bf16[64,16,512]{2,1,0:T(8,128)(2,1)}, u32[]{:S(2)}, u32[]{:S(2)}) %all-to-all-start.1) | async-done | bytes 1048608 | tf_op jit(solution)/shard_map/all_to_all | solution.py:33
  442.4 4.0 gather_fusion.1
  446.4 0.0 copy-done.1
  446.4 2.2 fusion.6
  448.7 19.7 %psum.7 = f32[512]{0:T(512)} all-reduce(f32[512]{0:T(512)S(1)} %get-tuple-element.2), channel_id=1, replica_groups=mesh['expert'=64,'tensor'=8] {'tensor'}, use_global_device_ids=true, to_apply=%region_5.6 | all-reduce | flops 512 | bytes 4096 | tf_op jit(solution)/shard_map/psum | solution.py:44
  (5 shorter events, 0.1 us)
Async XLA Ops:
  7.2 370.6 %copy-start = (bf16[1,512,3072]{2,1,0:T(8,128)(2,1)S(1)}, bf16[1,512,3072]{2,1,0:T(8,128)(2,1)}, u32[]{:S(2)}) copy-start(bf16[1,512,3072]{2,1,0:T(8,128)(2,1)} %param.9) | copy-start | bytes 9437188
  7.2 55.9 %all-gather.2.cloned.1.call-start = ((), (), s32[]{:S(2)}) async-start(), calls=%async_computation.2 | async-start | bytes 3538944 | tf_op jit(solution)/shard_map/all_gather | solution.py:26
  382.3 64.2 %copy-start.1 = (f32[512]{0:T(512)S(1)}, f32[512]{0:T(512)}, u32[]{:S(2)}) copy-start(f32[512]{0:T(512)} %param.7) | copy-start | bytes 6148
  382.3 60.2 %all-to-all-start.1 = ((bf16[64,16,512]{2,1,0:T(8,128)(2,1)}), bf16[64,16,512]{2,1,0:T(8,128)(2,1)}, u32[]{:S(2)}, u32[]{:S(2)}) async-start(bf16[64,16,512]{2,1,0:T(8,128)(2,1)} %fusion.2), calls=%async_computation.1 | async-start | bytes 2097152 | tf_op jit(solution)/shard_map/all_to_all | solution.py:33
Sparse Core Ops, SparseCore 0:
  10.1 52.9 all-gather.1
where the time goes:
time: 477 us; the launch traced here: 475 us
  blocking collectives  316 us (66%)
  waiting for transfers between devices  94.9 us (20%)
  local copies, waits for them, and re-layouts  25.1 us (5%)
  starting transfers between devices  14.8 us (3%)
  between operations  14.1 us (3%)
  other arithmetic  5.88 us (1%)
    all_to_all x1, blocking collectives, body(): lax.all_to_all(send, 'expert', split_axis=0, concat_axis=0, tiled=True)  296 us
    all_gather x1, waiting for transfers between devices, body(): outgoing = lax.all_gather(grad_out, 'tensor', axis=1, tiled=True)  48.8 us
    all_to_all x1, waiting for transfers between devices, body(): lax.all_to_all(product.astype(jnp.bfloat16).reshape(experts, slots, w_dow...  45.4 us
    psum x1, blocking collectives, body(): grad_gate = lax.psum(partial_sum, 'tensor')  19.7 us
    all_to_all x1, starting transfers between devices, body(): lax.all_to_all(product.astype(jnp.bfloat16).reshape(experts, slots, w_dow...  14.7 us
    gather x1, local copies, waits for them, and re-layouts, body(): send = padded[source].reshape(experts, capacity, outgoing.shape[1])  14.5 us
  transfers between devices with their start and end apart: 2, of which 2 were waited for; matrix products, arithmetic and copies ran while one was open for 1% of the time, Pallas kernels for 0%

commit v1 on v0

v1 whole, which is shorter than its diff:
```python
import jax
import jax.numpy as jnp
from jax import lax
from jax.sharding import PartitionSpec as P

CORES = 2


def line_pairs(chips, pairs):
    return [(a * CORES + c, b * CORES + c) for a, b in pairs for c in range(CORES)]


def body(grad_out, hidden_in, gate_prob, expert_ids, w_down):
    tokens, width = grad_out.shape
    groups = lax.axis_size("expert")
    shards = lax.axis_size("tensor")
    chips = shards // CORES
    local = w_down.shape[0]
    experts = local * groups
    capacity = 2 * tokens // experts
    slots = experts * capacity
    weight = w_down[0]
    bf16, f32 = jnp.bfloat16, jnp.float32

    with jax.named_scope("route"):
        chosen = expert_ids[:, 0]
        onehot = (chosen[:, None] == jnp.arange(experts, dtype=jnp.int32)[None, :]).astype(bf16)
        row = jnp.arange(tokens, dtype=jnp.int32)
        before = (row[None, :] < row[:, None]).astype(bf16)
        counts = jnp.dot(before, onehot, preferred_element_type=f32)
        earlier = jnp.sum(counts * onehot.astype(f32), axis=1).astype(jnp.int32)
        target = chosen * capacity + earlier
        place = (jnp.arange(slots, dtype=jnp.int32)[:, None] == target[None, :]).astype(bf16)
        send = jnp.dot(place, grad_out, preferred_element_type=f32).astype(bf16)

    with jax.named_scope("dispatch"):
        own = lax.all_to_all(send, "expert", split_axis=0, concat_axis=0, tiled=True)

    position = lax.axis_index("tensor")
    chip = position // CORES
    core = position % CORES
    core_pairs = [(p, p ^ 1) for p in range(shards)]

    def product(piece, shard, c):
        start = jnp.clip(shard, 0, chips - 1) * CORES + c
        part = lax.dynamic_slice_in_dim(weight, start * width, width, axis=1)
        return lax.dot_general(piece, part, (((1,), (1,)), ((), ())), preferred_element_type=f32)

    def both(piece, shard):
        other = lax.ppermute(piece, "tensor", core_pairs)
        return product(piece, shard, core) + product(other, shard, 1 - core)

    with jax.named_scope("expert"):
        total = both(own, chip)
        right = left = own
        for step in range(1, chips):
            right = lax.ppermute(right, "tensor", line_pairs(chips, [(i, i + 1) for i in range(step - 1, chips - 1)]))
            left = lax.ppermute(left, "tensor", line_pairs(chips, [(i, i - 1) for i in range(1, chips - step + 1)]))
            total = total + both(right, chip - step)
            total = total + both(left, chip + step)
        rows = total.astype(bf16)

    with jax.named_scope("return"):
        back = lax.all_to_all(rows, "expert", split_axis=0, concat_axis=0, tiled=True)

    with jax.named_scope("finish"):
        pick = (target[:, None] == jnp.arange(slots, dtype=jnp.int32)[None, :]).astype(bf16)
        returned = jnp.dot(pick, back, preferred_element_type=f32)
        grad_hidden = (gate_prob[:, None] * returned).astype(bf16)
        gate = jnp.sum(hidden_in.astype(f32) * returned, axis=1)
        gate = gate + lax.ppermute(gate, "tensor", core_pairs)
        turn = CORES
        while turn < shards:
            gate = gate + lax.ppermute(gate, "tensor", [(p, p ^ turn) for p in range(shards)])
            turn *= 2
    return grad_hidden, gate


def solution(mesh):
    return jax.shard_map(
        body,
        mesh=mesh,
        in_specs=(
            P("expert", "tensor"),
            P("expert", "tensor"),
            P("expert"),
            P("expert", None),
            P("expert", "tensor", None),
        ),
        out_specs=(P("expert", "tensor"), P("expert")),
        check_vma=False,
    )
```

time: 477 us -> 233 us (0.49)
  blocking collectives: 316 us -> 54.4 us
  starting transfers between devices: 14.8 us -> 79.7 us
  waiting for transfers between devices: 94.9 us -> 61.9 us
  matrix products: 4.48 us -> 29.3 us
  local copies, waits for them, and re-layouts: 25.1 us -> 4.11 us
  between operations: 14.1 us -> 0.93 us
    all_to_all x1, blocking collectives: 296 us -> 54.4 us  [body(): lax.all_to_all(send, 'expert', split_axis=0, concat_axis=0, tiled=True)]
    ppermute x0 -> x16, starting transfers between devices: none -> 71.4 us  [the longest x7 24.1 us: both(): other = lax.ppermute(piece, 'tensor', core_pairs)]
    all_gather x1 -> x0, waiting for transfers between devices: 48.8 us -> none  [body(): outgoing = lax.all_gather(grad_out, 'tensor', axis=1, tiled=True)]
    ppermute x0 -> x16, waiting for transfers between devices: none -> 25.1 us  [the longest x3 23.3 us: body(): lax.ppermute(left, 'tensor', line_pairs(chips, [(i, i - 1) for i in range...]
    dot_general x1 -> x17, matrix products: 4.48 us -> 29.3 us  [the longest x14 23.3 us: product(): lax.dot_general(piece, part, (((1,), (1,)), ((), ())), preferred_element_...]
    psum x1 -> x0, blocking collectives: 19.7 us -> none  [body(): grad_gate = lax.psum(partial_sum, 'tensor')]
    gather x2 -> x0, local copies, waits for them, and re-layouts: 18.5 us -> none  [the longest x1 14.5 us: body(): send = padded[source].reshape(experts, capacity, outgoing.shape[1])]
    all_to_all x1, waiting for transfers between devices: 45.4 us -> 36.9 us  [body(): lax.all_to_all(rows, 'expert', split_axis=0, concat_axis=0, tiled=True)]
  transfers between devices with their start and end apart: 2 -> 17, of which waited for: 2 -> 6; matrix products, arithmetic and copies ran while one was open for 1% -> 9% of each run, Pallas kernels for 0% -> 0%
where the time goes in v1:
time: 233 us; the launch traced here: 232 us
  starting transfers between devices  79.7 us (34%)
  waiting for transfers between devices  61.9 us (27%)
  blocking collectives  54.4 us (23%)
  matrix products  29.3 us (13%)
  local copies, waits for them, and re-layouts  4.11 us (2%)
    all_to_all x1, blocking collectives, body(): lax.all_to_all(send, 'expert', split_axis=0, concat_axis=0, tiled=True)  54.4 us
    all_to_all x1, waiting for transfers between devices, body(): lax.all_to_all(rows, 'expert', split_axis=0, concat_axis=0, tiled=True)  36.9 us
    ppermute x7, starting transfers between devices, both(): other = lax.ppermute(piece, 'tensor', core_pairs)  24.1 us
    dot_general x14, matrix products, product(): lax.dot_general(piece, part, (((1,), (1,)), ((), ())), preferred_element_...  23.3 us
    ppermute x3, waiting for transfers between devices, body(): lax.ppermute(left, 'tensor', line_pairs(chips, [(i, i - 1) for i in range...  23.3 us
    ppermute x2, starting transfers between devices, body(): lax.ppermute(gate, 'tensor', [(p, p ^ turn) for p in range(shards)])  20 us
    ppermute x3, starting transfers between devices, body(): lax.ppermute(right, 'tensor', line_pairs(chips, [(i, i + 1) for i in rang...  17.5 us
    all_to_all x1, starting transfers between devices, body(): lax.all_to_all(rows, 'expert', split_axis=0, concat_axis=0, tiled=True)  8.27 us
  transfers between devices with their start and end apart: 17, of which 6 were waited for; matrix products, arithmetic and copies ran while one was open for 9% of the time, Pallas kernels for 0%

profile of v1, /device:TPU:1, one launch (start us, length us, event | category | flops | bytes accessed | tf_op | source)
XLA Modules:
  0.0 231.6 jit_solution(6545248840148429791)
XLA Ops:
  0.6 0.0 copy-start
  0.6 1.1 fusion.3
  1.8 0.7 multiply_add_fusion
  2.5 1.7 fusion.2
  4.2 54.4 %all_to_all.24 = bf16[64,16,384]{2,1,0:T(8,128)(2,1)} all-to-all(bf16[64,16,384]{2,1,0:T(8,128)(2,1)S(1)} %bitcast.66), channel_id=1, replica_groups=mesh['expert'=64,'tensor'=8] {'expert'}, dimensions={0} | all-to-all | bytes 1572864 | tf_op jit(solution)/shard_map/dispatch/all_to_all | solution.py:37
  58.6 1.3 collective-permute-start.3
  59.9 16.1 %collective-permute-start.1 = (bf16[1024,384]{1,0:T(8,128)(2,1)}, bf16[1024,384]{1,0:T(8,128)(2,1)}, u32[]{:S(2)}, u32[]{:S(2)}) collective-permute-start(bf16[1024,384]{1,0:T(8,128)(2,1)} %bitcast.4), channel_id=1, source_target_pairs={{0,2},{1,3},{2,4},{3,5},{4,6},{5,7},{8,10},{9,11},{10,12},{11,13},... | collective-permute-start | bytes 2359304 | tf_op jit(solution)/shard_map/expert/ppermute | solution.py:57
  75.9 4.4 %collective-permute-start = (bf16[1024,384]{1,0:T(8,128)(2,1)}, bf16[1024,384]{1,0:T(8,128)(2,1)S(1)}, u32[]{:S(2)}, u32[]{:S(2)}) collective-permute-start(bf16[1024,384]{1,0:T(8,128)(2,1)} %bitcast.4), channel_id=1, source_target_pairs={{0,1},{1,0},{2,3},{3,2},{4,5},{5,4},{6,7},{7,6},{8,9},{9,8},{10,11... | collective-permute-start | bytes 2359304 | tf_op jit(solution)/shard_map/expert/ppermute | solution.py:50
  80.4 1.9 fusion.31
  82.3 6.7 %collective-permute-done.3 = bf16[1024,384]{1,0:T(8,128)(2,1)} collective-permute-done((bf16[1024,384]{1,0:T(8,128)(2,1)}, bf16[1024,384]{1,0:T(8,128)(2,1)}, u32[]{:S(2)}, u32[]{:S(2)}) %collective-permute-start.3) | collective-permute-done | bytes 786464 | tf_op jit(solution)/shard_map/expert/ppermute | solution.py:58
  89.0 1.3 collective-permute-start.7
  90.3 4.8 %collective-permute-start.4 = (bf16[1024,384]{1,0:T(8,128)(2,1)}, bf16[1024,384]{1,0:T(8,128)(2,1)S(1)}, u32[]{:S(2)}, u32[]{:S(2)}) collective-permute-start(bf16[1024,384]{1,0:T(8,128)(2,1)} %collective-permute-done.3), channel_id=1, source_target_pairs={{0,1},{1,0},{2,3},{3,2},{4,5},{5,4},{6,7},{7,6},{8,9},{9,8},{10,11... | collective-permute-start | bytes 2359304 | tf_op jit(solution)/shard_map/expert/ppermute | solution.py:50
  95.1 0.0 collective-permute-done.1
  95.1 0.7 collective-permute-start.5
  95.9 1.9 collective-permute-start.2
  97.8 1.9 fusion.23
  99.7 1.9 fusion.27
  101.6 0.0 collective-permute-done
  101.6 0.7 fusion.29
  102.3 4.9 %collective-permute-done.7 = bf16[1024,384]{1,0:T(8,128)(2,1)S(1)} collective-permute-done((bf16[1024,384]{1,0:T(8,128)(2,1)}, bf16[1024,384]{1,0:T(8,128)(2,1)S(1)}, u32[]{:S(2)}, u32[]{:S(2)}) %collective-permute-start.7) | collective-permute-done | bytes 786464 | tf_op jit(solution)/shard_map/expert/ppermute | solution.py:58
  107.2 5.7 %collective-permute-start.8 = (bf16[1024,384]{1,0:T(8,128)(2,1)S(1)}, bf16[1024,384]{1,0:T(8,128)(2,1)S(1)}, u32[]{:S(2)}, u32[]{:S(2)}) collective-permute-start(bf16[1024,384]{1,0:T(8,128)(2,1)S(1)} %collective-permute-done.7), channel_id=1, source_target_pairs={{0,1},{1,0},{2,3},{3,2},{4,5},{5,4},{6,7},{7,6},{8,9},{9,8},{10,11... | collective-permute-start | bytes 2359304 | tf_op jit(solution)/shard_map/expert/ppermute | solution.py:50
  113.0 1.3 collective-permute-start.11
  114.3 0.7 collective-permute-start.9
  115.0 0.8 fusion.15
  115.8 0.7 fusion.19
  116.5 1.9 collective-permute-start.6
  118.4 0.7 fusion.21
  119.2 0.7 fusion.25
  120.0 2.4 %collective-permute-start.10 = (bf16[1024,384]{1,0:T(8,128)(2,1)S(1)}, bf16[1024,384]{1,0:T(8,128)(2,1)S(1)}, u32[]{:S(2)}, u32[]{:S(2)}) collective-permute-start(bf16[1024,384]{1,0:T(8,128)(2,1)S(1)} %collective-permute-done.9), channel_id=1, source_target_pairs={{0,1},{1,0},{2,3},{3,2},{4,5},{5,4},{6,7},{7,6},{8,9},{9,8},{10,11... | collective-permute-start | bytes 2359304 | tf_op jit(solution)/shard_map/expert/ppermute | solution.py:50
  122.4 11.6 %collective-permute-done.11 = bf16[1024,384]{1,0:T(8,128)(2,1)S(1)} collective-permute-done((bf16[1024,384]{1,0:T(8,128)(2,1)S(1)}, bf16[1024,384]{1,0:T(8,128)(2,1)S(1)}, u32[]{:S(2)}, u32[]{:S(2)}) %collective-permute-start.11) | collective-permute-done | bytes 786464 | tf_op jit(solution)/shard_map/expert/ppermute | solution.py:58
  134.0 2.9 %collective-permute-start.12 = (bf16[1024,384]{1,0:T(8,128)(2,1)S(1)}, bf16[1024,384]{1,0:T(8,128)(2,1)}, u32[]{:S(2)}, u32[]{:S(2)}) collective-permute-start(bf16[1024,384]{1,0:T(8,128)(2,1)S(1)} %collective-permute-done.11), channel_id=1, source_target_pairs={{0,1},{1,0},{2,3},{3,2},{4,5},{5,4},{6,7},{7,6},{8,9},{9,8},{10,11... | collective-permute-start | bytes 2359304 | tf_op jit(solution)/shard_map/expert/ppermute | solution.py:50
  136.9 0.7 fusion.11
  137.7 0.7 fusion.7
  138.4 2.1 fusion.13
  140.5 2.1 fusion.17
  142.6 2.1 fusion.9
  144.7 6.2 %add_convert_fusion = bf16[1024,512]{1,0:T(8,128)(2,1)} fusion(f32[1024,512]{1,0:T(8,128)S(1)} %fusion.7, f32[1024,512]{1,0:T(8,128)S(1)} %fusion.11, f32[1024,512]{1,0:T(8,128)} %fusion.9, f32[1024,512]{1,0:T(8,128)S(1)} %fusion.15, f32[1024,512]{1,0:T(8,128)} %fusion.13, f32[1024,512]{1,0:T(8,128)S(1)} %fusion.19, f32[1024,512]{1,0:T(8,128)} %fusion.17, ...), kind=kOutput, calls=%fused_computation | convolution fusion | flops 409993216 | bytes 29491204 | tf_op jit(solution)/shard_map/expert/dot_general | solution.py:47
  150.9 8.3 %all-to-all-start.1 = ((bf16[64,16,512]{2,1,0:T(8,128)(2,1)}), bf16[64,16,512]{2,1,0:T(8,128)(2,1)}, u32[]{:S(2)}, u32[]{:S(2)}) async-start(bf16[64,16,512]{2,1,0:T(8,128)(2,1)} %bitcast.65), calls=%async_computation.1 | async-start | bytes 2097152 | tf_op jit(solution)/shard_map/return/all_to_all | solution.py:64
  159.2 2.0 copy.7
  161.2 36.9 %all-to-all-done.1 = bf16[64,16,512]{2,1,0:T(8,128)(2,1)} async-done(((bf16[64,16,512]{2,1,0:T(8,128)(2,1)}), bf16[64,16,512]{2,1,0:T(8,128)(2,1)}, u32[]{:S(2)}, u32[]{:S(2)}) %all-to-all-start.1) | async-done | bytes 1048608 | tf_op jit(solution)/shard_map/return/all_to_all | solution.py:64
  198.1 3.1 %multiply_reduce_fusion = (f32[512]{0:T(512)S(1)}, bf16[512,512]{0,1:T(8,128)(2,1)}) fusion(bf16[512,512]{0,1:T(8,128)(2,1)} %copy.7, f32[512]{0:T(512)S(1)} %copy-done.2, bf16[1024,512]{1,0:T(8,128)(2,1)} %bitcast.20, s32[512]{0:T(512)S(1)} %bitcast.70), kind=kOutput, calls=%fused_computation.8 | convolution fusion | flops 538705408 | bytes 2103296 | tf_op jit(solution)/shard_map/finish/dot_general | solution.py:68
  201.2 6.0 %collective-permute-start.13 = (f32[512]{0:T(512)S(1)}, f32[512]{0:T(512)S(1)}, u32[]{:S(2)}, u32[]{:S(2)}) collective-permute-start(f32[512]{0:T(512)S(1)} %get-tuple-element.4), channel_id=1, source_target_pairs={{0,1},{1,0},{2,3},{3,2},{4,5},{5,4},{6,7},{7,6},{8,9},{9,8},{10,11... | collective-permute-start | bytes 6152 | tf_op jit(solution)/shard_map/finish/ppermute | solution.py:71
  207.2 0.8 collective-permute-done.13
  208.0 14.2 %collective-permute-start.14 = (f32[512]{0:T(512)S(1)}, f32[512]{0:T(512)S(1)}, u32[]{:S(2)}, u32[]{:S(2)}) collective-permute-start(f32[512]{0:T(512)S(1)} %add.206), channel_id=1, source_target_pairs={{0,2},{1,3},{2,0},{3,1},{4,6},{5,7},{6,4},{7,5},{8,10},{9,11},{10,... | collective-permute-start | bytes 6152 | tf_op jit(solution)/shard_map/finish/ppermute | solution.py:74
  222.2 1.0 collective-permute-done.14
  223.2 5.8 %collective-permute-start.15 = (f32[512]{0:T(512)S(1)}, f32[512]{0:T(512)S(1)}, u32[]{:S(2)}, u32[]{:S(2)}) collective-permute-start(f32[512]{0:T(512)S(1)} %add.207), channel_id=1, source_target_pairs={{0,4},{1,5},{2,6},{3,7},{4,0},{5,1},{6,2},{7,3},{8,12},{9,13},{10,... | collective-permute-start | bytes 6152 | tf_op jit(solution)/shard_map/finish/ppermute | solution.py:74
  229.0 2.0 copy.8
  231.0 0.6 add.208
  (18 shorter events, 0.0 us)
Async XLA Ops:
  0.6 79.8 %copy-start = (bf16[1,512,3072]{2,1,0:T(8,128)(2,1)S(1)}, bf16[1,512,3072]{2,1,0:T(8,128)(2,1)}, u32[]{:S(2)}) copy-start(bf16[1,512,3072]{2,1,0:T(8,128)(2,1)} %param.9) | copy-start | bytes 9437188
  58.6 30.4 %collective-permute-start.3 = (bf16[1024,384]{1,0:T(8,128)(2,1)}, bf16[1024,384]{1,0:T(8,128)(2,1)}, u32[]{:S(2)}, u32[]{:S(2)}) collective-permute-start(bf16[1024,384]{1,0:T(8,128)(2,1)} %bitcast.4), channel_id=1, source_target_pairs={{2,0},{3,1},{4,2},{5,3},{6,4},{7,5},{10,8},{11,9},{12,10},{13,11},... | collective-permute-start | bytes 2359304 | tf_op jit(solution)/shard_map/expert/ppermute | solution.py:58
  59.9 35.3 %collective-permute-start.1 = (bf16[1024,384]{1,0:T(8,128)(2,1)}, bf16[1024,384]{1,0:T(8,128)(2,1)}, u32[]{:S(2)}, u32[]{:S(2)}) collective-permute-start(bf16[1024,384]{1,0:T(8,128)(2,1)} %bitcast.4), channel_id=1, source_target_pairs={{0,2},{1,3},{2,4},{3,5},{4,6},{5,7},{8,10},{9,11},{10,12},{11,13},... | collective-permute-start | bytes 2359304 | tf_op jit(solution)/shard_map/expert/ppermute | solution.py:57
  75.9 25.6 %collective-permute-start = (bf16[1024,384]{1,0:T(8,128)(2,1)}, bf16[1024,384]{1,0:T(8,128)(2,1)S(1)}, u32[]{:S(2)}, u32[]{:S(2)}) collective-permute-start(bf16[1024,384]{1,0:T(8,128)(2,1)} %bitcast.4), channel_id=1, source_target_pairs={{0,1},{1,0},{2,3},{3,2},{4,5},{5,4},{6,7},{7,6},{8,9},{9,8},{10,11... | collective-permute-start | bytes 2359304 | tf_op jit(solution)/shard_map/expert/ppermute | solution.py:50
  89.0 18.2 %collective-permute-start.7 = (bf16[1024,384]{1,0:T(8,128)(2,1)}, bf16[1024,384]{1,0:T(8,128)(2,1)S(1)}, u32[]{:S(2)}, u32[]{:S(2)}) collective-permute-start(bf16[1024,384]{1,0:T(8,128)(2,1)} %collective-permute-done.3), channel_id=1, source_target_pairs={{2,0},{3,1},{4,2},{5,3},{10,8},{11,9},{12,10},{13,11},{18,16},{19,... | collective-permute-start | bytes 2359304 | tf_op jit(solution)/shard_map/expert/ppermute | solution.py:58
  90.3 26.2 %collective-permute-start.4 = (bf16[1024,384]{1,0:T(8,128)(2,1)}, bf16[1024,384]{1,0:T(8,128)(2,1)S(1)}, u32[]{:S(2)}, u32[]{:S(2)}) collective-permute-start(bf16[1024,384]{1,0:T(8,128)(2,1)} %collective-permute-done.3), channel_id=1, source_target_pairs={{0,1},{1,0},{2,3},{3,2},{4,5},{5,4},{6,7},{7,6},{8,9},{9,8},{10,11... | collective-permute-start | bytes 2359304 | tf_op jit(solution)/shard_map/expert/ppermute | solution.py:50
  95.1 19.1 %collective-permute-start.5 = (bf16[1024,384]{1,0:T(8,128)(2,1)}, bf16[1024,384]{1,0:T(8,128)(2,1)S(1)}, u32[]{:S(2)}, u32[]{:S(2)}) collective-permute-start(bf16[1024,384]{1,0:T(8,128)(2,1)} %collective-permute-done.1), channel_id=1, source_target_pairs={{2,4},{3,5},{4,6},{5,7},{10,12},{11,13},{12,14},{13,15},{18,20},{1... | collective-permute-start | bytes 2359304 | tf_op jit(solution)/shard_map/expert/ppermute | solution.py:57
  95.9 23.3 %collective-permute-start.2 = (bf16[1024,384]{1,0:T(8,128)(2,1)}, bf16[1024,384]{1,0:T(8,128)(2,1)S(1)}, u32[]{:S(2)}, u32[]{:S(2)}) collective-permute-start(bf16[1024,384]{1,0:T(8,128)(2,1)} %collective-permute-done.1), channel_id=1, source_target_pairs={{0,1},{1,0},{2,3},{3,2},{4,5},{5,4},{6,7},{7,6},{8,9},{9,8},{10,11... | collective-permute-start | bytes 2359304 | tf_op jit(solution)/shard_map/expert/ppermute | solution.py:50
  107.2 31.2 %collective-permute-start.8 = (bf16[1024,384]{1,0:T(8,128)(2,1)S(1)}, bf16[1024,384]{1,0:T(8,128)(2,1)S(1)}, u32[]{:S(2)}, u32[]{:S(2)}) collective-permute-start(bf16[1024,384]{1,0:T(8,128)(2,1)S(1)} %collective-permute-done.7), channel_id=1, source_target_pairs={{0,1},{1,0},{2,3},{3,2},{4,5},{5,4},{6,7},{7,6},{8,9},{9,8},{10,11... | collective-permute-start | bytes 2359304 | tf_op jit(solution)/shard_map/expert/ppermute | solution.py:50
  113.0 21.1 %collective-permute-start.11 = (bf16[1024,384]{1,0:T(8,128)(2,1)S(1)}, bf16[1024,384]{1,0:T(8,128)(2,1)S(1)}, u32[]{:S(2)}, u32[]{:S(2)}) collective-permute-start(bf16[1024,384]{1,0:T(8,128)(2,1)S(1)} %collective-permute-done.7), channel_id=1, source_target_pairs={{2,0},{3,1},{10,8},{11,9},{18,16},{19,17},{26,24},{27,25},{34,32},... | collective-permute-start | bytes 2359304 | tf_op jit(solution)/shard_map/expert/ppermute | solution.py:58
  114.3 5.7 %collective-permute-start.9 = (bf16[1024,384]{1,0:T(8,128)(2,1)S(1)}, bf16[1024,384]{1,0:T(8,128)(2,1)S(1)}, u32[]{:S(2)}, u32[]{:S(2)}) collective-permute-start(bf16[1024,384]{1,0:T(8,128)(2,1)S(1)} %collective-permute-done.5), channel_id=1, source_target_pairs={{4,6},{5,7},{12,14},{13,15},{20,22},{21,23},{28,30},{29,31},{36,38... | collective-permute-start | bytes 2359304 | tf_op jit(solution)/shard_map/expert/ppermute | solution.py:57
  116.5 24.0 %collective-permute-start.6 = (bf16[1024,384]{1,0:T(8,128)(2,1)S(1)}, bf16[1024,384]{1,0:T(8,128)(2,1)S(1)}, u32[]{:S(2)}, u32[]{:S(2)}) collective-permute-start(bf16[1024,384]{1,0:T(8,128)(2,1)S(1)} %collective-permute-done.5), channel_id=1, source_target_pairs={{0,1},{1,0},{2,3},{3,2},{4,5},{5,4},{6,7},{7,6},{8,9},{9,8},{10,11... | collective-permute-start | bytes 2359304 | tf_op jit(solution)/shard_map/expert/ppermute | solution.py:50
  120.0 22.6 %collective-permute-start.10 = (bf16[1024,384]{1,0:T(8,128)(2,1)S(1)}, bf16[1024,384]{1,0:T(8,128)(2,1)S(1)}, u32[]{:S(2)}, u32[]{:S(2)}) collective-permute-start(bf16[1024,384]{1,0:T(8,128)(2,1)S(1)} %collective-permute-done.9), channel_id=1, source_target_pairs={{0,1},{1,0},{2,3},{3,2},{4,5},{5,4},{6,7},{7,6},{8,9},{9,8},{10,11... | collective-permute-start | bytes 2359304 | tf_op jit(solution)/shard_map/expert/ppermute | solution.py:50
  134.0 10.7 %collective-permute-start.12 = (bf16[1024,384]{1,0:T(8,128)(2,1)S(1)}, bf16[1024,384]{1,0:T(8,128)(2,1)}, u32[]{:S(2)}, u32[]{:S(2)}) collective-permute-start(bf16[1024,384]{1,0:T(8,128)(2,1)S(1)} %collective-permute-done.11), channel_id=1, source_target_pairs={{0,1},{1,0},{2,3},{3,2},{4,5},{5,4},{6,7},{7,6},{8,9},{9,8},{10,11... | collective-permute-start | bytes 2359304 | tf_op jit(solution)/shard_map/expert/ppermute | solution.py:50
  150.9 10.3 %copy-start.1 = (s32[512,1]{0,1:T(1,128)S(1)}, s32[512,1]{0,1:T(1,128)}, u32[]{:S(2)}) copy-start(s32[512,1]{0,1:T(1,128)} %param.8) | copy-start | bytes 6148
  150.9 47.2 %copy-start.2 = (f32[512]{0:T(512)S(1)}, f32[512]{0:T(512)}, u32[]{:S(2)}) copy-start(f32[512]{0:T(512)} %param.7) | copy-start | bytes 6148
  150.9 47.2 %all-to-all-start.1 = ((bf16[64,16,512]{2,1,0:T(8,128)(2,1)}), bf16[64,16,512]{2,1,0:T(8,128)(2,1)}, u32[]{:S(2)}, u32[]{:S(2)}) async-start(bf16[64,16,512]{2,1,0:T(8,128)(2,1)} %bitcast.65), calls=%async_computation.1 | async-start | bytes 2097152 | tf_op jit(solution)/shard_map/return/all_to_all | solution.py:64
  201.2 6.8 %collective-permute-start.13 = (f32[512]{0:T(512)S(1)}, f32[512]{0:T(512)S(1)}, u32[]{:S(2)}, u32[]{:S(2)}) collective-permute-start(f32[512]{0:T(512)S(1)} %get-tuple-element.4), channel_id=1, source_target_pairs={{0,1},{1,0},{2,3},{3,2},{4,5},{5,4},{6,7},{7,6},{8,9},{9,8},{10,11... | collective-permute-start | bytes 6152 | tf_op jit(solution)/shard_map/finish/ppermute | solution.py:71
  208.0 15.2 %collective-permute-start.14 = (f32[512]{0:T(512)S(1)}, f32[512]{0:T(512)S(1)}, u32[]{:S(2)}, u32[]{:S(2)}) collective-permute-start(f32[512]{0:T(512)S(1)} %add.206), channel_id=1, source_target_pairs={{0,2},{1,3},{2,0},{3,1},{4,6},{5,7},{6,4},{7,5},{8,10},{9,11},{10,... | collective-permute-start | bytes 6152 | tf_op jit(solution)/shard_map/finish/ppermute | solution.py:74
  223.2 7.8 %collective-permute-start.15 = (f32[512]{0:T(512)S(1)}, f32[512]{0:T(512)S(1)}, u32[]{:S(2)}, u32[]{:S(2)}) collective-permute-start(f32[512]{0:T(512)S(1)} %add.207), channel_id=1, source_target_pairs={{0,4},{1,5},{2,6},{3,7},{4,0},{5,1},{6,2},{7,3},{8,12},{9,13},{10,... | collective-permute-start | bytes 6152 | tf_op jit(solution)/shard_map/finish/ppermute | solution.py:74

commit v2 on v1

v2 whole, which is shorter than its diff:
```python
import functools

import jax
import jax.numpy as jnp
from jax import lax
from jax.experimental import pallas as pl
from jax.experimental.pallas import tpu as pltpu
from jax.sharding import PartitionSpec as P

SEGMENTS = 4
COLUMNS = 16
CORES = 2


def products(lists, chips, position_ref, *refs):
    count = 2 * chips - 1
    pieces, weight_ref = refs[: lists * count], refs[lists * count]
    mine_ref, other_ref, total = refs[lists * count + 1 :]
    rows, width = pieces[0].shape
    hidden = mine_ref.shape[1]
    position = position_ref[0]
    total[...] = jnp.zeros_like(total)
    for n in range(count):
        shard = position + chips - 1 - n

        @pl.when((shard >= 0) & (shard < chips))
        def _():
            part = weight_ref[:, pl.ds(pl.multiple_of(shard * width, 128), width)]
            for k in range(lists):
                total[k * rows : (k + 1) * rows, :] += lax.dot_general(
                    pieces[k * count + n][...], part, (((1,), (1,)), ((), ())), preferred_element_type=jnp.float32
                )

    mine_ref[...] = total[:, :hidden]
    other_ref[...] = total[:, hidden:]


def expert_rows(position, lists, weight, chips):
    rows = lists[0][0][2]
    width = lists[0][0][0].shape[1]
    hidden = weight.shape[0] // CORES
    arrays, specs = [], []
    for entries in lists:
        for array, first, _ in entries:
            arrays.append(array)
            specs.append(pl.BlockSpec((rows, width), functools.partial(lambda b, i: (b, 0), first // rows)))
    total = rows * len(lists)
    out = jax.ShapeDtypeStruct((total, hidden), jnp.float32)
    return pl.pallas_call(
        functools.partial(products, len(lists), chips),
        grid=(1,),
        out_shape=[out, out],
        in_specs=[pl.BlockSpec(memory_space=pltpu.SMEM)] + specs + [pl.BlockSpec(weight.shape, lambda i: (0, 0))],
        out_specs=[pl.BlockSpec((total, hidden), lambda i: (0, 0))] * 2,
        scratch_shapes=[pltpu.VMEM((total, CORES * hidden), jnp.float32)],
        compiler_params=pltpu.CompilerParams(vmem_limit_bytes=40 * 1024 * 1024),
        cost_estimate=pl.CostEstimate(
            flops=2 * total * weight.size, bytes_accessed=2 * weight.size + 2 * len(arrays) * rows * width, transcendentals=0
        ),
    )(position, *arrays, weight)


def body(grad_out, hidden_in, gate_prob, expert_ids, w_down):
    tokens, width = grad_out.shape
    groups = lax.axis_size("expert")
    shards = lax.axis_size("tensor")
    chips = shards // CORES
    experts = w_down.shape[0] * groups
    capacity = 2 * tokens // experts
    slots = experts * capacity
    block = COLUMNS * capacity
    half = block // 2
    weight = w_down[0]
    bf16, f32 = jnp.bfloat16, jnp.float32

    position = lax.axis_index("tensor")
    segment = lax.axis_index("expert") // COLUMNS
    chip, core = position // CORES, position % CORES
    core_pairs = [(p, p ^ 1) for p in range(shards)]
    length = SEGMENTS * chips

    def device(z, column, c):
        z = z % length
        return ((z // chips) * COLUMNS + column) * shards + (z % chips) * CORES + c

    def ring(way):
        return [
            (device(z, column, c), device(z + way, column, c))
            for z in range(length)
            for column in range(COLUMNS)
            for c in range(CORES)
        ]

    with jax.named_scope("route"):
        chosen = expert_ids[:, 0]
        onehot = (chosen[:, None] == jnp.arange(experts, dtype=jnp.int32)[None, :]).astype(bf16)
        row = jnp.arange(tokens, dtype=jnp.int32)
        before = (row[None, :] < row[:, None]).astype(bf16)
        counts = jnp.dot(before, onehot, preferred_element_type=f32)
        earlier = jnp.sum(counts * onehot.astype(f32), axis=1).astype(jnp.int32)
        target = chosen * capacity + earlier
        away = (chosen // COLUMNS - segment) % SEGMENTS
        sent_to = ((chosen % COLUMNS) * SEGMENTS + away) * capacity + earlier
        place = (jnp.arange(slots, dtype=jnp.int32)[:, None] == sent_to[None, :]).astype(bf16)
        send = jnp.dot(place, grad_out, preferred_element_type=f32).astype(bf16)

    with jax.named_scope("plane"):
        planes = [[s * COLUMNS + k for k in range(COLUMNS)] for s in range(SEGMENTS)]
        got = lax.all_to_all(send, "expert", split_axis=0, concat_axis=0, axis_index_groups=planes, tiled=True)
        got = got.reshape(COLUMNS, SEGMENTS, capacity, width)
        far = got[:, 2]
        right = jnp.concatenate([got[:, 0], got[:, 1], far[: COLUMNS // 2]], axis=0).reshape(-1, width)
        left = jnp.concatenate([got[:, 0], got[:, 3], far[COLUMNS // 2 :]], axis=0).reshape(-1, width)

    with jax.named_scope("weights"):
        def shards_of(c):
            return jnp.concatenate(
                [lax.dynamic_slice_in_dim(weight, (i * CORES + c) * width, width, axis=1) for i in range(chips)], axis=1
            )

        both = jnp.concatenate([shards_of(core), lax.ppermute(shards_of(1 - core), "tensor", core_pairs)], axis=0)
        where = chip.astype(jnp.int32).reshape(1)

    def finish_rows(pair):
        mine, other = pair
        return (mine + lax.ppermute(other, "tensor", core_pairs)).astype(bf16)

    with jax.named_scope("ring"):
        rights, lefts = [right], [left]
        steps = 3 * chips - 1
        for step in range(1, steps + 1):
            drop = block if step in (chips, 2 * chips) else 0
            right = lax.ppermute(right[drop:], ("expert", "tensor"), ring(1))
            left = lax.ppermute(left[drop:], ("expert", "tensor"), ring(-1))
            rights.append(right)
            lefts.append(left)
        first = {0: 0, 1: block, 2: 2 * block}

        def entry(array, which, rows):
            gone = right_rows - array.shape[0]
            return array, first[which] - gone, rows

        right_rows = 2 * block + half
        span = range(1, 2 * chips)
        own = [entry(lefts[chips - 1 - n], 0, block) for n in range(chips - 1)] + [
            entry(rights[n], 0, block) for n in range(chips)
        ]
        near = [[entry(rights[k], 1, block) for k in span], [entry(lefts[k], 1, block) for k in reversed(span)]]
        away2 = [
            [entry(rights[k + chips], 2, half) for k in span],
            [entry(lefts[k + chips], 2, half) for k in reversed(span)],
        ]
        own_rows = finish_rows(expert_rows(where, [own], both, chips))
        near_rows = finish_rows(expert_rows(where, near, both, chips))
        far_rows = finish_rows(expert_rows(where, away2, both, chips))
        around = jnp.concatenate([own_rows, near_rows[block:], far_rows, near_rows[:block]], axis=0)
        around = jnp.concatenate([around, around], axis=0)
        rows = lax.dynamic_slice_in_dim(around, ((SEGMENTS - segment) % SEGMENTS) * block, slots, axis=0)

    with jax.named_scope("return"):
        back = lax.all_to_all(rows, "expert", split_axis=0, concat_axis=0, tiled=True)

    with jax.named_scope("finish"):
        pick = (target[:, None] == jnp.arange(slots, dtype=jnp.int32)[None, :]).astype(bf16)
        returned = jnp.dot(pick, back, preferred_element_type=f32)
        grad_hidden = (gate_prob[:, None] * returned).astype(bf16)
        gate = jnp.sum(hidden_in.astype(f32) * returned, axis=1)
        gate = gate + lax.ppermute(gate, "tensor", core_pairs)
        turn = CORES
        while turn < shards:
            gate = gate + lax.ppermute(gate, "tensor", [(p, p ^ turn) for p in range(shards)])
            turn *= 2
    return grad_hidden, gate


def solution(mesh):
    return jax.shard_map(
        body,
        mesh=mesh,
        in_specs=(
            P("expert", "tensor"),
            P("expert", "tensor"),
            P("expert"),
            P("expert", None),
            P("expert", "tensor", None),
        ),
        out_specs=(P("expert", "tensor"), P("expert")),
        check_vma=False,
    )
```

time: 233 us -> 264 us (1.13)
  starting transfers between devices: 79.7 us -> 131 us
  blocking collectives: 54.4 us -> 19.6 us
  matrix products: 29.3 us -> 2.68 us
  local copies, waits for them, and re-layouts: 4.11 us -> 18.8 us
  Pallas kernels: 0 us -> 11.8 us
  waiting for transfers between devices: 61.9 us -> 69 us
  other arithmetic: 1.29 us -> 7.42 us
    ppermute x13 -> x26, starting transfers between devices: 45.5 us -> 103 us  [the longest x11 56.9 us: body(): left = lax.ppermute(left[drop:], ('expert', 'tensor'), ring(-1))]
    all_to_all x1, blocking collectives: 54.4 us -> 19.6 us  [body(): lax.all_to_all(send, 'expert', split_axis=0, concat_axis=0, axis_index_gr...]
    dot_general x14 -> x0, matrix products: 23.3 us -> none  [product(): lax.dot_general(piece, part, (((1,), (1,)), ((), ())), preferred_element_...]
    pallas_call x0 -> x3, Pallas kernels: none -> 11.8 us  [expert_rows(): pl.pallas_call(functools.partial(products, len(lists), chips), grid=(1,),...]
    ppermute x2, starting transfers between devices: 20 us -> 9.6 us  [body(): lax.ppermute(gate, 'tensor', [(p, p ^ turn) for p in range(shards)])]
    unnamed x8 -> x85, local copies, waits for them, and re-layouts: 4.11 us -> 14.3 us
    all_to_all x1, waiting for transfers between devices: 36.9 us -> 45.8 us  [body(): lax.all_to_all(rows, 'expert', split_axis=0, concat_axis=0, tiled=True)]
    dynamic_slice x0 -> x2, local copies, waits for them, and re-layouts: none -> 4.38 us  [the longest x1 3.28 us: shards_of(): lax.dynamic_slice_in_dim(weight, (i * CORES + c) * width, width, axis=1)]
  transfers between devices with their start and end apart: 17 -> 30, of which waited for: 6 -> 14; matrix products, arithmetic and copies ran while one was open for 9% -> 4% of each run, Pallas kernels for 0% -> 2%
where the time goes in v2:
time: 264 us; the launch traced here: 262 us
  starting transfers between devices  131 us (50%)
  waiting for transfers between devices  69 us (26%)
  blocking collectives  19.6 us (7%)
  local copies, waits for them, and re-layouts  18.8 us (7%)
  Pallas kernels  11.8 us (4%)
  other arithmetic  7.42 us (3%)
  matrix products  2.68 us (1%)
    ppermute x11, starting transfers between devices, body(): left = lax.ppermute(left[drop:], ('expert', 'tensor'), ring(-1))  56.9 us
    all_to_all x1, waiting for transfers between devices, body(): lax.all_to_all(rows, 'expert', split_axis=0, concat_axis=0, tiled=True)  45.8 us
    ppermute x11, starting transfers between devices, body(): right = lax.ppermute(right[drop:], ('expert', 'tensor'), ring(1))  23.9 us
    all_to_all x1, blocking collectives, body(): lax.all_to_all(send, 'expert', split_axis=0, concat_axis=0, axis_index_gr...  19.6 us
    ppermute x11, waiting for transfers between devices, body(): right = lax.ppermute(right[drop:], ('expert', 'tensor'), ring(1))  18.3 us
    ppermute x3, starting transfers between devices, finish_rows(): return (mine + lax.ppermute(other, 'tensor', core_pairs)).astype(bf16)  17 us
    unnamed x85, local copies, waits for them, and re-layouts  14.3 us
    pallas_call x3, Pallas kernels, expert_rows(): pl.pallas_call(functools.partial(products, len(lists), chips), grid=(1,),...  11.8 us
  transfers between devices with their start and end apart: 30, of which 14 were waited for; matrix products, arithmetic and copies ran while one was open for 4% of the time, Pallas kernels for 2%

profile of v2, /device:TPU:1, one launch (start us, length us, event | category | flops | bytes accessed | tf_op | source)
XLA Modules:
  0.0 261.9 jit_solution(8412936537618843555)
XLA Ops:
  0.7 1.0 fusion.3
  3.2 19.6 %all_to_all.21 = bf16[16,64,384]{2,1,0:T(8,128)(2,1)S(1)} all-to-all(bf16[16,64,384]{2,1,0:T(8,128)(2,1)S(1)} %bitcast.49), channel_id=1, replica_groups={{0,8,16,24,32,40,48,56,64,72,80,88,96,104,112,120},{128,136,144,152,160..., dimensions={0} | all-to-all | bytes 1572864 | tf_op jit(solution)/shard_map/plane/all_to_all | solution.py:109
  23.0 4.8 %collective-permute-start.3 = (bf16[640,384]{1,0:T(8,128)(2,1)S(1)}, bf16[640,384]{1,0:T(8,128)(2,1)S(1)}, u32[]{:S(2)}, u32[]{:S(2)}) collective-permute-start(bf16[640,384]{1,0:T(8,128)(2,1)S(1)} %bitcast.44), channel_id=1, source_target_pairs={{0,2},{1,3},{8,10},{9,11},{16,18},{17,19},{24,26},{25,27},{32,34},... | collective-permute-start | bytes 1474568 | tf_op jit(solution)/shard_map/ring/ppermute | solution.py:133
  27.8 9.5 %collective-permute-start = (bf16[640,384]{1,0:T(8,128)(2,1)S(1)}, bf16[640,384]{1,0:T(8,128)(2,1)S(1)}, u32[]{:S(2)}, u32[]{:S(2)}) collective-permute-start(bf16[640,384]{1,0:T(8,128)(2,1)S(1)} %bitcast.50), channel_id=1, source_target_pairs={{0,390},{1,391},{8,398},{9,399},{16,406},{17,407},{24,414},{25,415... | collective-permute-start | bytes 1474568 | tf_op jit(solution)/shard_map/ring/ppermute | solution.py:134
  37.4 7.8 %collective-permute-done.3.refs_4_.refs_0_ = bf16[640,384]{1,0:T(8,128)(2,1)S(1)} collective-permute-done((bf16[640,384]{1,0:T(8,128)(2,1)S(1)}, bf16[640,384]{1,0:T(8,128)(2,1)S(1)}, u32[]{:S(2)}, u32[]{:S(2)}) %collective-permute-start.3) | collective-permute-done | bytes 491552 | tf_op jit(solution)/shard_map/ring/ppermute | solution.py:133
  45.1 1.9 collective-permute-start.4
  47.1 4.6 %collective-permute-start.1 = (bf16[640,384]{1,0:T(8,128)(2,1)S(1)}, bf16[640,384]{1,0:T(8,128)(2,1)S(1)}, u32[]{:S(2)}, u32[]{:S(2)}) collective-permute-start(bf16[640,384]{1,0:T(8,128)(2,1)S(1)} %collective-permute-done.refs_2_.refs_13_), channel_id=1, source_target_pairs={{0,390},{1,391},{8,398},{9,399},{16,406},{17,407},{24,414},{25,415... | collective-permute-start | bytes 1474568 | tf_op jit(solution)/shard_map/ring/ppermute | solution.py:134
  51.6 3.3 %dynamic-slice_bitcast_fusion.7 = (bf16[512,384]{1,0:T(8,128)(2,1)}, bf16[512,384]{1,0:T(8,128)(2,1)S(1)}, bf16[512,384]{1,0:T(8,128)(2,1)S(1)}, bf16[512,384]{1...) fusion(bf16[1,512,3072]{2,1,0:T(8,128)(2,1)} %param.9, ...), kind=kLoop, calls=%fused_computation.28 | loop fusion | bytes 6291488 | tf_op jit(solution)/shard_map/weights/dynamic_slice | solution.py:118
  55.1 4.9 %collective-permute-start.6 = (bf16[512,1536]{1,0:T(8,128)(2,1)S(1)}, bf16[512,1536]{1,0:T(8,128)(2,1)}, u32[]{:S(2)}, u32[]{:S(2)}) collective-permute-start(bf16[512,1536]{1,0:T(8,128)(2,1)S(1)} %pad_maximum_fusion.1), channel_id=1, source_target_pairs={{0,1},{1,0},{2,3},{3,2},{4,5},{5,4},{6,7},{7,6},{8,9},{9,8},{10,11... | collective-permute-start | bytes 4718600 | tf_op jit(solution)/shard_map/weights/ppermute | solution.py:121
  60.0 1.9 collective-permute-start.5
  62.0 4.6 %collective-permute-start.2 = (bf16[640,384]{1,0:T(8,128)(2,1)S(1)}, bf16[640,384]{1,0:T(8,128)(2,1)S(1)}, u32[]{:S(2)}, u32[]{:S(2)}) collective-permute-start(bf16[640,384]{1,0:T(8,128)(2,1)S(1)} %collective-permute-done.1.refs_1_.refs_12_), channel_id=1, source_target_pairs={{0,390},{1,391},{8,398},{9,399},{16,406},{17,407},{24,414},{25,415... | collective-permute-start | bytes 1474568 | tf_op jit(solution)/shard_map/ring/ppermute | solution.py:134
  67.3 6.7 %collective-permute-done.5.refs_6_.refs_2_ = bf16[640,384]{1,0:T(8,128)(2,1)S(1)} collective-permute-done((bf16[640,384]{1,0:T(8,128)(2,1)S(1)}, bf16[640,384]{1,0:T(8,128)(2,1)S(1)}, u32[]{:S(2)}, u32[]{:S(2)}) %collective-permute-start.5) | collective-permute-done | bytes 491552 | tf_op jit(solution)/shard_map/ring/ppermute | solution.py:133
  74.8 1.9 collective-permute-start.8
  77.6 4.6 %collective-permute-start.12 = (bf16[384,384]{1,0:T(8,128)(2,1)S(1)}, bf16[384,384]{1,0:T(8,128)(2,1)S(1)}, u32[]{:S(2)}, u32[]{:S(2)}) collective-permute-start(bf16[384,384]{1,0:T(8,128)(2,1)S(1)} %slice.62), channel_id=1, source_target_pairs={{0,390},{1,391},{8,398},{9,399},{16,406},{17,407},{24,414},{25,415... | collective-permute-start | bytes 884744 | tf_op jit(solution)/shard_map/ring/ppermute | solution.py:134
  82.2 1.3 collective-permute-done.8.refs_3_
  83.5 1.9 collective-permute-start.9
  86.1 4.7 %collective-permute-start.13 = (bf16[384,384]{1,0:T(8,128)(2,1)S(1)}, bf16[384,384]{1,0:T(8,128)(2,1)S(1)}, u32[]{:S(2)}, u32[]{:S(2)}) collective-permute-start(bf16[384,384]{1,0:T(8,128)(2,1)S(1)} %collective-permute-done.12.refs_10_), channel_id=1, source_target_pairs={{0,390},{1,391},{8,398},{9,399},{16,406},{17,407},{24,414},{25,415... | collective-permute-start | bytes 884744 | tf_op jit(solution)/shard_map/ring/ppermute | solution.py:134
  92.2 1.9 collective-permute-start.10
  94.8 4.7 %collective-permute-start.14 = (bf16[384,384]{1,0:T(8,128)(2,1)S(1)}, bf16[384,384]{1,0:T(8,128)(2,1)}, u32[]{:S(2)}, u32[]{:S(2)}) collective-permute-start(bf16[384,384]{1,0:T(8,128)(2,1)S(1)} %collective-permute-done.13.refs_9_.refs_13_), channel_id=1, source_target_pairs={{0,390},{1,391},{8,398},{9,399},{16,406},{17,407},{24,414},{25,415... | collective-permute-start | bytes 884744 | tf_op jit(solution)/shard_map/ring/ppermute | solution.py:134
  100.9 1.9 collective-permute-start.11
  103.1 5.1 %collective-permute-start.15 = (bf16[384,384]{1,0:T(8,128)(2,1)}, bf16[384,384]{1,0:T(8,128)(2,1)S(1)}, u32[]{:S(2)}, u32[]{:S(2)}) collective-permute-start(bf16[384,384]{1,0:T(8,128)(2,1)} %collective-permute-done.14.refs_8_.refs_12_), channel_id=1, source_target_pairs={{0,390},{1,391},{8,398},{9,399},{16,406},{17,407},{24,414},{25,415... | collective-permute-start | bytes 884744 | tf_op jit(solution)/shard_map/ring/ppermute | solution.py:134
  108.4 3.0 %pad_maximum_fusion.refs_7_.refs_14_ = bf16[1024,1536]{1,0:T(8,128)(2,1)S(1)} fusion(bf16[512,1536]{1,0:T(8,128)(2,1)} %collective-permute-done.6, bf16[512,384]{1,0:T(8,128)(2,1)} %get-tuple-element.25, bf16[512,384]{1,0:T(8,128)(2,1)} %get-tuple-element.26, bf16[512,384]{1,0:T(8,128)(2,1)} %get-tuple-element.27, bf16[512,384]{1,0:T(8,128)(2,1)} %get-tuple-element.22), kind=kLoop, calls=%fused_computation | loop fusion | flops 15728640 | bytes 6291456 | tf_op jit(solution)/shard_map/weights/concatenate | solution.py:121
  112.3 5.3 %ring.4 = (f32[512,512]{1,0:T(8,128)S(1)}, f32[512,512]{1,0:T(8,128)}) custom-call(s32[1]{0:T(128)} %bitcast.3.position_ref, bf16[640,384]{1,0:T(8,128)(2,1)S(1)} %copy-done.8, bf16[640,384]{1,0:T(8,128)(2,1)S(1)} %copy-done.12, bf16[640,384]{1,0:T(8,128)(2,1)S(1)} %copy-done.2, bf16[384,384]{1,0:T(8,128)(2,1)S(1)} %copy-done.29, ...), custom_call_target="tpu_custom_call" | custom-call | flops 1610612736 | bytes 5898240 | tf_op jit(solution)/shard_map/ring/pallas_call | solution.py:49
  117.6 9.2 %collective-permute-start.16 = (f32[512,512]{1,0:T(8,128)}, f32[512,512]{1,0:T(8,128)}, u32[]{:S(2)}, u32[]{:S(2)}) collective-permute-start(f32[512,512]{1,0:T(8,128)} %get-tuple-element.11), channel_id=1, source_target_pairs={{0,1},{1,0},{2,3},{3,2},{4,5},{5,4},{6,7},{7,6},{8,9},{9,8},{10,11... | collective-permute-start | bytes 3145736 | tf_op jit(solution)/shard_map/ring/ppermute | solution.py:126
  126.8 2.7 %ring.3 = (f32[256,512]{1,0:T(8,128)S(1)}, f32[256,512]{1,0:T(8,128)}) custom-call(s32[1]{0:T(128)} %bitcast.3.position_ref, bf16[640,384]{1,0:T(8,128)(2,1)S(1)} %copy-done.4, bf16[640,384]{1,0:T(8,128)(2,1)S(1)} %copy-done.14, bf16[640,384]{1,0:T(8,128)(2,1)S(1)} %copy-done.10, bf16[640,384]{1,0:T(8,128)(2,1)S(1)} %bitcast.45, ...), custom_call_target="tpu_custom_call" | custom-call | flops 805306368 | bytes 4521984 | tf_op jit(solution)/shard_map/ring/pallas_call | solution.py:49
  130.4 1.9 collective-permute-start.7
  132.3 1.9 collective-permute-start.17
  134.3 5.3 %collective-permute-start.21 = (bf16[128,384]{1,0:T(8,128)(2,1)S(1)}, bf16[128,384]{1,0:T(8,128)(2,1)S(1)}, u32[]{:S(2)}, u32[]{:S(2)}) collective-permute-start(bf16[128,384]{1,0:T(8,128)(2,1)S(1)} %slice.65), channel_id=1, source_target_pairs={{0,390},{1,391},{8,398},{9,399},{16,406},{17,407},{24,414},{25,415... | collective-permute-start | bytes 294920 | tf_op jit(solution)/shard_map/ring/ppermute | solution.py:134
  140.4 1.9 collective-permute-start.18
  142.9 4.6 %collective-permute-start.22 = (bf16[128,384]{1,0:T(8,128)(2,1)S(1)}, bf16[128,384]{1,0:T(8,128)(2,1)}, u32[]{:S(2)}, u32[]{:S(2)}) collective-permute-start(bf16[128,384]{1,0:T(8,128)(2,1)S(1)} %collective-permute-done.21.refs_10_), channel_id=1, source_target_pairs={{0,390},{1,391},{8,398},{9,399},{16,406},{17,407},{24,414},{25,415... | collective-permute-start | bytes 294920 | tf_op jit(solution)/shard_map/ring/ppermute | solution.py:134
  148.2 1.9 collective-permute-start.19
  150.1 4.6 %collective-permute-start.23 = (bf16[128,384]{1,0:T(8,128)(2,1)}, bf16[128,384]{1,0:T(8,128)(2,1)}, u32[]{:S(2)}, u32[]{:S(2)}) collective-permute-start(bf16[128,384]{1,0:T(8,128)(2,1)} %collective-permute-done.22.refs_9_), channel_id=1, source_target_pairs={{0,390},{1,391},{8,398},{9,399},{16,406},{17,407},{24,414},{25,415... | collective-permute-start | bytes 294920 | tf_op jit(solution)/shard_map/ring/ppermute | solution.py:134
  155.0 1.9 collective-permute-start.20
  157.0 4.8 %collective-permute-start.24 = (bf16[128,384]{1,0:T(8,128)(2,1)}, bf16[128,384]{1,0:T(8,128)(2,1)S(1)}, u32[]{:S(2)}, u32[]{:S(2)}) collective-permute-start(bf16[128,384]{1,0:T(8,128)(2,1)} %collective-permute-done.23.refs_8_), channel_id=1, source_target_pairs={{0,390},{1,391},{8,398},{9,399},{16,406},{17,407},{24,414},{25,415... | collective-permute-start | bytes 294920 | tf_op jit(solution)/shard_map/ring/ppermute | solution.py:134
  161.7 1.4 constant_dynamic-update-slice_fusion.3
  163.7 1.0 copy-done.16
  165.6 1.0 copy-done.21
  169.3 3.8 %ring.5 = (f32[256,512]{1,0:T(8,128)S(1)}, f32[256,512]{1,0:T(8,128)S(1)}) custom-call(s32[1]{0:T(128)} %bitcast.3.position_ref, bf16[384,384]{1,0:T(8,128)(2,1)S(1)} %copy-done.21, bf16[384,384]{1,0:T(8,128)(2,1)} %collective-permute-done.10.refs_5_.refs_1_, bf16[384,384]{1,0:T(8,128)(2,1)S(1)} %copy-done.16, bf16[128,384]{1,0:T(8,128)(2,1)S(1)} %copy-done.33, ...), custom_call_target="tpu_custom_call" | custom-call | flops 805306368 | bytes 4521984 | tf_op jit(solution)/shard_map/ring/pallas_call | solution.py:49
  173.1 5.9 %collective-permute-start.25 = (f32[256,512]{1,0:T(8,128)S(1)}, f32[256,512]{1,0:T(8,128)S(1)}, u32[]{:S(2)}, u32[]{:S(2)}) collective-permute-start(f32[256,512]{1,0:T(8,128)S(1)} %get-tuple-element.13), channel_id=1, source_target_pairs={{0,1},{1,0},{2,3},{3,2},{4,5},{5,4},{6,7},{7,6},{8,9},{9,8},{10,11... | collective-permute-start | bytes 1572872 | tf_op jit(solution)/shard_map/ring/ppermute | solution.py:126
  179.0 1.4 add_convert_fusion
  180.7 1.1 constant_dynamic-slice_fusion
  181.8 11.2 %all-to-all-start.1 = ((bf16[64,16,512]{2,1,0:T(8,128)(2,1)}), bf16[64,16,512]{2,1,0:T(8,128)(2,1)S(1)}, u32[]{:S(2)}, u32[]{:S(2)}) async-start(bf16[64,16,512]{2,1,0:T(8,128)(2,1)} %bitcast.21), calls=%async_computation.1 | async-start | bytes 2097152 | tf_op jit(solution)/shard_map/return/all_to_all | solution.py:161
  193.2 45.8 %all-to-all-done.1 = bf16[64,16,512]{2,1,0:T(8,128)(2,1)S(1)} async-done(((bf16[64,16,512]{2,1,0:T(8,128)(2,1)}), bf16[64,16,512]{2,1,0:T(8,128)(2,1)S(1)}, u32[]{:S(2)}, u32[]{:S(2)}) %all-to-all-start.1) | async-done | bytes 1048608 | tf_op jit(solution)/shard_map/return/all_to_all | solution.py:161
  240.0 7.5 %collective-permute-start.26 = (f32[512]{0:T(512)S(1)}, f32[512]{0:T(512)S(1)}, u32[]{:S(2)}, u32[]{:S(2)}) collective-permute-start(f32[512]{0:T(512)S(1)} %get-tuple-element.30), channel_id=1, source_target_pairs={{0,1},{1,0},{2,3},{3,2},{4,5},{5,4},{6,7},{7,6},{8,9},{9,8},{10,11... | collective-permute-start | bytes 6152 | tf_op jit(solution)/shard_map/finish/ppermute | solution.py:168
  248.3 1.9 collective-permute-start.27
  250.2 2.4 collective-permute-done.27
  252.6 7.7 %collective-permute-start.28 = (f32[512]{0:T(512)S(1)}, f32[512]{0:T(512)S(1)}, u32[]{:S(2)}, u32[]{:S(2)}) collective-permute-start(f32[512]{0:T(512)S(1)} %add.142), channel_id=1, source_target_pairs={{0,4},{1,5},{2,6},{3,7},{4,0},{5,1},{6,2},{7,3},{8,12},{9,13},{10,... | collective-permute-start | bytes 6152 | tf_op jit(solution)/shard_map/finish/ppermute | solution.py:171
  260.3 1.0 copy.13
  (125 shorter events, 19.8 us)
Async XLA Ops:
  23.0 31.9 %copy-start.5 = (bf16[40,16,384]{2,1,0:T(8,128)(2,1)}, bf16[40,16,384]{2,1,0:T(8,128)(2,1)S(1)}, u32[]{:S(2)}) copy-start(bf16[40,16,384]{2,1,0:T(8,128)(2,1)S(1)} %get-tuple-element.37) | copy-start | bytes 1474564
  23.0 22.1 %collective-permute-start.3 = (bf16[640,384]{1,0:T(8,128)(2,1)S(1)}, bf16[640,384]{1,0:T(8,128)(2,1)S(1)}, u32[]{:S(2)}, u32[]{:S(2)}) collective-permute-start(bf16[640,384]{1,0:T(8,128)(2,1)S(1)} %bitcast.44), channel_id=1, source_target_pairs={{0,2},{1,3},{8,10},{9,11},{16,18},{17,19},{24,26},{25,27},{32,34},... | collective-permute-start | bytes 1474568 | tf_op jit(solution)/shard_map/ring/ppermute | solution.py:133
  27.8 19.2 %collective-permute-start = (bf16[640,384]{1,0:T(8,128)(2,1)S(1)}, bf16[640,384]{1,0:T(8,128)(2,1)S(1)}, u32[]{:S(2)}, u32[]{:S(2)}) collective-permute-start(bf16[640,384]{1,0:T(8,128)(2,1)S(1)} %bitcast.50), channel_id=1, source_target_pairs={{0,390},{1,391},{8,398},{9,399},{16,406},{17,407},{24,414},{25,415... | collective-permute-start | bytes 1474568 | tf_op jit(solution)/shard_map/ring/ppermute | solution.py:134
  45.1 9.8 %copy-start.7 = (bf16[640,384]{1,0:T(8,128)(2,1)}, bf16[640,384]{1,0:T(8,128)(2,1)S(1)}, u32[]{:S(2)}) copy-start(bf16[640,384]{1,0:T(8,128)(2,1)S(1)} %collective-permute-done.3.refs_4_.refs_0_) | copy-start | bytes 1474564
  45.1 14.9 %collective-permute-start.4 = (bf16[640,384]{1,0:T(8,128)(2,1)S(1)}, bf16[640,384]{1,0:T(8,128)(2,1)S(1)}, u32[]{:S(2)}, u32[]{:S(2)}) collective-permute-start(bf16[640,384]{1,0:T(8,128)(2,1)S(1)} %collective-permute-done.3.refs_4_.refs_0_), channel_id=1, source_target_pairs={{0,2},{1,3},{8,10},{9,11},{16,18},{17,19},{24,26},{25,27},{32,34},... | collective-permute-start | bytes 1474568 | tf_op jit(solution)/shard_map/ring/ppermute | solution.py:133
  47.1 7.9 %copy-start.9 = (bf16[640,384]{1,0:T(8,128)(2,1)}, bf16[640,384]{1,0:T(8,128)(2,1)S(1)}, u32[]{:S(2)}) copy-start(bf16[640,384]{1,0:T(8,128)(2,1)S(1)} %collective-permute-done.refs_2_.refs_13_) | copy-start | bytes 1474564
  47.1 14.9 %collective-permute-start.1 = (bf16[640,384]{1,0:T(8,128)(2,1)S(1)}, bf16[640,384]{1,0:T(8,128)(2,1)S(1)}, u32[]{:S(2)}, u32[]{:S(2)}) collective-permute-start(bf16[640,384]{1,0:T(8,128)(2,1)S(1)} %collective-permute-done.refs_2_.refs_13_), channel_id=1, source_target_pairs={{0,390},{1,391},{8,398},{9,399},{16,406},{17,407},{24,414},{25,415... | collective-permute-start | bytes 1474568 | tf_op jit(solution)/shard_map/ring/ppermute | solution.py:134
  55.1 53.2 %collective-permute-start.6 = (bf16[512,1536]{1,0:T(8,128)(2,1)S(1)}, bf16[512,1536]{1,0:T(8,128)(2,1)}, u32[]{:S(2)}, u32[]{:S(2)}) collective-permute-start(bf16[512,1536]{1,0:T(8,128)(2,1)S(1)} %pad_maximum_fusion.1), channel_id=1, source_target_pairs={{0,1},{1,0},{2,3},{3,2},{4,5},{5,4},{6,7},{7,6},{8,9},{9,8},{10,11... | collective-permute-start | bytes 4718600 | tf_op jit(solution)/shard_map/weights/ppermute | solution.py:121
  60.0 16.8 %copy-start.11 = (bf16[640,384]{1,0:T(8,128)(2,1)}, bf16[640,384]{1,0:T(8,128)(2,1)S(1)}, u32[]{:S(2)}) copy-start(bf16[640,384]{1,0:T(8,128)(2,1)S(1)} %collective-permute-done.4.refs_5_.refs_1_) | copy-start | bytes 1474564
  60.0 14.0 %collective-permute-start.5 = (bf16[640,384]{1,0:T(8,128)(2,1)S(1)}, bf16[640,384]{1,0:T(8,128)(2,1)S(1)}, u32[]{:S(2)}, u32[]{:S(2)}) collective-permute-start(bf16[640,384]{1,0:T(8,128)(2,1)S(1)} %collective-permute-done.4.refs_5_.refs_1_), channel_id=1, source_target_pairs={{0,2},{1,3},{8,10},{9,11},{16,18},{17,19},{24,26},{25,27},{32,34},... | collective-permute-start | bytes 1474568 | tf_op jit(solution)/shard_map/ring/ppermute | solution.py:133
  62.0 14.8 %collective-permute-start.2 = (bf16[640,384]{1,0:T(8,128)(2,1)S(1)}, bf16[640,384]{1,0:T(8,128)(2,1)S(1)}, u32[]{:S(2)}, u32[]{:S(2)}) collective-permute-start(bf16[640,384]{1,0:T(8,128)(2,1)S(1)} %collective-permute-done.1.refs_1_.refs_12_), channel_id=1, source_target_pairs={{0,390},{1,391},{8,398},{9,399},{16,406},{17,407},{24,414},{25,415... | collective-permute-start | bytes 1474568 | tf_op jit(solution)/shard_map/ring/ppermute | solution.py:134
  74.8 8.7 %collective-permute-start.8 = (bf16[384,384]{1,0:T(8,128)(2,1)S(1)}, bf16[384,384]{1,0:T(8,128)(2,1)S(1)}, u32[]{:S(2)}, u32[]{:S(2)}) collective-permute-start(bf16[384,384]{1,0:T(8,128)(2,1)S(1)} %slice.61), channel_id=1, source_target_pairs={{0,2},{1,3},{8,10},{9,11},{16,18},{17,19},{24,26},{25,27},{32,34},... | collective-permute-start | bytes 884744 | tf_op jit(solution)/shard_map/ring/ppermute | solution.py:133
  77.6 8.6 %collective-permute-start.12 = (bf16[384,384]{1,0:T(8,128)(2,1)S(1)}, bf16[384,384]{1,0:T(8,128)(2,1)S(1)}, u32[]{:S(2)}, u32[]{:S(2)}) collective-permute-start(bf16[384,384]{1,0:T(8,128)(2,1)S(1)} %slice.62), channel_id=1, source_target_pairs={{0,390},{1,391},{8,398},{9,399},{16,406},{17,407},{24,414},{25,415... | collective-permute-start | bytes 884744 | tf_op jit(solution)/shard_map/ring/ppermute | solution.py:134
  83.5 8.7 %collective-permute-start.9 = (bf16[384,384]{1,0:T(8,128)(2,1)S(1)}, bf16[384,384]{1,0:T(8,128)(2,1)S(1)}, u32[]{:S(2)}, u32[]{:S(2)}) collective-permute-start(bf16[384,384]{1,0:T(8,128)(2,1)S(1)} %collective-permute-done.8.refs_3_), channel_id=1, source_target_pairs={{0,2},{1,3},{8,10},{9,11},{16,18},{17,19},{24,26},{25,27},{32,34},... | collective-permute-start | bytes 884744 | tf_op jit(solution)/shard_map/ring/ppermute | solution.py:133
  86.1 8.7 %collective-permute-start.13 = (bf16[384,384]{1,0:T(8,128)(2,1)S(1)}, bf16[384,384]{1,0:T(8,128)(2,1)S(1)}, u32[]{:S(2)}, u32[]{:S(2)}) collective-permute-start(bf16[384,384]{1,0:T(8,128)(2,1)S(1)} %collective-permute-done.12.refs_10_), channel_id=1, source_target_pairs={{0,390},{1,391},{8,398},{9,399},{16,406},{17,407},{24,414},{25,415... | collective-permute-start | bytes 884744 | tf_op jit(solution)/shard_map/ring/ppermute | solution.py:134
  92.2 8.8 %collective-permute-start.10 = (bf16[384,384]{1,0:T(8,128)(2,1)S(1)}, bf16[384,384]{1,0:T(8,128)(2,1)}, u32[]{:S(2)}, u32[]{:S(2)}) collective-permute-start(bf16[384,384]{1,0:T(8,128)(2,1)S(1)} %collective-permute-done.9.refs_4_.refs_0_), channel_id=1, source_target_pairs={{0,2},{1,3},{8,10},{9,11},{16,18},{17,19},{24,26},{25,27},{32,34},... | collective-permute-start | bytes 884744 | tf_op jit(solution)/shard_map/ring/ppermute | solution.py:133
  94.8 8.3 %collective-permute-start.14 = (bf16[384,384]{1,0:T(8,128)(2,1)S(1)}, bf16[384,384]{1,0:T(8,128)(2,1)}, u32[]{:S(2)}, u32[]{:S(2)}) collective-permute-start(bf16[384,384]{1,0:T(8,128)(2,1)S(1)} %collective-permute-done.13.refs_9_.refs_13_), channel_id=1, source_target_pairs={{0,390},{1,391},{8,398},{9,399},{16,406},{17,407},{24,414},{25,415... | collective-permute-start | bytes 884744 | tf_op jit(solution)/shard_map/ring/ppermute | solution.py:134
  100.9 10.5 %collective-permute-start.11 = (bf16[384,384]{1,0:T(8,128)(2,1)}, bf16[384,384]{1,0:T(8,128)(2,1)S(1)}, u32[]{:S(2)}, u32[]{:S(2)}) collective-permute-start(bf16[384,384]{1,0:T(8,128)(2,1)} %collective-permute-done.10.refs_5_.refs_1_), channel_id=1, source_target_pairs={{0,2},{1,3},{8,10},{9,11},{16,18},{17,19},{24,26},{25,27},{32,34},... | collective-permute-start | bytes 884744 | tf_op jit(solution)/shard_map/ring/ppermute | solution.py:133
  103.1 9.1 %collective-permute-start.15 = (bf16[384,384]{1,0:T(8,128)(2,1)}, bf16[384,384]{1,0:T(8,128)(2,1)S(1)}, u32[]{:S(2)}, u32[]{:S(2)}) collective-permute-start(bf16[384,384]{1,0:T(8,128)(2,1)} %collective-permute-done.14.refs_8_.refs_12_), channel_id=1, source_target_pairs={{0,390},{1,391},{8,398},{9,399},{16,406},{17,407},{24,414},{25,415... | collective-permute-start | bytes 884744 | tf_op jit(solution)/shard_map/ring/ppermute | solution.py:134
  108.3 4.0 %copy-start.2 = (bf16[640,384]{1,0:T(8,128)(2,1)S(1)}, bf16[640,384]{1,0:T(8,128)(2,1)}, u32[]{:S(2)}) copy-start(bf16[640,384]{1,0:T(8,128)(2,1)} %copy-done.1) | copy-start | bytes 1474564
  108.3 3.9 %copy-start.4 = (bf16[640,384]{1,0:T(8,128)(2,1)S(1)}, bf16[640,384]{1,0:T(8,128)(2,1)}, u32[]{:S(2)}) copy-start(bf16[640,384]{1,0:T(8,128)(2,1)} %copy-done.3) | copy-start | bytes 1474564
  108.3 3.9 %copy-start.8 = (bf16[640,384]{1,0:T(8,128)(2,1)S(1)}, bf16[640,384]{1,0:T(8,128)(2,1)}, u32[]{:S(2)}) copy-start(bf16[640,384]{1,0:T(8,128)(2,1)} %copy-done.7) | copy-start | bytes 1474564
  108.3 3.9 %copy-start.10 = (bf16[640,384]{1,0:T(8,128)(2,1)S(1)}, bf16[640,384]{1,0:T(8,128)(2,1)}, u32[]{:S(2)}) copy-start(bf16[640,384]{1,0:T(8,128)(2,1)} %copy-done.9) | copy-start | bytes 1474564
  108.3 3.9 %copy-start.12 = (bf16[640,384]{1,0:T(8,128)(2,1)S(1)}, bf16[640,384]{1,0:T(8,128)(2,1)}, u32[]{:S(2)}) copy-start(bf16[640,384]{1,0:T(8,128)(2,1)} %copy-done.11) | copy-start | bytes 1474564
  108.3 3.9 %copy-start.14 = (bf16[640,384]{1,0:T(8,128)(2,1)S(1)}, bf16[640,384]{1,0:T(8,128)(2,1)}, u32[]{:S(2)}) copy-start(bf16[640,384]{1,0:T(8,128)(2,1)} %copy-done.13) | copy-start | bytes 1474564
  111.4 20.8 %copy-start.15 = (bf16[384,384]{1,0:T(8,128)(2,1)}, bf16[384,384]{1,0:T(8,128)(2,1)S(1)}, u32[]{:S(2)}) copy-start(bf16[384,384]{1,0:T(8,128)(2,1)S(1)} %collective-permute-done.11.refs_6_.refs_2_) | copy-start | bytes 884740
  112.2 22.0 %copy-start.17 = (bf16[384,384]{1,0:T(8,128)(2,1)}, bf16[384,384]{1,0:T(8,128)(2,1)S(1)}, u32[]{:S(2)}) copy-start(bf16[384,384]{1,0:T(8,128)(2,1)S(1)} %collective-permute-done.15.refs_7_.refs_11_) | copy-start | bytes 884740
  112.3 14.5 %copy-start.6 = (bf16[40,16,384]{2,1,0:T(8,128)(2,1)S(1)}, bf16[40,16,384]{2,1,0:T(8,128)(2,1)}, u32[]{:S(2)}) copy-start(bf16[40,16,384]{2,1,0:T(8,128)(2,1)} %copy-done.5) | copy-start | bytes 1474564
  117.6 12.0 %copy-start.25 = (f32[512,512]{1,0:T(8,128)}, f32[512,512]{1,0:T(8,128)S(1)}, u32[]{:S(2)}) copy-start(f32[512,512]{1,0:T(8,128)S(1)} %get-tuple-element.10) | copy-start | bytes 3145732
  117.6 61.4 %collective-permute-start.16 = (f32[512,512]{1,0:T(8,128)}, f32[512,512]{1,0:T(8,128)}, u32[]{:S(2)}, u32[]{:S(2)}) collective-permute-start(f32[512,512]{1,0:T(8,128)} %get-tuple-element.11), channel_id=1, source_target_pairs={{0,1},{1,0},{2,3},{3,2},{4,5},{5,4},{6,7},{7,6},{8,9},{9,8},{10,11... | collective-permute-start | bytes 3145736 | tf_op jit(solution)/shard_map/ring/ppermute | solution.py:126
  130.4 31.4 %collective-permute-start.7 = (f32[256,512]{1,0:T(8,128)}, f32[256,512]{1,0:T(8,128)}, u32[]{:S(2)}, u32[]{:S(2)}) collective-permute-start(f32[256,512]{1,0:T(8,128)} %get-tuple-element.9), channel_id=1, source_target_pairs={{0,1},{1,0},{2,3},{3,2},{4,5},{5,4},{6,7},{7,6},{8,9},{9,8},{10,11... | collective-permute-start | bytes 1572872 | tf_op jit(solution)/shard_map/ring/ppermute | solution.py:126
  132.3 8.1 %collective-permute-start.17 = (bf16[128,384]{1,0:T(8,128)(2,1)S(1)}, bf16[128,384]{1,0:T(8,128)(2,1)S(1)}, u32[]{:S(2)}, u32[]{:S(2)}) collective-permute-start(bf16[128,384]{1,0:T(8,128)(2,1)S(1)} %slice.64), channel_id=1, source_target_pairs={{0,2},{1,3},{8,10},{9,11},{16,18},{17,19},{24,26},{25,27},{32,34},... | collective-permute-start | bytes 294920 | tf_op jit(solution)/shard_map/ring/ppermute | solution.py:133
  134.3 8.7 %collective-permute-start.21 = (bf16[128,384]{1,0:T(8,128)(2,1)S(1)}, bf16[128,384]{1,0:T(8,128)(2,1)S(1)}, u32[]{:S(2)}, u32[]{:S(2)}) collective-permute-start(bf16[128,384]{1,0:T(8,128)(2,1)S(1)} %slice.65), channel_id=1, source_target_pairs={{0,390},{1,391},{8,398},{9,399},{16,406},{17,407},{24,414},{25,415... | collective-permute-start | bytes 294920 | tf_op jit(solution)/shard_map/ring/ppermute | solution.py:134
  140.4 7.8 %collective-permute-start.18 = (bf16[128,384]{1,0:T(8,128)(2,1)S(1)}, bf16[128,384]{1,0:T(8,128)(2,1)}, u32[]{:S(2)}, u32[]{:S(2)}) collective-permute-start(bf16[128,384]{1,0:T(8,128)(2,1)S(1)} %collective-permute-done.17.refs_3_), channel_id=1, source_target_pairs={{0,2},{1,3},{8,10},{9,11},{16,18},{17,19},{24,26},{25,27},{32,34},... | collective-permute-start | bytes 294920 | tf_op jit(solution)/shard_map/ring/ppermute | solution.py:133
  142.9 7.1 %collective-permute-start.22 = (bf16[128,384]{1,0:T(8,128)(2,1)S(1)}, bf16[128,384]{1,0:T(8,128)(2,1)}, u32[]{:S(2)}, u32[]{:S(2)}) collective-permute-start(bf16[128,384]{1,0:T(8,128)(2,1)S(1)} %collective-permute-done.21.refs_10_), channel_id=1, source_target_pairs={{0,390},{1,391},{8,398},{9,399},{16,406},{17,407},{24,414},{25,415... | collective-permute-start | bytes 294920 | tf_op jit(solution)/shard_map/ring/ppermute | solution.py:134
  148.2 6.9 %collective-permute-start.19 = (bf16[128,384]{1,0:T(8,128)(2,1)}, bf16[128,384]{1,0:T(8,128)(2,1)}, u32[]{:S(2)}, u32[]{:S(2)}) collective-permute-start(bf16[128,384]{1,0:T(8,128)(2,1)} %collective-permute-done.18.refs_4_), channel_id=1, source_target_pairs={{0,2},{1,3},{8,10},{9,11},{16,18},{17,19},{24,26},{25,27},{32,34},... | collective-permute-start | bytes 294920 | tf_op jit(solution)/shard_map/ring/ppermute | solution.py:133
  150.1 6.9 %collective-permute-start.23 = (bf16[128,384]{1,0:T(8,128)(2,1)}, bf16[128,384]{1,0:T(8,128)(2,1)}, u32[]{:S(2)}, u32[]{:S(2)}) collective-permute-start(bf16[128,384]{1,0:T(8,128)(2,1)} %collective-permute-done.22.refs_9_), channel_id=1, source_target_pairs={{0,390},{1,391},{8,398},{9,399},{16,406},{17,407},{24,414},{25,415... | collective-permute-start | bytes 294920 | tf_op jit(solution)/shard_map/ring/ppermute | solution.py:134
  155.0 8.1 %collective-permute-start.20 = (bf16[128,384]{1,0:T(8,128)(2,1)}, bf16[128,384]{1,0:T(8,128)(2,1)S(1)}, u32[]{:S(2)}, u32[]{:S(2)}) collective-permute-start(bf16[128,384]{1,0:T(8,128)(2,1)} %collective-permute-done.19.refs_5_), channel_id=1, source_target_pairs={{0,2},{1,3},{8,10},{9,11},{16,18},{17,19},{24,26},{25,27},{32,34},... | collective-permute-start | bytes 294920 | tf_op jit(solution)/shard_map/ring/ppermute | solution.py:133
  157.0 6.7 %collective-permute-start.24 = (bf16[128,384]{1,0:T(8,128)(2,1)}, bf16[128,384]{1,0:T(8,128)(2,1)S(1)}, u32[]{:S(2)}, u32[]{:S(2)}) collective-permute-start(bf16[128,384]{1,0:T(8,128)(2,1)} %collective-permute-done.23.refs_8_), channel_id=1, source_target_pairs={{0,390},{1,391},{8,398},{9,399},{16,406},{17,407},{24,414},{25,415... | collective-permute-start | bytes 294920 | tf_op jit(solution)/shard_map/ring/ppermute | solution.py:134
  161.7 17.2 %copy-start.26 = (f32[512,512]{1,0:T(8,128)S(1)}, f32[512,512]{1,0:T(8,128)}, u32[]{:S(2)}) copy-start(f32[512,512]{1,0:T(8,128)} %copy-done.25) | copy-start | bytes 3145732
  173.1 7.4 %collective-permute-start.25 = (f32[256,512]{1,0:T(8,128)S(1)}, f32[256,512]{1,0:T(8,128)S(1)}, u32[]{:S(2)}, u32[]{:S(2)}) collective-permute-start(f32[256,512]{1,0:T(8,128)S(1)} %get-tuple-element.13), channel_id=1, source_target_pairs={{0,1},{1,0},{2,3},{3,2},{4,5},{5,4},{6,7},{7,6},{8,9},{9,8},{10,11... | collective-permute-start | bytes 1572872 | tf_op jit(solution)/shard_map/ring/ppermute | solution.py:126
  180.7 12.3 %copy-start.36 = (bf16[512,512]{1,0:T(8,128)(2,1)S(1)}, bf16[512,512]{1,0:T(8,128)(2,1)}, u32[]{:S(2)}) copy-start(bf16[512,512]{1,0:T(8,128)(2,1)} %param.6) | copy-start | bytes 1572868
  181.8 11.4 %copy-start.37 = (s32[512,1]{0,1:T(1,128)S(1)}, s32[512,1]{0,1:T(1,128)}, u32[]{:S(2)}) copy-start(s32[512,1]{0,1:T(1,128)} %param.8) | copy-start | bytes 6148
  181.8 57.3 %copy-start.38 = (f32[512]{0:T(512)S(1)}, f32[512]{0:T(512)}, u32[]{:S(2)}) copy-start(f32[512]{0:T(512)} %param.7) | copy-start | bytes 6148
  181.8 57.3 %all-to-all-start.1 = ((bf16[64,16,512]{2,1,0:T(8,128)(2,1)}), bf16[64,16,512]{2,1,0:T(8,128)(2,1)S(1)}, u32[]{:S(2)}, u32[]{:S(2)}) async-start(bf16[64,16,512]{2,1,0:T(8,128)(2,1)} %bitcast.21), calls=%async_computation.1 | async-start | bytes 2097152 | tf_op jit(solution)/shard_map/return/all_to_all | solution.py:161
  240.0 8.3 %collective-permute-start.26 = (f32[512]{0:T(512)S(1)}, f32[512]{0:T(512)S(1)}, u32[]{:S(2)}, u32[]{:S(2)}) collective-permute-start(f32[512]{0:T(512)S(1)} %get-tuple-element.30), channel_id=1, source_target_pairs={{0,1},{1,0},{2,3},{3,2},{4,5},{5,4},{6,7},{7,6},{8,9},{9,8},{10,11... | collective-permute-start | bytes 6152 | tf_op jit(solution)/shard_map/finish/ppermute | solution.py:168
  248.3 4.3 %collective-permute-start.27 = (f32[512]{0:T(512)S(1)}, f32[512]{0:T(512)S(1)}, u32[]{:S(2)}, u32[]{:S(2)}) collective-permute-start(f32[512]{0:T(512)S(1)} %add.141), channel_id=1, source_target_pairs={{0,2},{1,3},{2,0},{3,1},{4,6},{5,7},{6,4},{7,5},{8,10},{9,11},{10,... | collective-permute-start | bytes 6152 | tf_op jit(solution)/shard_map/finish/ppermute | solution.py:171
  252.6 8.7 %collective-permute-start.28 = (f32[512]{0:T(512)S(1)}, f32[512]{0:T(512)S(1)}, u32[]{:S(2)}, u32[]{:S(2)}) collective-permute-start(f32[512]{0:T(512)S(1)} %add.142), channel_id=1, source_target_pairs={{0,4},{1,5},{2,6},{3,7},{4,0},{5,1},{6,2},{7,3},{8,12},{9,13},{10,... | collective-permute-start | bytes 6152 | tf_op jit(solution)/shard_map/finish/ppermute | solution.py:171
  (21 other events, 30.5 us)

commit v3 on v1

v3 whole, which is shorter than its diff:
```python
import functools

import jax
import jax.numpy as jnp
from jax import lax
from jax.experimental import pallas as pl
from jax.experimental.pallas import tpu as pltpu
from jax.sharding import PartitionSpec as P

CORES = 2
HALVES = 2
KINDS = 5


def line_shards(chip, chips):
    edge = (chip == 0) | (chip == chips - 1)
    shards = [chip, chip - 1, chip + 1, lax.rem(chip + 2, chips), chips - 1 - chip]
    valid = [chip >= 0, chip > 0, chip < chips - 1, chip >= 0, edge]
    return [jnp.clip(s, 0, chips - 1) for s in shards], valid


def near_kernel(chip_ref, *refs):
    kinds = KINDS - 1
    pieces, sources = refs[: HALVES * kinds], refs[HALVES * kinds : HALVES * kinds + CORES]
    out, tokens, weights, token_sems, weight_sems = refs[HALVES * kinds + CORES :]
    rows, width = pieces[0].shape
    hidden = weights.shape[1]
    shards, valid = line_shards(chip_ref[0], tokens.shape[1] // width)

    def token_copy(h, k):
        first = pl.multiple_of(shards[k] * width, 128)
        return pltpu.make_async_copy(
            pieces[h * kinds + k], tokens.at[pl.ds(h * rows, rows), pl.ds(first, width)], token_sems.at[h, k]
        )

    def weight_copy(n):
        return pltpu.make_async_copy(sources[n], weights.at[n], weight_sems.at[n])

    @pl.when(jnp.logical_not(valid[1] & valid[2]))
    def _():
        last = pl.multiple_of((tokens.shape[1] // width - 1 - chip_ref[0]) * width, 128)
        tokens[:, pl.ds(last, width)] = jnp.zeros((tokens.shape[0], width), tokens.dtype)

    for h in range(HALVES):
        weight_copy(h).start()
        for k in range(kinds):
            pl.when(valid[k])(token_copy(h, k).start)
    for h in range(HALVES):
        for k in range(kinds):
            pl.when(valid[k])(token_copy(h, k).wait)
    for n in range(CORES):
        weight_copy(n).wait()
        out[:, n * hidden : (n + 1) * hidden] = lax.dot_general(
            tokens[...], weights[n], (((1,), (1,)), ((), ())), preferred_element_type=jnp.float32
        )


def last_kernel(chips, chip_ref, total_ref, *refs):
    pieces, sources, out = refs[:HALVES], refs[HALVES : HALVES + CORES], refs[HALVES + CORES]
    weights, sems = refs[HALVES + CORES + 1 :]
    rows, width = pieces[0].shape
    hidden = weights.shape[1]
    shards, valid = line_shards(chip_ref[0], chips)
    first = pl.multiple_of(shards[-1] * width, 128)

    def weight_copy(n):
        return pltpu.make_async_copy(sources[n].at[:, pl.ds(first, width)], weights.at[n], sems.at[n])

    @pl.when(valid[-1])
    def _():
        for n in range(CORES):
            weight_copy(n).start()
        for n in range(CORES):
            weight_copy(n).wait()
            for h in range(HALVES):
                here = (slice(h * rows, (h + 1) * rows), slice(n * hidden, (n + 1) * hidden))
                more = lax.dot_general(
                    pieces[h][...], weights[n], (((1,), (1,)), ((), ())), preferred_element_type=jnp.float32
                )
                out[here] = (total_ref[here] + more).astype(out.dtype)

    @pl.when(jnp.logical_not(valid[-1]))
    def _():
        out[...] = total_ref[...].astype(out.dtype)


ANY = pl.BlockSpec(memory_space=pl.ANY)
SMEM = pl.BlockSpec(memory_space=pltpu.SMEM)
VMEM = pl.BlockSpec(memory_space=pltpu.VMEM)


def multiply_near(chip, pieces, weights):
    rows = pieces[0].shape[0] * HALVES
    hidden, depth = weights[0].shape
    return pl.pallas_call(
        near_kernel,
        out_shape=jax.ShapeDtypeStruct((rows, CORES * hidden), jnp.float32),
        in_specs=[SMEM] + [ANY] * (len(pieces) + CORES),
        out_specs=VMEM,
        scratch_shapes=[
            pltpu.VMEM((rows, depth), jnp.bfloat16),
            pltpu.VMEM((CORES, hidden, depth), jnp.bfloat16),
            pltpu.SemaphoreType.DMA((HALVES, KINDS)),
            pltpu.SemaphoreType.DMA((CORES,)),
        ],
        compiler_params=pltpu.CompilerParams(vmem_limit_bytes=32 * 1024 * 1024),
        cost_estimate=pl.CostEstimate(
            flops=2 * CORES * rows * hidden * depth, bytes_accessed=2 * (rows + CORES * hidden) * depth, transcendentals=0
        ),
    )(chip.reshape(1), *pieces, *weights)


def multiply_last(chip, chips, total, pieces, weights):
    width = pieces[0].shape[1]
    hidden = weights[0].shape[0]
    return pl.pallas_call(
        functools.partial(last_kernel, chips),
        out_shape=jax.ShapeDtypeStruct(total.shape, jnp.bfloat16),
        in_specs=[SMEM] + [VMEM] * (1 + len(pieces)) + [ANY] * CORES,
        out_specs=VMEM,
        scratch_shapes=[pltpu.VMEM((CORES, hidden, width), jnp.bfloat16), pltpu.SemaphoreType.DMA((CORES,))],
        compiler_params=pltpu.CompilerParams(vmem_limit_bytes=24 * 1024 * 1024),
        cost_estimate=pl.CostEstimate(
            flops=2 * total.size * width, bytes_accessed=8 * total.size, transcendentals=0
        ),
    )(chip.reshape(1), total, *pieces, *weights)


def place_kernel(to_ref, mine_ref, other_ref, out_ref):
    slots, tokens = out_ref.shape[0], mine_ref.shape[0]
    width = mine_ref.shape[1]
    core = to_ref[1:2, :]
    place = (lax.broadcasted_iota(jnp.int32, (slots, tokens), 0) == to_ref[0:1, :]).astype(jnp.bfloat16)
    mine = jnp.dot(place, mine_ref[...], preferred_element_type=jnp.float32).astype(jnp.bfloat16)
    other = jnp.dot(place, other_ref[...], preferred_element_type=jnp.float32).astype(jnp.bfloat16)
    first = core[:, :1] == 0
    out_ref[:, :width] = jnp.where(first, mine, other)
    out_ref[:, width:] = jnp.where(first, other, mine)


def body(grad_out, hidden_in, gate_prob, expert_ids, w_down):
    tokens, width = grad_out.shape
    groups = lax.axis_size("expert")
    shards = lax.axis_size("tensor")
    chips = shards // CORES
    experts = w_down.shape[0] * groups
    capacity = 2 * tokens // experts
    share = capacity // CORES
    slots = experts * capacity
    weight = w_down[0]
    hidden = weight.shape[0]
    bf16, f32 = jnp.bfloat16, jnp.float32

    position = lax.axis_index("tensor").astype(jnp.int32)
    chip, core = position // CORES, position % CORES
    core_pairs = [(p, p ^ 1) for p in range(shards)]

    def line(array, pairs):
        return lax.ppermute(array, "tensor", [(a * CORES + c, b * CORES + c) for a, b in pairs for c in range(CORES)])

    def swap(array):
        return lax.ppermute(array, "tensor", core_pairs)

    with jax.named_scope("route"):
        other_out = swap(grad_out)
        chosen = expert_ids[:, 0]
        onehot = (chosen[:, None] == jnp.arange(experts, dtype=jnp.int32)[None, :]).astype(bf16)
        row = jnp.arange(tokens, dtype=jnp.int32)
        before = (row[None, :] < row[:, None]).astype(bf16)
        counts = jnp.dot(before, onehot, preferred_element_type=f32)
        earlier = jnp.sum(counts * onehot.astype(f32), axis=1).astype(jnp.int32)
        away = jnp.where(earlier // share == core, 0, 1)
        target = away * (slots // CORES) + chosen * share + earlier % share
        sent_to = jnp.stack([target, jnp.full_like(target, core)])
        send = pl.pallas_call(
            place_kernel, out_shape=jax.ShapeDtypeStruct((slots // CORES, CORES * width), bf16)
        )(sent_to, grad_out, other_out)

    with jax.named_scope("weights"):
        other_weight = swap(weight)

    with jax.named_scope("dispatch"):
        got = lax.all_to_all(send, "expert", split_axis=0, concat_axis=0, tiled=True)

    with jax.named_scope("gather"):
        rows = got.shape[0] // HALVES
        own = [got[h * rows : (h + 1) * rows] for h in range(HALVES)]
        right1 = [line(x, [(0, 1), (1, 2), (2, 3)]) for x in own]
        left1 = [line(x, [(1, 0), (2, 1), (3, 2)]) for x in own]
        second = [line(r, [(1, 2), (2, 3)]) + line(l, [(2, 1), (1, 0)]) for r, l in zip(right1, left1)]
        third = [line(m, [(2, 3), (1, 0)]) for m in second]

    with jax.named_scope("products"):
        weights = [weight, other_weight]
        near = [x for h in range(HALVES) for x in (own[h], right1[h], left1[h], second[h])]
        total = multiply_near(chip, near, weights)
        filled = multiply_last(chip, chips, total, third, weights)

    with jax.named_scope("return"):
        back = lax.all_to_all(filled, "expert", split_axis=0, concat_axis=0, tiled=True)

    with jax.named_scope("finish"):
        back = jnp.concatenate([back[:, :hidden], swap(back[:, hidden:])], axis=0)
        pick = (target[:, None] == jnp.arange(slots, dtype=jnp.int32)[None, :]).astype(bf16)
        returned = jnp.dot(pick, back, preferred_element_type=f32)
        grad_hidden = (gate_prob[:, None] * returned).astype(bf16)
        part = jnp.sum(hidden_in.astype(f32) * returned, axis=1)
        parts = jnp.broadcast_to(part[None, :], (shards, tokens))
        gate = jnp.sum(lax.all_to_all(parts, "tensor", split_axis=0, concat_axis=0, tiled=True), axis=0)
    return grad_hidden, gate


def solution(mesh):
    return jax.shard_map(
        body,
        mesh=mesh,
        in_specs=(
            P("expert", "tensor"),
            P("expert", "tensor"),
            P("expert"),
            P("expert", None),
            P("expert", "tensor", None),
        ),
        out_specs=(P("expert", "tensor"), P("expert")),
        check_vma=False,
    )
```

time: 233 us -> 212 us (0.910)
  matrix products: 29.3 us -> 1.97 us
  starting transfers between devices: 79.7 us -> 57.3 us
  Pallas kernels: 0 us -> 11.7 us
  local copies, waits for them, and re-layouts: 4.11 us -> 14.1 us
  blocking collectives: 54.4 us -> 60 us
    ppermute x16 -> x13, starting transfers between devices: 71.4 us -> 37.9 us  [the longest x10 23.9 us: line(): lax.ppermute(array, 'tensor', [(a * CORES + c, b * CORES + c) for a, b in...]
    dot_general x15 -> x0, matrix products: 25 us -> none  [the longest x14 23.3 us: product(): lax.dot_general(piece, part, (((1,), (1,)), ((), ())), preferred_element_...]
    pallas_call x0 -> x3, Pallas kernels: none -> 11.7 us  [the longest x1 6.16 us: multiply_near(): pl.pallas_call(near_kernel, out_shape=jax.ShapeDtypeStruct((rows, CORES *...]
    all_to_all x1 -> x2, starting transfers between devices: 8.27 us -> 19.4 us  [the longest x1 15.8 us: body(): lax.all_to_all(send, 'expert', split_axis=0, concat_axis=0, tiled=True)]
    unnamed x8 -> x36, local copies, waits for them, and re-layouts: 4.11 us -> 11.7 us
    all_to_all x1, blocking collectives: 54.4 us -> 60 us  [body(): lax.all_to_all(filled, 'expert', split_axis=0, concat_axis=0, tiled=True)]
    ppermute x16 -> x13, waiting for transfers between devices: 25.1 us -> 23.4 us  [the longest x10 22.1 us: line(): lax.ppermute(array, 'tensor', [(a * CORES + c, b * CORES + c) for a, b in...]
    all_to_all x1 -> x2, waiting for transfers between devices: 36.9 us -> 38.3 us  [the longest x1 34.4 us: body(): lax.all_to_all(send, 'expert', split_axis=0, concat_axis=0, tiled=True)]
  transfers between devices with their start and end apart: 17 -> 15, of which waited for: 6 -> 9; matrix products, arithmetic and copies ran while one was open for 9% -> 3% of each run, Pallas kernels for 0% -> 3%
where the time goes in v3:
time: 212 us; the launch traced here: 211 us
  waiting for transfers between devices  61.7 us (29%)
  blocking collectives  60 us (28%)
  starting transfers between devices  57.3 us (27%)
  local copies, waits for them, and re-layouts  14.1 us (7%)
  Pallas kernels  11.7 us (6%)
  other arithmetic  3.07 us (1%)
    all_to_all x1, blocking collectives, body(): lax.all_to_all(filled, 'expert', split_axis=0, concat_axis=0, tiled=True)  60 us
    all_to_all x1, waiting for transfers between devices, body(): lax.all_to_all(send, 'expert', split_axis=0, concat_axis=0, tiled=True)  34.4 us
    ppermute x10, starting transfers between devices, line(): lax.ppermute(array, 'tensor', [(a * CORES + c, b * CORES + c) for a, b in...  23.9 us
    ppermute x10, waiting for transfers between devices, line(): lax.ppermute(array, 'tensor', [(a * CORES + c, b * CORES + c) for a, b in...  22.1 us
    all_to_all x1, starting transfers between devices, body(): lax.all_to_all(send, 'expert', split_axis=0, concat_axis=0, tiled=True)  15.8 us
    ppermute x3, starting transfers between devices, swap(): return lax.ppermute(array, 'tensor', core_pairs)  14 us
    unnamed x36, local copies, waits for them, and re-layouts  11.7 us
    pallas_call x1, Pallas kernels, multiply_near(): pl.pallas_call(near_kernel, out_shape=jax.ShapeDtypeStruct((rows, CORES *...  6.16 us
  transfers between devices with their start and end apart: 15, of which 9 were waited for; matrix products, arithmetic and copies ran while one was open for 3% of the time, Pallas kernels for 3%

profile of v3, /device:TPU:1, one launch (start us, length us, event | category | flops | bytes accessed | tf_op | source)
XLA Modules:
  0.0 210.9 jit_solution(679455546169350270)
XLA Ops:
  0.6 9.1 %collective-permute-start = (bf16[512,384]{1,0:T(8,128)(2,1)}, bf16[512,384]{1,0:T(8,128)(2,1)S(1)}, u32[]{:S(2)}, u32[]{:S(2)}) collective-permute-start(bf16[512,384]{1,0:T(8,128)(2,1)} %mine_ref.1), channel_id=1, source_target_pairs={{0,1},{1,0},{2,3},{3,2},{4,5},{5,4},{6,7},{7,6},{8,9},{9,8},{10,11... | collective-permute-start | bytes 1179656 | tf_op jit(solution)/shard_map/route/ppermute | solution.py:162
  9.7 1.0 fusion.1
  10.8 0.7 fusion.9
  12.1 0.7 copy-done.14
  12.8 2.7 %route.1 = bf16[512,768]{1,0:T(8,128)(2,1)} custom-call(s32[2,512]{1,0:T(2,128)} %stack.4.to_ref, bf16[512,384]{1,0:T(8,128)(2,1)} %mine_ref.1, bf16[512,384]{1,0:T(8,128)(2,1)} %copy-done.14), custom_call_target="tpu_custom_call" | custom-call | tf_op jit(solution)/shard_map/route/pallas_call | solution.py:175
  15.5 15.8 %all-to-all-start = ((bf16[64,8,768]{2,1,0:T(8,128)(2,1)}), bf16[64,8,768]{2,1,0:T(8,128)(2,1)}, u32[]{:S(2)}, u32[]{:S(2)}) async-start(bf16[64,8,768]{2,1,0:T(8,128)(2,1)} %bitcast.20), calls=%async_computation | async-start | bytes 1572864 | tf_op jit(solution)/shard_map/dispatch/all_to_all | solution.py:183
  31.3 2.2 %collective-permute-start.9 = (bf16[512,3072]{1,0:T(8,128)(2,1)S(1)}, bf16[512,3072]{1,0:T(8,128)(2,1)}, u32[]{:S(2)}, u32[]{:S(2)}) collective-permute-start(bf16[512,3072]{1,0:T(8,128)(2,1)S(1)} %bitcast.16), channel_id=1, source_target_pairs={{0,1},{1,0},{2,3},{3,2},{4,5},{5,4},{6,7},{7,6},{8,9},{9,8},{10,11... | collective-permute-start | bytes 9437192 | tf_op jit(solution)/shard_map/weights/ppermute | solution.py:162
  33.5 34.4 %all-to-all-done = bf16[64,8,768]{2,1,0:T(8,128)(2,1)} async-done(((bf16[64,8,768]{2,1,0:T(8,128)(2,1)}), bf16[64,8,768]{2,1,0:T(8,128)(2,1)}, u32[]{:S(2)}, u32[]{:S(2)}) %all-to-all-start) | async-done | bytes 786464 | tf_op jit(solution)/shard_map/dispatch/all_to_all | solution.py:183
  67.9 1.2 slice_bitcast_fusion
  69.1 10.8 %collective-permute-start.5 = (bf16[256,768]{1,0:T(8,128)(2,1)S(1)}, bf16[256,768]{1,0:T(8,128)(2,1)S(1)}, u32[]{:S(2)}, u32[]{:S(2)}) collective-permute-start(bf16[256,768]{1,0:T(8,128)(2,1)S(1)} %get-tuple-element.12.refs_4_), channel_id=1, source_target_pairs={{0,2},{1,3},{2,4},{3,5},{4,6},{5,7},{8,10},{9,11},{10,12},{11,13},... | collective-permute-start | bytes 1179656 | tf_op jit(solution)/shard_map/gather/ppermute | solution.py:159
  79.9 1.3 collective-permute-start.6
  81.2 0.7 copy-done.1
  82.0 4.0 %collective-permute-start.1 = (bf16[256,768]{1,0:T(8,128)(2,1)S(1)}, bf16[256,768]{1,0:T(8,128)(2,1)S(1)}, u32[]{:S(2)}, u32[]{:S(2)}) collective-permute-start(bf16[256,768]{1,0:T(8,128)(2,1)S(1)} %get-tuple-element.13.refs_0_), channel_id=1, source_target_pairs={{0,2},{1,3},{2,4},{3,5},{4,6},{5,7},{8,10},{9,11},{10,12},{11,13},... | collective-permute-start | bytes 1179656 | tf_op jit(solution)/shard_map/gather/ppermute | solution.py:159
  86.0 1.3 collective-permute-start.2
  87.3 0.7 copy-done.3
  88.0 0.7 collective-permute-start.7
  88.7 0.8 copy-done.5
  89.5 0.6 collective-permute-done.6.refs_6_
  90.1 1.3 collective-permute-start.8
  91.4 0.7 copy-done.7
  92.2 2.8 %collective-permute-done.1.refs_1_ = bf16[256,768]{1,0:T(8,128)(2,1)S(1)} collective-permute-done((bf16[256,768]{1,0:T(8,128)(2,1)S(1)}, bf16[256,768]{1,0:T(8,128)(2,1)S(1)}, u32[]{:S(2)}, u32[]{:S(2)}) %collective-permute-start.1) | collective-permute-done | bytes 393248 | tf_op jit(solution)/shard_map/gather/ppermute | solution.py:159
  94.9 0.7 collective-permute-start.3
  95.6 0.7 copy-done.9
  96.4 2.7 %collective-permute-done.2.refs_2_ = bf16[256,768]{1,0:T(8,128)(2,1)S(1)} collective-permute-done((bf16[256,768]{1,0:T(8,128)(2,1)S(1)}, bf16[256,768]{1,0:T(8,128)(2,1)S(1)}, u32[]{:S(2)}, u32[]{:S(2)}) %collective-permute-start.2) | collective-permute-done | bytes 393248 | tf_op jit(solution)/shard_map/gather/ppermute | solution.py:159
  99.1 1.3 collective-permute-start.4
  100.4 7.1 %collective-permute-done.8 = bf16[256,768]{1,0:T(8,128)(2,1)S(1)} collective-permute-done((bf16[256,768]{1,0:T(8,128)(2,1)S(1)}, bf16[256,768]{1,0:T(8,128)(2,1)S(1)}, u32[]{:S(2)}, u32[]{:S(2)}) %collective-permute-start.8) | collective-permute-done | bytes 393248 | tf_op jit(solution)/shard_map/gather/ppermute | solution.py:159
  107.5 0.9 add.84.refs_7_
  108.4 1.3 collective-permute-start.11
  109.7 6.3 %collective-permute-done.4 = bf16[256,768]{1,0:T(8,128)(2,1)S(1)} collective-permute-done((bf16[256,768]{1,0:T(8,128)(2,1)S(1)}, bf16[256,768]{1,0:T(8,128)(2,1)S(1)}, u32[]{:S(2)}, u32[]{:S(2)}) %collective-permute-start.4) | collective-permute-done | bytes 393248 | tf_op jit(solution)/shard_map/gather/ppermute | solution.py:159
  115.9 0.9 add.83.refs_3_
  116.8 1.3 collective-permute-start.10
  118.1 1.0 copy-done.2
  119.1 1.0 copy-done.4
  120.1 1.0 copy-done.6
  121.1 1.0 copy-done.8
  122.1 1.0 copy-done.10
  123.1 1.0 copy-done.12
  124.1 6.2 %products.2.total_ref = f32[512,1024]{1,0:T(8,128)S(1)} custom-call(s32[1]{0:T(128)} %bitcast.3.chip_ref, bf16[256,768]{1,0:T(8,128)(2,1)S(1)} %copy-done.4, bf16[256,768]{1,0:T(8,128)(2,1)S(1)} %copy-done.10, bf16[256,768]{1,0:T(8,128)(2,1)S(1)} %copy-done.12, bf16[256,768]{1,0:T(8,128)(2,1)} %add.83.refs_3_, bf16[256,768]{1,0:T(8,128)(2,1)S(1)} %copy-done.2, ...), custom_call_target="tpu_custom_call" | custom-call | flops 3221225472 | bytes 9437184 | tf_op jit(solution)/shard_map/products/pallas_call | solution.py:95
  130.3 2.6 %collective-permute-done.10.refs_0_ = bf16[256,768]{1,0:T(8,128)(2,1)} collective-permute-done((bf16[256,768]{1,0:T(8,128)(2,1)}, bf16[256,768]{1,0:T(8,128)(2,1)}, u32[]{:S(2)}, u32[]{:S(2)}) %collective-permute-start.10) | collective-permute-done | bytes 393248 | tf_op jit(solution)/shard_map/gather/ppermute | solution.py:159
  132.9 2.9 %products.3 = bf16[512,1024]{1,0:T(8,128)(2,1)S(1)} custom-call(s32[1]{0:T(128)} %bitcast.3.chip_ref, f32[512,1024]{1,0:T(8,128)S(1)} %products.2.total_ref, bf16[256,768]{1,0:T(8,128)(2,1)} %collective-permute-done.10.refs_0_, bf16[256,768]{1,0:T(8,128)(2,1)S(1)} %collective-permute-done.11.refs_1_, bf16[512,3072]{1,0:T(8,128)(2,1)S(1)} %bitcast.18, ...), custom_call_target="tpu_custom_call" | custom-call | flops 805306368 | bytes 4194304 | tf_op jit(solution)/shard_map/products/pallas_call | solution.py:116
  135.8 60.0 %all_to_all.27 = bf16[64,8,1024]{2,1,0:T(8,128)(2,1)S(1)} all-to-all(bf16[64,8,1024]{2,1,0:T(8,128)(2,1)S(1)} %bitcast.15), channel_id=1, replica_groups=mesh['expert'=64,'tensor'=8] {'expert'}, dimensions={0} | all-to-all | bytes 2097152 | tf_op jit(solution)/shard_map/return/all_to_all | solution.py:200
  195.8 2.8 %collective-permute-start.12 = (bf16[512,512]{1,0:T(8,128)(2,1)S(1)}, bf16[512,512]{1,0:T(8,128)(2,1)S(1)}, u32[]{:S(2)}, u32[]{:S(2)}) collective-permute-start(bf16[512,512]{1,0:T(8,128)(2,1)S(1)} %get-tuple-element.11), channel_id=1, source_target_pairs={{0,1},{1,0},{2,3},{3,2},{4,5},{5,4},{6,7},{7,6},{8,9},{9,8},{10,11... | collective-permute-start | bytes 1572872 | tf_op jit(solution)/shard_map/finish/ppermute | solution.py:162
  198.9 1.2 collective-permute-done.12
  200.2 0.9 multiply_reduce_fusion
  201.1 0.6 broadcast_in_dim.4
  201.7 3.6 %all-to-all-start.2 = ((f32[8,1,512]{2,1,0:T(1,128)}), f32[8,1,512]{2,1,0:T(1,128)S(1)}, u32[]{:S(2)}, u32[]{:S(2)}) async-start(f32[8,1,512]{2,1,0:T(1,128)} %broadcast_in_dim.4), calls=%async_computation.2 | async-start | bytes 32768 | tf_op jit(solution)/shard_map/finish/all_to_all | solution.py:209
  205.3 1.0 copy.13
  206.3 4.0 %all-to-all-done.2 = f32[8,1,512]{2,1,0:T(1,128)S(1)} async-done(((f32[8,1,512]{2,1,0:T(1,128)}), f32[8,1,512]{2,1,0:T(1,128)S(1)}, u32[]{:S(2)}, u32[]{:S(2)}) %all-to-all-start.2) | async-done | bytes 16416 | tf_op jit(solution)/shard_map/finish/all_to_all | solution.py:209
  (34 shorter events, 1.6 us)
Async XLA Ops:
  0.6 30.7 %copy-start = (bf16[1,512,3072]{2,1,0:T(8,128)(2,1)S(1)}, bf16[1,512,3072]{2,1,0:T(8,128)(2,1)}, u32[]{:S(2)}) copy-start(bf16[1,512,3072]{2,1,0:T(8,128)(2,1)} %param.9) | copy-start | bytes 9437188
  0.6 11.4 %collective-permute-start = (bf16[512,384]{1,0:T(8,128)(2,1)}, bf16[512,384]{1,0:T(8,128)(2,1)S(1)}, u32[]{:S(2)}, u32[]{:S(2)}) collective-permute-start(bf16[512,384]{1,0:T(8,128)(2,1)} %mine_ref.1), channel_id=1, source_target_pairs={{0,1},{1,0},{2,3},{3,2},{4,5},{5,4},{6,7},{7,6},{8,9},{9,8},{10,11... | collective-permute-start | bytes 1179656 | tf_op jit(solution)/shard_map/route/ppermute | solution.py:162
  12.1 0.7 copy-start.14
  15.5 52.4 %all-to-all-start = ((bf16[64,8,768]{2,1,0:T(8,128)(2,1)}), bf16[64,8,768]{2,1,0:T(8,128)(2,1)}, u32[]{:S(2)}, u32[]{:S(2)}) async-start(bf16[64,8,768]{2,1,0:T(8,128)(2,1)} %bitcast.20), calls=%async_computation | async-start | bytes 1572864 | tf_op jit(solution)/shard_map/dispatch/all_to_all | solution.py:183
  31.3 86.8 %collective-permute-start.9 = (bf16[512,3072]{1,0:T(8,128)(2,1)S(1)}, bf16[512,3072]{1,0:T(8,128)(2,1)}, u32[]{:S(2)}, u32[]{:S(2)}) collective-permute-start(bf16[512,3072]{1,0:T(8,128)(2,1)S(1)} %bitcast.16), channel_id=1, source_target_pairs={{0,1},{1,0},{2,3},{3,2},{4,5},{5,4},{6,7},{7,6},{8,9},{9,8},{10,11... | collective-permute-start | bytes 9437192 | tf_op jit(solution)/shard_map/weights/ppermute | solution.py:162
  69.1 18.9 %collective-permute-start.5 = (bf16[256,768]{1,0:T(8,128)(2,1)S(1)}, bf16[256,768]{1,0:T(8,128)(2,1)S(1)}, u32[]{:S(2)}, u32[]{:S(2)}) collective-permute-start(bf16[256,768]{1,0:T(8,128)(2,1)S(1)} %get-tuple-element.12.refs_4_), channel_id=1, source_target_pairs={{0,2},{1,3},{2,4},{3,5},{4,6},{5,7},{8,10},{9,11},{10,12},{11,13},... | collective-permute-start | bytes 1179656 | tf_op jit(solution)/shard_map/gather/ppermute | solution.py:159
  79.9 10.2 %collective-permute-start.6 = (bf16[256,768]{1,0:T(8,128)(2,1)S(1)}, bf16[256,768]{1,0:T(8,128)(2,1)S(1)}, u32[]{:S(2)}, u32[]{:S(2)}) collective-permute-start(bf16[256,768]{1,0:T(8,128)(2,1)S(1)} %get-tuple-element.12.refs_4_), channel_id=1, source_target_pairs={{2,0},{3,1},{4,2},{5,3},{6,4},{7,5},{10,8},{11,9},{12,10},{13,11},... | collective-permute-start | bytes 1179656 | tf_op jit(solution)/shard_map/gather/ppermute | solution.py:159
  81.2 0.8 copy-start.1
  82.0 13.0 %collective-permute-start.1 = (bf16[256,768]{1,0:T(8,128)(2,1)S(1)}, bf16[256,768]{1,0:T(8,128)(2,1)S(1)}, u32[]{:S(2)}, u32[]{:S(2)}) collective-permute-start(bf16[256,768]{1,0:T(8,128)(2,1)S(1)} %get-tuple-element.13.refs_0_), channel_id=1, source_target_pairs={{0,2},{1,3},{2,4},{3,5},{4,6},{5,7},{8,10},{9,11},{10,12},{11,13},... | collective-permute-start | bytes 1179656 | tf_op jit(solution)/shard_map/gather/ppermute | solution.py:159
  86.0 13.1 %collective-permute-start.2 = (bf16[256,768]{1,0:T(8,128)(2,1)S(1)}, bf16[256,768]{1,0:T(8,128)(2,1)S(1)}, u32[]{:S(2)}, u32[]{:S(2)}) collective-permute-start(bf16[256,768]{1,0:T(8,128)(2,1)S(1)} %get-tuple-element.13.refs_0_), channel_id=1, source_target_pairs={{2,0},{3,1},{4,2},{5,3},{6,4},{7,5},{10,8},{11,9},{12,10},{13,11},... | collective-permute-start | bytes 1179656 | tf_op jit(solution)/shard_map/gather/ppermute | solution.py:159
  87.3 0.7 copy-start.3
  88.0 12.3 %collective-permute-start.7 = (bf16[256,768]{1,0:T(8,128)(2,1)S(1)}, bf16[256,768]{1,0:T(8,128)(2,1)S(1)}, u32[]{:S(2)}, u32[]{:S(2)}) collective-permute-start(bf16[256,768]{1,0:T(8,128)(2,1)S(1)} %collective-permute-done.5.refs_5_), channel_id=1, source_target_pairs={{2,4},{3,5},{4,6},{5,7},{10,12},{11,13},{12,14},{13,15},{18,20},{1... | collective-permute-start | bytes 1179656 | tf_op jit(solution)/shard_map/gather/ppermute | solution.py:159
  88.7 0.8 copy-start.5
  90.1 17.4 %collective-permute-start.8 = (bf16[256,768]{1,0:T(8,128)(2,1)S(1)}, bf16[256,768]{1,0:T(8,128)(2,1)S(1)}, u32[]{:S(2)}, u32[]{:S(2)}) collective-permute-start(bf16[256,768]{1,0:T(8,128)(2,1)S(1)} %collective-permute-done.6.refs_6_), channel_id=1, source_target_pairs={{4,2},{5,3},{2,0},{3,1},{12,10},{13,11},{10,8},{11,9},{20,18},{21,... | collective-permute-start | bytes 1179656 | tf_op jit(solution)/shard_map/gather/ppermute | solution.py:159
  91.4 0.7 copy-start.7
  94.9 14.7 %collective-permute-start.3 = (bf16[256,768]{1,0:T(8,128)(2,1)S(1)}, bf16[256,768]{1,0:T(8,128)(2,1)S(1)}, u32[]{:S(2)}, u32[]{:S(2)}) collective-permute-start(bf16[256,768]{1,0:T(8,128)(2,1)S(1)} %collective-permute-done.1.refs_1_), channel_id=1, source_target_pairs={{2,4},{3,5},{4,6},{5,7},{10,12},{11,13},{12,14},{13,15},{18,20},{1... | collective-permute-start | bytes 1179656 | tf_op jit(solution)/shard_map/gather/ppermute | solution.py:159
  95.6 0.7 copy-start.9
  99.1 10.6 %copy-start.11 = (bf16[256,768]{1,0:T(8,128)(2,1)}, bf16[256,768]{1,0:T(8,128)(2,1)S(1)}, u32[]{:S(2)}) copy-start(bf16[256,768]{1,0:T(8,128)(2,1)S(1)} %collective-permute-done.2.refs_2_) | copy-start | bytes 1179652
  99.1 16.9 %collective-permute-start.4 = (bf16[256,768]{1,0:T(8,128)(2,1)S(1)}, bf16[256,768]{1,0:T(8,128)(2,1)S(1)}, u32[]{:S(2)}, u32[]{:S(2)}) collective-permute-start(bf16[256,768]{1,0:T(8,128)(2,1)S(1)} %collective-permute-done.2.refs_2_), channel_id=1, source_target_pairs={{4,2},{5,3},{2,0},{3,1},{12,10},{13,11},{10,8},{11,9},{20,18},{21,... | collective-permute-start | bytes 1179656 | tf_op jit(solution)/shard_map/gather/ppermute | solution.py:159
  108.4 21.9 %collective-permute-start.11 = (bf16[256,768]{1,0:T(8,128)(2,1)}, bf16[256,768]{1,0:T(8,128)(2,1)S(1)}, u32[]{:S(2)}, u32[]{:S(2)}) collective-permute-start(bf16[256,768]{1,0:T(8,128)(2,1)} %add.84.refs_7_), channel_id=1, source_target_pairs={{4,6},{5,7},{2,0},{3,1},{12,14},{13,15},{10,8},{11,9},{20,22},{21,... | collective-permute-start | bytes 1179656 | tf_op jit(solution)/shard_map/gather/ppermute | solution.py:159
  116.8 16.1 %collective-permute-start.10 = (bf16[256,768]{1,0:T(8,128)(2,1)}, bf16[256,768]{1,0:T(8,128)(2,1)}, u32[]{:S(2)}, u32[]{:S(2)}) collective-permute-start(bf16[256,768]{1,0:T(8,128)(2,1)} %add.83.refs_3_), channel_id=1, source_target_pairs={{4,6},{5,7},{2,0},{3,1},{12,14},{13,15},{10,8},{11,9},{20,22},{21,... | collective-permute-start | bytes 1179656 | tf_op jit(solution)/shard_map/gather/ppermute | solution.py:159
  118.1 1.0 copy-start.2
  119.1 1.0 copy-start.4
  120.1 1.0 copy-start.6
  121.1 1.0 copy-start.8
  122.1 1.0 copy-start.10
  123.1 1.0 copy-start.12
  135.8 62.9 %copy-start.13 = (bf16[512,512]{1,0:T(8,128)(2,1)S(1)}, bf16[512,512]{1,0:T(8,128)(2,1)}, u32[]{:S(2)}) copy-start(bf16[512,512]{1,0:T(8,128)(2,1)} %param.6) | copy-start | bytes 1572868
  195.8 3.1 %copy-start.15 = (s32[512,1]{0,1:T(1,128)S(1)}, s32[512,1]{0,1:T(1,128)}, u32[]{:S(2)}) copy-start(s32[512,1]{0,1:T(1,128)} %param.8) | copy-start | bytes 6148
  195.8 4.4 %copy-start.16 = (f32[512]{0:T(512)S(1)}, f32[512]{0:T(512)}, u32[]{:S(2)}) copy-start(f32[512]{0:T(512)} %param.7) | copy-start | bytes 6148
  195.8 4.3 %collective-permute-start.12 = (bf16[512,512]{1,0:T(8,128)(2,1)S(1)}, bf16[512,512]{1,0:T(8,128)(2,1)S(1)}, u32[]{:S(2)}, u32[]{:S(2)}) collective-permute-start(bf16[512,512]{1,0:T(8,128)(2,1)S(1)} %get-tuple-element.11), channel_id=1, source_target_pairs={{0,1},{1,0},{2,3},{3,2},{4,5},{5,4},{6,7},{7,6},{8,9},{9,8},{10,11... | collective-permute-start | bytes 1572872 | tf_op jit(solution)/shard_map/finish/ppermute | solution.py:162
  201.7 8.6 %all-to-all-start.2 = ((f32[8,1,512]{2,1,0:T(1,128)}), f32[8,1,512]{2,1,0:T(1,128)S(1)}, u32[]{:S(2)}, u32[]{:S(2)}) async-start(f32[8,1,512]{2,1,0:T(1,128)} %broadcast_in_dim.4), calls=%async_computation.2 | async-start | bytes 32768 | tf_op jit(solution)/shard_map/finish/all_to_all | solution.py:209

commit v4 on v3

v4 whole, which is shorter than its diff:
```python
import functools

import jax
import jax.numpy as jnp
from jax import lax
from jax.experimental import pallas as pl
from jax.experimental.pallas import tpu as pltpu
from jax.sharding import PartitionSpec as P

CORES = 2
HALVES = 2
KINDS = 5


def line_shards(chip, chips):
    edge = (chip == 0) | (chip == chips - 1)
    shards = [chip, chip - 1, chip + 1, lax.rem(chip + 2, chips), chips - 1 - chip]
    valid = [chip >= 0, chip > 0, chip < chips - 1, chip >= 0, edge]
    return [jnp.clip(s, 0, chips - 1) for s in shards], valid


def near_kernel(place_ref, *refs):
    kinds = KINDS - 1
    count = HALVES * kinds
    pieces, sources = refs[:count], refs[count : count + CORES]
    out, tokens, weights, token_sems, weight_sems = refs[count + CORES :]
    width = pieces[0].shape[1]
    hidden = weights.shape[1]
    core = place_ref[1]
    shards, valid = line_shards(place_ref[0], tokens.shape[1] // (width * HALVES))

    def columns(h, k):
        block = shards[k] * HALVES + (core if h == 0 else 1 - core)
        return pl.ds(pl.multiple_of(block * width, 128), width)

    def token_copy(n):
        return pltpu.make_async_copy(pieces[n], tokens.at[:, columns(*divmod(n, kinds))], token_sems.at[n])

    def weight_copy(n):
        return pltpu.make_async_copy(sources[n], weights.at[n], weight_sems.at[n])

    @pl.when(valid[-1])
    def _():
        for h in range(HALVES):
            tokens[:, columns(h, KINDS - 1)] = jnp.zeros((tokens.shape[0], width), tokens.dtype)

    weight_copy(0).start()
    for n in range(count):
        pl.when(valid[n % kinds])(token_copy(n).start)
    weight_copy(1).start()
    for n in range(count):
        pl.when(valid[n % kinds])(token_copy(n).wait)
    for n in range(CORES):
        weight_copy(n).wait()
        out[:, n * hidden : (n + 1) * hidden] = lax.dot_general(
            tokens[...], weights[n], (((1,), (1,)), ((), ())), preferred_element_type=jnp.float32
        )


def last_kernel(chips, place_ref, total_ref, *refs):
    pieces, sources, out = refs[:HALVES], refs[HALVES : HALVES + CORES], refs[HALVES + CORES]
    weights, sems = refs[HALVES + CORES + 1 :]
    width = pieces[0].shape[1]
    hidden = weights.shape[2]
    core = place_ref[1]
    shards, valid = line_shards(place_ref[0], chips)

    def weight_copy(h, n):
        block = shards[-1] * HALVES + (core if h == 0 else 1 - core)
        part = sources[n].at[:, pl.ds(pl.multiple_of(block * width, 128), width)]
        return pltpu.make_async_copy(part, weights.at[h, n], sems.at[h, n])

    @pl.when(valid[-1])
    def _():
        for n in range(CORES):
            for h in range(HALVES):
                weight_copy(h, n).start()
        for n in range(CORES):
            here = slice(n * hidden, (n + 1) * hidden)
            more = total_ref[:, here]
            for h in range(HALVES):
                weight_copy(h, n).wait()
                more = more + lax.dot_general(
                    pieces[h][...], weights[h, n], (((1,), (1,)), ((), ())), preferred_element_type=jnp.float32
                )
            out[:, here] = more.astype(out.dtype)

    @pl.when(jnp.logical_not(valid[-1]))
    def _():
        out[...] = total_ref[...].astype(out.dtype)


HBM = pl.BlockSpec(memory_space=pltpu.HBM)
SMEM = pl.BlockSpec(memory_space=pltpu.SMEM)
VMEM = pl.BlockSpec(memory_space=pltpu.VMEM)


def multiply_near(where, pieces, weights):
    rows = pieces[0].shape[0]
    hidden, depth = weights[0].shape
    return pl.pallas_call(
        near_kernel,
        out_shape=jax.ShapeDtypeStruct((rows, CORES * hidden), jnp.float32),
        in_specs=[SMEM] + [HBM] * (len(pieces) + CORES),
        out_specs=VMEM,
        scratch_shapes=[
            pltpu.VMEM((rows, depth), jnp.bfloat16),
            pltpu.VMEM((CORES, hidden, depth), jnp.bfloat16),
            pltpu.SemaphoreType.DMA((HALVES * (KINDS - 1),)),
            pltpu.SemaphoreType.DMA((CORES,)),
        ],
        compiler_params=pltpu.CompilerParams(vmem_limit_bytes=32 * 1024 * 1024),
        cost_estimate=pl.CostEstimate(
            flops=2 * CORES * rows * hidden * depth, bytes_accessed=2 * (rows + CORES * hidden) * depth, transcendentals=0
        ),
    )(where, *pieces, *weights)


def multiply_last(where, chips, total, pieces, weights):
    width = pieces[0].shape[1]
    hidden = weights[0].shape[0]
    return pl.pallas_call(
        functools.partial(last_kernel, chips),
        out_shape=jax.ShapeDtypeStruct(total.shape, jnp.bfloat16),
        in_specs=[SMEM] + [VMEM] * (1 + HALVES) + [HBM] * CORES,
        out_specs=VMEM,
        scratch_shapes=[
            pltpu.VMEM((HALVES, CORES, hidden, width), jnp.bfloat16),
            pltpu.SemaphoreType.DMA((HALVES, CORES)),
        ],
        compiler_params=pltpu.CompilerParams(vmem_limit_bytes=24 * 1024 * 1024),
        cost_estimate=pl.CostEstimate(
            flops=2 * HALVES * total.size * width, bytes_accessed=8 * total.size, transcendentals=0
        ),
    )(where, total, *pieces, *weights)


def route_kernel(capacity, ids_ref, rows_ref, send_ref, target_ref):
    tokens = rows_ref.shape[0]
    slots = send_ref.shape[0]
    ids = ids_ref[...]
    chosen = (lax.broadcasted_iota(jnp.int32, (slots // capacity, tokens), 0) == ids).astype(jnp.float32)
    before = (
        lax.broadcasted_iota(jnp.int32, (tokens, tokens), 0) < lax.broadcasted_iota(jnp.int32, (tokens, tokens), 1)
    ).astype(jnp.bfloat16)
    counts = jnp.dot(chosen.astype(jnp.bfloat16), before, preferred_element_type=jnp.float32)
    earlier = jnp.sum(chosen * counts, axis=0, keepdims=True)
    target = ids * capacity + earlier.astype(jnp.int32)
    target_ref[...] = target
    place = (lax.broadcasted_iota(jnp.int32, (slots, tokens), 0) == target).astype(jnp.bfloat16)
    send_ref[...] = jnp.dot(place, rows_ref[...], preferred_element_type=jnp.float32).astype(send_ref.dtype)


def body(grad_out, hidden_in, gate_prob, expert_ids, w_down):
    tokens, width = grad_out.shape
    groups = lax.axis_size("expert")
    shards = lax.axis_size("tensor")
    chips = shards // CORES
    experts = w_down.shape[0] * groups
    capacity = 2 * tokens // experts
    share = capacity // CORES
    slots = experts * capacity
    weight = w_down[0]
    hidden = weight.shape[0]
    bf16, f32 = jnp.bfloat16, jnp.float32

    position = lax.axis_index("tensor").astype(jnp.int32)
    chip, core = position // CORES, position % CORES
    core_pairs = [(p, p ^ 1) for p in range(shards)]

    def line(array, pairs, flip=0):
        return lax.ppermute(
            array, "tensor", [(a * CORES + c, b * CORES + (c ^ flip)) for a, b in pairs for c in range(CORES)]
        )

    def swap(array):
        return lax.ppermute(array, "tensor", core_pairs)

    with jax.named_scope("route"):
        send, target = pl.pallas_call(
            functools.partial(route_kernel, capacity),
            out_shape=[jax.ShapeDtypeStruct((slots, width), bf16), jax.ShapeDtypeStruct((1, tokens), jnp.int32)],
        )(expert_ids.reshape(1, tokens), grad_out)

    with jax.named_scope("dispatch"):
        got = lax.all_to_all(send, "expert", split_axis=0, concat_axis=0, tiled=True)
        got = got.reshape(groups, CORES, share, width)

    with jax.named_scope("gather"):
        weights = [weight, swap(weight)]
        def part(c):
            return lax.dynamic_index_in_dim(got, c, axis=1, keepdims=False).reshape(groups * share, width)

        def gather(x, flip):
            right = line(x, [(0, 1), (1, 2), (2, 3)], flip)
            left = line(x, [(1, 0), (2, 1), (3, 2)], flip)
            second = line(right, [(1, 2), (2, 3)]) + line(left, [(2, 1), (1, 0)])
            return [swap(x) if flip else x, right, left, second, line(second, [(2, 3), (1, 0)])]

        halves = [gather(part(core), 0), gather(part(1 - core), 1)]

    with jax.named_scope("products"):
        where = jnp.stack([chip, core])
        total = multiply_near(where, halves[0][:-1] + halves[1][:-1], weights)
        filled = multiply_last(where, chips, total, [halves[0][-1], halves[1][-1]], weights)

    with jax.named_scope("return"):
        back = lax.all_to_all(filled, "expert", split_axis=0, concat_axis=0, tiled=True)

    with jax.named_scope("finish"):
        target = target.reshape(tokens)
        away = jnp.where(target % capacity // share == core, 0, 1)
        local = away * (slots // CORES) + target // capacity * share + target % share
        pick = (local[:, None] == jnp.arange(slots, dtype=jnp.int32)[None, :]).astype(bf16)
        back = jnp.concatenate([back[:, :hidden], swap(back[:, hidden:])], axis=0)
        returned = jnp.dot(pick, back, preferred_element_type=f32)
        grad_hidden = (gate_prob[:, None] * returned).astype(bf16)
        gate_part = jnp.sum(hidden_in.astype(f32) * returned, axis=1)
        parts = jnp.broadcast_to(gate_part[None, :], (shards, tokens))
        gate = jnp.sum(lax.all_to_all(parts, "tensor", split_axis=0, concat_axis=0, tiled=True), axis=0)
    return grad_hidden, gate


def solution(mesh):
    return jax.shard_map(
        body,
        mesh=mesh,
        in_specs=(
            P("expert", "tensor"),
            P("expert", "tensor"),
            P("expert"),
            P("expert", None),
            P("expert", "tensor", None),
        ),
        out_specs=(P("expert", "tensor"), P("expert")),
        check_vma=False,
    )
```

time: 212 us -> 208 us (0.981)
  starting transfers between devices: 57.3 us -> 67.5 us
  local copies, waits for them, and re-layouts: 14.1 us -> 5.37 us
  waiting for transfers between devices: 61.7 us -> 59.4 us
    unnamed x36 -> x16, local copies, waits for them, and re-layouts: 11.7 us -> 2.74 us
    ppermute x10, starting transfers between devices: 23.9 us -> 30.6 us  [line(): lax.ppermute(array, 'tensor', [(a * CORES + c, b * CORES + (c ^ flip)) fo...]
    all_to_all x1, starting transfers between devices: 15.8 us -> 22 us  [body(): lax.all_to_all(send, 'expert', split_axis=0, concat_axis=0, tiled=True)]
    all_to_all x1, waiting for transfers between devices: 34.4 us -> 29.4 us  [body(): lax.all_to_all(send, 'expert', split_axis=0, concat_axis=0, tiled=True)]
    ppermute x3, starting transfers between devices: 14 us -> 10.6 us  [swap(): return lax.ppermute(array, 'tensor', core_pairs)]
    ppermute x10, waiting for transfers between devices: 22.1 us -> 24.8 us  [line(): lax.ppermute(array, 'tensor', [(a * CORES + c, b * CORES + (c ^ flip)) fo...]
  transfers between devices with their start and end apart: 15 -> 15, of which waited for: 9 -> 10; matrix products, arithmetic and copies ran while one was open for 3% -> 3% of each run, Pallas kernels for 3% -> 3%
where the time goes in v4:
time: 208 us
  starting transfers between devices  67.5 us (32%)
  waiting for transfers between devices  59.4 us (29%)
  blocking collectives  59.1 us (28%)
  Pallas kernels  11.2 us (5%)
  local copies, waits for them, and re-layouts  5.37 us (3%)
  other arithmetic  3.13 us (2%)
    all_to_all x1, blocking collectives, body(): lax.all_to_all(filled, 'expert', split_axis=0, concat_axis=0, tiled=True)  59.1 us
    ppermute x10, starting transfers between devices, line(): lax.ppermute(array, 'tensor', [(a * CORES + c, b * CORES + (c ^ flip)) fo...  30.6 us
    all_to_all x1, waiting for transfers between devices, body(): lax.all_to_all(send, 'expert', split_axis=0, concat_axis=0, tiled=True)  29.4 us
    ppermute x10, waiting for transfers between devices, line(): lax.ppermute(array, 'tensor', [(a * CORES + c, b * CORES + (c ^ flip)) fo...  24.8 us
    all_to_all x1, starting transfers between devices, body(): lax.all_to_all(send, 'expert', split_axis=0, concat_axis=0, tiled=True)  22 us
    ppermute x3, starting transfers between devices, swap(): return lax.ppermute(array, 'tensor', core_pairs)  10.6 us
    pallas_call x1, Pallas kernels, multiply_near(): pl.pallas_call(near_kernel, out_shape=jax.ShapeDtypeStruct((rows, CORES *...  5.9 us
    all_to_all x1, starting transfers between devices, body(): lax.all_to_all(parts, 'tensor', split_axis=0, concat_axis=0, tiled=True)  4.3 us
  transfers between devices with their start and end apart: 15, of which 10 were waited for; matrix products, arithmetic and copies ran while one was open for 3% of the time, Pallas kernels for 3%

profile of v4, /device:TPU:1, one launch (start us, length us, event | category | flops | bytes accessed | tf_op | source)
XLA Modules:
  0.0 207.6 jit_solution(10163278119951678125)
XLA Ops:
  0.6 2.8 %route.1 = (bf16[1024,384]{1,0:T(8,128)(2,1)}, s32[1,512]{1,0:T(1,128)}) custom-call(s32[1,512]{1,0:T(1,128)} %bitcast.19, bf16[512,384]{1,0:T(8,128)(2,1)} %rows_ref.1), custom_call_target="tpu_custom_call" | custom-call | tf_op jit(solution)/shard_map/route/pallas_call | solution.py:180
  3.4 22.0 %all-to-all-start = ((bf16[64,16,384]{2,1,0:T(8,128)(2,1)}), bf16[64,16,384]{2,1,0:T(8,128)(2,1)}, u32[]{:S(2)}, u32[]{:S(2)}) async-start(bf16[64,16,384]{2,1,0:T(8,128)(2,1)} %bitcast.18), calls=%async_computation | async-start | bytes 1572864 | tf_op jit(solution)/shard_map/dispatch/all_to_all | solution.py:186
  25.4 0.0 copy-start
  25.4 3.1 %collective-permute-start.9 = (bf16[512,3072]{1,0:T(8,128)(2,1)}, bf16[512,3072]{1,0:T(8,128)(2,1)}, u32[]{:S(2)}, u32[]{:S(2)}) collective-permute-start(bf16[512,3072]{1,0:T(8,128)(2,1)} %bitcast.14), channel_id=1, source_target_pairs={{0,1},{1,0},{2,3},{3,2},{4,5},{5,4},{6,7},{7,6},{8,9},{9,8},{10,11... | collective-permute-start | bytes 9437192 | tf_op jit(solution)/shard_map/gather/ppermute | solution.py:177
  28.6 29.4 %all-to-all-done = bf16[64,16,384]{2,1,0:T(8,128)(2,1)} async-done(((bf16[64,16,384]{2,1,0:T(8,128)(2,1)}), bf16[64,16,384]{2,1,0:T(8,128)(2,1)}, u32[]{:S(2)}, u32[]{:S(2)}) %all-to-all-start) | async-done | bytes 786464 | tf_op jit(solution)/shard_map/dispatch/all_to_all | solution.py:186
  58.0 1.9 dynamic-slice_bitcast_fusion
  60.0 16.7 %collective-permute-start.5 = (bf16[512,384]{1,0:T(8,128)(2,1)}, bf16[512,384]{1,0:T(8,128)(2,1)S(1)}, u32[]{:S(2)}, u32[]{:S(2)}) collective-permute-start(bf16[512,384]{1,0:T(8,128)(2,1)} %get-tuple-element.18), channel_id=1, source_target_pairs={{0,3},{1,2},{2,5},{3,4},{4,7},{5,6},{8,11},{9,10},{10,13},{11,12},... | collective-permute-start | bytes 1179656 | tf_op jit(solution)/shard_map/gather/ppermute | solution.py:172
  76.7 1.3 collective-permute-start.6
  78.0 4.1 %collective-permute-start = (bf16[512,384]{1,0:T(8,128)(2,1)S(1)}, bf16[512,384]{1,0:T(8,128)(2,1)}, u32[]{:S(2)}, u32[]{:S(2)}) collective-permute-start(bf16[512,384]{1,0:T(8,128)(2,1)S(1)} %get-tuple-element.19.refs_0_), channel_id=1, source_target_pairs={{0,2},{1,3},{2,4},{3,5},{4,6},{5,7},{8,10},{9,11},{10,12},{11,13},... | collective-permute-start | bytes 1179656 | tf_op jit(solution)/shard_map/gather/ppermute | solution.py:172
  82.1 1.3 collective-permute-start.1
  83.4 1.8 collective-permute-done.5.refs_5_
  85.2 0.7 collective-permute-start.7
  85.9 0.8 copy-done.1
  86.7 3.7 %collective-permute-done.6.refs_6_ = bf16[512,384]{1,0:T(8,128)(2,1)} collective-permute-done((bf16[512,384]{1,0:T(8,128)(2,1)}, bf16[512,384]{1,0:T(8,128)(2,1)}, u32[]{:S(2)}, u32[]{:S(2)}) %collective-permute-start.6) | collective-permute-done | bytes 393248 | tf_op jit(solution)/shard_map/gather/ppermute | solution.py:172
  90.3 1.3 collective-permute-start.8
  91.6 1.1 collective-permute-done.refs_1_
  92.7 1.4 collective-permute-start.2
  94.1 2.5 %collective-permute-done.1.refs_2_ = bf16[512,384]{1,0:T(8,128)(2,1)} collective-permute-done((bf16[512,384]{1,0:T(8,128)(2,1)S(1)}, bf16[512,384]{1,0:T(8,128)(2,1)}, u32[]{:S(2)}, u32[]{:S(2)}) %collective-permute-start.1) | collective-permute-done | bytes 393248 | tf_op jit(solution)/shard_map/gather/ppermute | solution.py:172
  96.6 1.3 collective-permute-start.3
  97.9 0.0 collective-permute-done.7
  97.9 0.7 copy-done.4
  98.7 4.7 %collective-permute-start.4 = (bf16[512,384]{1,0:T(8,128)(2,1)}, bf16[512,384]{1,0:T(8,128)(2,1)}, u32[]{:S(2)}, u32[]{:S(2)}) collective-permute-start(bf16[512,384]{1,0:T(8,128)(2,1)} %get-tuple-element.18), channel_id=1, source_target_pairs={{0,1},{1,0},{2,3},{3,2},{4,5},{5,4},{6,7},{7,6},{8,9},{9,8},{10,11... | collective-permute-start | bytes 1179656 | tf_op jit(solution)/shard_map/gather/ppermute | solution.py:177
  103.4 1.6 collective-permute-done.8
  105.1 1.2 add.69.refs_7_
  106.3 1.3 collective-permute-start.11
  107.6 0.0 collective-permute-done.2
  107.6 5.9 %collective-permute-done.3 = bf16[512,384]{1,0:T(8,128)(2,1)} collective-permute-done((bf16[512,384]{1,0:T(8,128)(2,1)}, bf16[512,384]{1,0:T(8,128)(2,1)}, u32[]{:S(2)}, u32[]{:S(2)}) %collective-permute-start.3) | collective-permute-done | bytes 393248 | tf_op jit(solution)/shard_map/gather/ppermute | solution.py:172
  113.5 1.2 add.67.refs_3_
  114.7 1.3 collective-permute-start.10
  116.0 0.1 pad_add_fusion.place_ref
  116.1 0.0 collective-permute-done.9.refs_9_.refs_3_
  116.1 0.0 collective-permute-done.4.refs_4_
  116.1 5.9 %products.2.total_ref = f32[512,1024]{1,0:T(8,128)S(1)} custom-call(s32[2]{0:T(128)S(1)} %pad_add_fusion.place_ref, bf16[512,384]{1,0:T(8,128)(2,1)S(1)} %get-tuple-element.19.refs_0_, bf16[512,384]{1,0:T(8,128)(2,1)} %collective-permute-done.refs_1_, bf16[512,384]{1,0:T(8,128)(2,1)} %collective-permute-done.1.refs_2_, bf16[512,384]{1,0:T(8,128)(2,1)S(1)} %add.67.refs_3_, ...), custom_call_target="tpu_custom_call" | custom-call | flops 3221225472 | bytes 9437184 | tf_op jit(solution)/shard_map/products/pallas_call | solution.py:101
  122.0 0.0 collective-permute-done.11.refs_1_
  122.0 8.2 %collective-permute-done.10.refs_0_ = bf16[512,384]{1,0:T(8,128)(2,1)S(1)} collective-permute-done((bf16[512,384]{1,0:T(8,128)(2,1)S(1)}, bf16[512,384]{1,0:T(8,128)(2,1)S(1)}, u32[]{:S(2)}, u32[]{:S(2)}) %collective-permute-start.10) | collective-permute-done | bytes 393248 | tf_op jit(solution)/shard_map/gather/ppermute | solution.py:172
  130.2 2.5 %products.3 = bf16[512,1024]{1,0:T(8,128)(2,1)S(1)} custom-call(s32[2]{0:T(128)S(1)} %pad_add_fusion.place_ref, f32[512,1024]{1,0:T(8,128)S(1)} %products.2.total_ref, bf16[512,384]{1,0:T(8,128)(2,1)S(1)} %collective-permute-done.10.refs_0_, bf16[512,384]{1,0:T(8,128)(2,1)S(1)} %collective-permute-done.11.refs_1_, bf16[512,3072]{1,0:T(8,128)(2,1)S(1)} %bitcast.16, ...), custom_call_target="tpu_custom_call" | custom-call | flops 805306368 | bytes 4194304 | tf_op jit(solution)/shard_map/products/pallas_call | solution.py:122
  132.7 0.0 copy-start.3
  132.8 59.1 %all_to_all.27 = bf16[64,8,1024]{2,1,0:T(8,128)(2,1)S(1)} all-to-all(bf16[64,8,1024]{2,1,0:T(8,128)(2,1)S(1)} %bitcast.13), channel_id=1, replica_groups=mesh['expert'=64,'tensor'=8] {'expert'}, dimensions={0} | all-to-all | bytes 2097152 | tf_op jit(solution)/shard_map/return/all_to_all | solution.py:208
  191.8 0.1 fusion.14
  191.9 2.8 %collective-permute-start.12 = (bf16[512,512]{1,0:T(8,128)(2,1)S(1)}, bf16[512,512]{1,0:T(8,128)(2,1)S(1)}, u32[]{:S(2)}, u32[]{:S(2)}) collective-permute-start(bf16[512,512]{1,0:T(8,128)(2,1)S(1)} %get-tuple-element.17), channel_id=1, source_target_pairs={{0,1},{1,0},{2,3},{3,2},{4,5},{5,4},{6,7},{7,6},{8,9},{9,8},{10,11... | collective-permute-start | bytes 1572872 | tf_op jit(solution)/shard_map/finish/ppermute | solution.py:177
  194.7 0.2 copy.13
  195.0 1.3 collective-permute-done.12
  196.2 0.9 multiply_reduce_fusion
  197.2 0.6 broadcast_in_dim.6
  197.8 4.3 %all-to-all-start.2 = ((f32[8,1,512]{2,1,0:T(1,128)}), f32[8,1,512]{2,1,0:T(1,128)S(1)}, u32[]{:S(2)}, u32[]{:S(2)}) async-start(f32[8,1,512]{2,1,0:T(1,128)} %broadcast_in_dim.6), calls=%async_computation.2 | async-start | bytes 32768 | tf_op jit(solution)/shard_map/finish/all_to_all | solution.py:220
  202.1 1.0 copy.15
  203.1 3.9 %all-to-all-done.2 = f32[8,1,512]{2,1,0:T(1,128)S(1)} async-done(((f32[8,1,512]{2,1,0:T(1,128)}), f32[8,1,512]{2,1,0:T(1,128)S(1)}, u32[]{:S(2)}, u32[]{:S(2)}) %all-to-all-start.2) | async-done | bytes 16416 | tf_op jit(solution)/shard_map/finish/all_to_all | solution.py:220
  207.0 0.6 reduce_sum.19
  (11 shorter events, 0.0 us)
Async XLA Ops:
  3.4 54.6 %all-to-all-start = ((bf16[64,16,384]{2,1,0:T(8,128)(2,1)}), bf16[64,16,384]{2,1,0:T(8,128)(2,1)}, u32[]{:S(2)}, u32[]{:S(2)}) async-start(bf16[64,16,384]{2,1,0:T(8,128)(2,1)} %bitcast.18), calls=%async_computation | async-start | bytes 1572864 | tf_op jit(solution)/shard_map/dispatch/all_to_all | solution.py:186
  25.4 90.7 %copy-start = (bf16[1,512,3072]{2,1,0:T(8,128)(2,1)S(1)}, bf16[1,512,3072]{2,1,0:T(8,128)(2,1)}, u32[]{:S(2)}) copy-start(bf16[1,512,3072]{2,1,0:T(8,128)(2,1)} %param.9) | copy-start | bytes 9437188
  25.4 90.6 %collective-permute-start.9 = (bf16[512,3072]{1,0:T(8,128)(2,1)}, bf16[512,3072]{1,0:T(8,128)(2,1)}, u32[]{:S(2)}, u32[]{:S(2)}) collective-permute-start(bf16[512,3072]{1,0:T(8,128)(2,1)} %bitcast.14), channel_id=1, source_target_pairs={{0,1},{1,0},{2,3},{3,2},{4,5},{5,4},{6,7},{7,6},{8,9},{9,8},{10,11... | collective-permute-start | bytes 9437192 | tf_op jit(solution)/shard_map/gather/ppermute | solution.py:177
  60.0 25.2 %collective-permute-start.5 = (bf16[512,384]{1,0:T(8,128)(2,1)}, bf16[512,384]{1,0:T(8,128)(2,1)S(1)}, u32[]{:S(2)}, u32[]{:S(2)}) collective-permute-start(bf16[512,384]{1,0:T(8,128)(2,1)} %get-tuple-element.18), channel_id=1, source_target_pairs={{0,3},{1,2},{2,5},{3,4},{4,7},{5,6},{8,11},{9,10},{10,13},{11,12},... | collective-permute-start | bytes 1179656 | tf_op jit(solution)/shard_map/gather/ppermute | solution.py:172
  76.7 13.6 %collective-permute-start.6 = (bf16[512,384]{1,0:T(8,128)(2,1)}, bf16[512,384]{1,0:T(8,128)(2,1)}, u32[]{:S(2)}, u32[]{:S(2)}) collective-permute-start(bf16[512,384]{1,0:T(8,128)(2,1)} %get-tuple-element.18), channel_id=1, source_target_pairs={{2,1},{3,0},{4,3},{5,2},{6,5},{7,4},{10,9},{11,8},{12,11},{13,10},... | collective-permute-start | bytes 1179656 | tf_op jit(solution)/shard_map/gather/ppermute | solution.py:172
  78.0 14.7 %collective-permute-start = (bf16[512,384]{1,0:T(8,128)(2,1)S(1)}, bf16[512,384]{1,0:T(8,128)(2,1)}, u32[]{:S(2)}, u32[]{:S(2)}) collective-permute-start(bf16[512,384]{1,0:T(8,128)(2,1)S(1)} %get-tuple-element.19.refs_0_), channel_id=1, source_target_pairs={{0,2},{1,3},{2,4},{3,5},{4,6},{5,7},{8,10},{9,11},{10,12},{11,13},... | collective-permute-start | bytes 1179656 | tf_op jit(solution)/shard_map/gather/ppermute | solution.py:172
  82.1 14.5 %collective-permute-start.1 = (bf16[512,384]{1,0:T(8,128)(2,1)S(1)}, bf16[512,384]{1,0:T(8,128)(2,1)}, u32[]{:S(2)}, u32[]{:S(2)}) collective-permute-start(bf16[512,384]{1,0:T(8,128)(2,1)S(1)} %get-tuple-element.19.refs_0_), channel_id=1, source_target_pairs={{2,0},{3,1},{4,2},{5,3},{6,4},{7,5},{10,8},{11,9},{12,10},{13,11},... | collective-permute-start | bytes 1179656 | tf_op jit(solution)/shard_map/gather/ppermute | solution.py:172
  85.2 12.7 %collective-permute-start.7 = (bf16[512,384]{1,0:T(8,128)(2,1)S(1)}, bf16[512,384]{1,0:T(8,128)(2,1)S(1)}, u32[]{:S(2)}, u32[]{:S(2)}) collective-permute-start(bf16[512,384]{1,0:T(8,128)(2,1)S(1)} %collective-permute-done.5.refs_5_), channel_id=1, source_target_pairs={{2,4},{3,5},{4,6},{5,7},{10,12},{11,13},{12,14},{13,15},{18,20},{1... | collective-permute-start | bytes 1179656 | tf_op jit(solution)/shard_map/gather/ppermute | solution.py:172
  85.9 0.8 copy-start.1
  90.3 14.7 %collective-permute-start.8 = (bf16[512,384]{1,0:T(8,128)(2,1)}, bf16[512,384]{1,0:T(8,128)(2,1)}, u32[]{:S(2)}, u32[]{:S(2)}) collective-permute-start(bf16[512,384]{1,0:T(8,128)(2,1)} %collective-permute-done.6.refs_6_), channel_id=1, source_target_pairs={{4,2},{5,3},{2,0},{3,1},{12,10},{13,11},{10,8},{11,9},{20,18},{21,... | collective-permute-start | bytes 1179656 | tf_op jit(solution)/shard_map/gather/ppermute | solution.py:172
  92.7 14.9 %collective-permute-start.2 = (bf16[512,384]{1,0:T(8,128)(2,1)}, bf16[512,384]{1,0:T(8,128)(2,1)}, u32[]{:S(2)}, u32[]{:S(2)}) collective-permute-start(bf16[512,384]{1,0:T(8,128)(2,1)} %collective-permute-done.refs_1_), channel_id=1, source_target_pairs={{2,4},{3,5},{4,6},{5,7},{10,12},{11,13},{12,14},{13,15},{18,20},{1... | collective-permute-start | bytes 1179656 | tf_op jit(solution)/shard_map/gather/ppermute | solution.py:172
  96.6 16.9 %collective-permute-start.3 = (bf16[512,384]{1,0:T(8,128)(2,1)}, bf16[512,384]{1,0:T(8,128)(2,1)}, u32[]{:S(2)}, u32[]{:S(2)}) collective-permute-start(bf16[512,384]{1,0:T(8,128)(2,1)} %collective-permute-done.1.refs_2_), channel_id=1, source_target_pairs={{4,2},{5,3},{2,0},{3,1},{12,10},{13,11},{10,8},{11,9},{20,18},{21,... | collective-permute-start | bytes 1179656 | tf_op jit(solution)/shard_map/gather/ppermute | solution.py:172
  97.9 0.7 copy-start.4
  98.7 17.4 %collective-permute-start.4 = (bf16[512,384]{1,0:T(8,128)(2,1)}, bf16[512,384]{1,0:T(8,128)(2,1)}, u32[]{:S(2)}, u32[]{:S(2)}) collective-permute-start(bf16[512,384]{1,0:T(8,128)(2,1)} %get-tuple-element.18), channel_id=1, source_target_pairs={{0,1},{1,0},{2,3},{3,2},{4,5},{5,4},{6,7},{7,6},{8,9},{9,8},{10,11... | collective-permute-start | bytes 1179656 | tf_op jit(solution)/shard_map/gather/ppermute | solution.py:177
  103.4 12.7 %copy-start.2 = (bf16[512,384]{1,0:T(8,128)(2,1)S(1)}, bf16[512,384]{1,0:T(8,128)(2,1)}, u32[]{:S(2)}) copy-start(bf16[512,384]{1,0:T(8,128)(2,1)} %copy-done.1) | copy-start | bytes 1179652
  106.3 15.7 %collective-permute-start.11 = (bf16[512,384]{1,0:T(8,128)(2,1)S(1)}, bf16[512,384]{1,0:T(8,128)(2,1)S(1)}, u32[]{:S(2)}, u32[]{:S(2)}) collective-permute-start(bf16[512,384]{1,0:T(8,128)(2,1)S(1)} %add.69.refs_7_), channel_id=1, source_target_pairs={{4,6},{5,7},{2,0},{3,1},{12,14},{13,15},{10,8},{11,9},{20,22},{21,... | collective-permute-start | bytes 1179656 | tf_op jit(solution)/shard_map/gather/ppermute | solution.py:172
  114.7 15.5 %collective-permute-start.10 = (bf16[512,384]{1,0:T(8,128)(2,1)S(1)}, bf16[512,384]{1,0:T(8,128)(2,1)S(1)}, u32[]{:S(2)}, u32[]{:S(2)}) collective-permute-start(bf16[512,384]{1,0:T(8,128)(2,1)S(1)} %add.67.refs_3_), channel_id=1, source_target_pairs={{4,6},{5,7},{2,0},{3,1},{12,14},{13,15},{10,8},{11,9},{20,22},{21,... | collective-permute-start | bytes 1179656 | tf_op jit(solution)/shard_map/gather/ppermute | solution.py:172
  132.7 62.0 %copy-start.3 = (bf16[512,512]{1,0:T(8,128)(2,1)S(1)}, bf16[512,512]{1,0:T(8,128)(2,1)}, u32[]{:S(2)}) copy-start(bf16[512,512]{1,0:T(8,128)(2,1)} %param.6) | copy-start | bytes 1572868
  191.8 3.1 %copy-start.5 = (s32[1,512]{1,0:T(1,128)S(1)}, s32[1,512]{1,0:T(1,128)}, u32[]{:S(2)}) copy-start(s32[1,512]{1,0:T(1,128)} %get-tuple-element.4) | copy-start | bytes 6148
  191.8 4.4 %copy-start.6 = (f32[512]{0:T(512)S(1)}, f32[512]{0:T(512)}, u32[]{:S(2)}) copy-start(f32[512]{0:T(512)} %param.7) | copy-start | bytes 6148
  191.9 4.3 %collective-permute-start.12 = (bf16[512,512]{1,0:T(8,128)(2,1)S(1)}, bf16[512,512]{1,0:T(8,128)(2,1)S(1)}, u32[]{:S(2)}, u32[]{:S(2)}) collective-permute-start(bf16[512,512]{1,0:T(8,128)(2,1)S(1)} %get-tuple-element.17), channel_id=1, source_target_pairs={{0,1},{1,0},{2,3},{3,2},{4,5},{5,4},{6,7},{7,6},{8,9},{9,8},{10,11... | collective-permute-start | bytes 1572872 | tf_op jit(solution)/shard_map/finish/ppermute | solution.py:177
  197.8 9.2 %all-to-all-start.2 = ((f32[8,1,512]{2,1,0:T(1,128)}), f32[8,1,512]{2,1,0:T(1,128)S(1)}, u32[]{:S(2)}, u32[]{:S(2)}) async-start(f32[8,1,512]{2,1,0:T(1,128)} %broadcast_in_dim.6), calls=%async_computation.2 | async-start | bytes 32768 | tf_op jit(solution)/shard_map/finish/all_to_all | solution.py:220

commit v5 on v4

--- a/solution.py
+++ b/solution.py
@@ -13,43 +13,49 @@
 
 
 def line_shards(chip, chips):
-    edge = (chip == 0) | (chip == chips - 1)
-    shards = [chip, chip - 1, chip + 1, lax.rem(chip + 2, chips), chips - 1 - chip]
-    valid = [chip >= 0, chip > 0, chip < chips - 1, chip >= 0, edge]
-    return [jnp.clip(s, 0, chips - 1) for s in shards], valid
+    steps = [0, -1, 1, -2, 2]
+    shards = [chip + n for n in steps]
+    return [jnp.clip(s, 0, chips - 1) for s in shards], [(s >= 0) & (s < chips) for s in shards]
+
+
+def at_end(chip, chips):
+    return (chip == 0) | (chip == chips - 1)
 
 
 def near_kernel(place_ref, *refs):
-    kinds = KINDS - 1
-    count = HALVES * kinds
+    count = HALVES * KINDS
     pieces, sources = refs[:count], refs[count : count + CORES]
     out, tokens, weights, token_sems, weight_sems = refs[count + CORES :]
     width = pieces[0].shape[1]
     hidden = weights.shape[1]
-    core = place_ref[1]
-    shards, valid = line_shards(place_ref[0], tokens.shape[1] // (width * HALVES))
+    chip, core = place_ref[0], place_ref[1]
+    chips = tokens.shape[1] // (width * HALVES)
+    shards, valid = line_shards(chip, chips)
+
+    def part(shard, h):
+        block = shard * HALVES + (core if h == 0 else 1 - core)
+        return pl.ds(pl.multiple_of(block * width, 128), width)
 
     def columns(h, k):
-        block = shards[k] * HALVES + (core if h == 0 else 1 - core)
-        return pl.ds(pl.multiple_of(block * width, 128), width)
+        return part(shards[k], h)
 
     def token_copy(n):
-        return pltpu.make_async_copy(pieces[n], tokens.at[:, columns(*divmod(n, kinds))], token_sems.at[n])
+        return pltpu.make_async_copy(pieces[n], tokens.at[:, columns(*divmod(n, KINDS))], token_sems.at[n])
 
     def weight_copy(n):
         return pltpu.make_async_copy(sources[n], weights.at[n], weight_sems.at[n])
 
-    @pl.when(valid[-1])
+    @pl.when(at_end(chip, chips))
     def _():
         for h in range(HALVES):
-            tokens[:, columns(h, KINDS - 1)] = jnp.zeros((tokens.shape[0], width), tokens.dtype)
+            tokens[:, part(chips - 1 - chip, h)] = jnp.zeros((tokens.shape[0], width), tokens.dtype)
 
     weight_copy(0).start()
     for n in range(count):
-        pl.when(valid[n % kinds])(token_copy(n).start)
+        pl.when(valid[n % KINDS])(token_copy(n).start)
     weight_copy(1).start()
     for n in range(count):
-        pl.when(valid[n % kinds])(token_copy(n).wait)
+        pl.when(valid[n % KINDS])(token_copy(n).wait)
     for n in range(CORES):
         weight_copy(n).wait()
         out[:, n * hidden : (n + 1) * hidden] = lax.dot_general(
@@ -58,20 +64,21 @@
 
 
 def last_kernel(chips, place_ref, total_ref, *refs):
-    pieces, sources, out = refs[:HALVES], refs[HALVES : HALVES + CORES], refs[HALVES + CORES]
-    weights, sems = refs[HALVES + CORES + 1 :]
+    pieces, sources = refs[: 2 * HALVES], refs[2 * HALVES : 2 * HALVES + CORES]
+    out, weights, sems = refs[2 * HALVES + CORES :]
     width = pieces[0].shape[1]
     hidden = weights.shape[2]
-    core = place_ref[1]
-    shards, valid = line_shards(place_ref[0], chips)
+    chip, core = place_ref[0], place_ref[1]
+    end = at_end(chip, chips)
 
     def weight_copy(h, n):
-        block = shards[-1] * HALVES + (core if h == 0 else 1 - core)
+        block = (chips - 1 - chip) * HALVES + (core if h == 0 else 1 - core)
         part = sources[n].at[:, pl.ds(pl.multiple_of(block * width, 128), width)]
         return pltpu.make_async_copy(part, weights.at[h, n], sems.at[h, n])
 
-    @pl.when(valid[-1])
+    @pl.when(end)
     def _():
+        last = [jnp.where(chip == 0, pieces[2 * h + 1][...], pieces[2 * h][...]) for h in range(HALVES)]
         for n in range(CORES):
             for h in range(HALVES):
                 weight_copy(h, n).start()
@@ -81,11 +88,11 @@
             for h in range(HALVES):
                 weight_copy(h, n).wait()
                 more = more + lax.dot_general(
-                    pieces[h][...], weights[h, n], (((1,), (1,)), ((), ())), preferred_element_type=jnp.float32
+                    last[h], weights[h, n], (((1,), (1,)), ((), ())), preferred_element_type=jnp.float32
                 )
             out[:, here] = more.astype(out.dtype)
 
-    @pl.when(jnp.logical_not(valid[-1]))
+    @pl.when(jnp.logical_not(end))
     def _():
         out[...] = total_ref[...].astype(out.dtype)
 
@@ -106,7 +113,7 @@
         scratch_shapes=[
             pltpu.VMEM((rows, depth), jnp.bfloat16),
             pltpu.VMEM((CORES, hidden, depth), jnp.bfloat16),
-            pltpu.SemaphoreType.DMA((HALVES * (KINDS - 1),)),
+            pltpu.SemaphoreType.DMA((HALVES * KINDS,)),
             pltpu.SemaphoreType.DMA((CORES,)),
         ],
         compiler_params=pltpu.CompilerParams(vmem_limit_bytes=32 * 1024 * 1024),
@@ -122,7 +129,7 @@
     return pl.pallas_call(
         functools.partial(last_kernel, chips),
         out_shape=jax.ShapeDtypeStruct(total.shape, jnp.bfloat16),
-        in_specs=[SMEM] + [VMEM] * (1 + HALVES) + [HBM] * CORES,
+        in_specs=[SMEM] + [VMEM] * (1 + 2 * HALVES) + [HBM] * CORES,
         out_specs=VMEM,
         scratch_shapes=[
             pltpu.VMEM((HALVES, CORES, hidden, width), jnp.bfloat16),
@@ -151,6 +158,53 @@
     send_ref[...] = jnp.dot(place, rows_ref[...], preferred_element_type=jnp.float32).astype(send_ref.dtype)
 
 
+def finish_kernel(shards, local_ref, gate_ref, back_ref, across_ref, hidden_ref, grad_ref, parts_ref):
+    tokens, hidden = hidden_ref.shape
+    slots = back_ref.shape[0]
+
+    def column(row):
+        return jnp.broadcast_to(row, (128, tokens)).T
+
+    def wide(array, width):
+        return jnp.concatenate([array] * (width // 128), axis=1)
+
+    local = wide(column(local_ref[...].astype(jnp.float32)).astype(jnp.int32), slots)
+    slot = lax.broadcasted_iota(jnp.int32, (tokens, slots), 1)
+    mine = (local == slot).astype(jnp.bfloat16)
+    other = (local == slot + slots).astype(jnp.bfloat16)
+    returned = jnp.dot(mine, back_ref[...], preferred_element_type=jnp.float32)
+    returned = returned + jnp.dot(other, across_ref[...], preferred_element_type=jnp.float32)
+    grad_ref[...] = (wide(column(gate_ref[...]), hidden) * returned).astype(grad_ref.dtype)
+    product = hidden_ref[...].astype(jnp.float32) * returned
+    folded = sum(product[:, n * 128 : (n + 1) * 128] for n in range(hidden // 128))
+    part = jnp.sum(folded.T, axis=0, keepdims=True)
+    parts_ref[...] = jnp.broadcast_to(part, (shards, tokens))
+
+
+def finish(local, gate_prob, back, across, hidden_in, shards):
+    tokens, hidden = hidden_in.shape
+    slots = back.shape[0]
+    steps = 2
+    step = tokens // steps
+    row = pl.BlockSpec((1, step), lambda i: (0, i))
+    rows = pl.BlockSpec((step, hidden), lambda i: (i, 0))
+    whole = pl.BlockSpec((slots, hidden), lambda i: (0, 0))
+    return pl.pallas_call(
+        functools.partial(finish_kernel, shards),
+        grid=(steps,),
+        out_shape=[
+            jax.ShapeDtypeStruct((tokens, hidden), jnp.bfloat16),
+            jax.ShapeDtypeStruct((shards, tokens), jnp.float32),
+        ],
+        in_specs=[row, row, whole, whole, rows],
+        out_specs=[rows, pl.BlockSpec((shards, step), lambda i: (0, i))],
+        compiler_params=pltpu.CompilerParams(vmem_limit_bytes=24 * 1024 * 1024),
+        cost_estimate=pl.CostEstimate(
+            flops=4 * tokens * hidden * slots, bytes_accessed=8 * tokens * hidden, transcendentals=0
+        ),
+    )(local, gate_prob.reshape(1, tokens), back, across, hidden_in)
+
+
 def body(grad_out, hidden_in, gate_prob, expert_ids, w_down):
     tokens, width = grad_out.shape
     groups = lax.axis_size("expert")
@@ -194,29 +248,26 @@
         def gather(x, flip):
             right = line(x, [(0, 1), (1, 2), (2, 3)], flip)
             left = line(x, [(1, 0), (2, 1), (3, 2)], flip)
-            second = line(right, [(1, 2), (2, 3)]) + line(left, [(2, 1), (1, 0)])
-            return [swap(x) if flip else x, right, left, second, line(second, [(2, 3), (1, 0)])]
-
-        halves = [gather(part(core), 0), gather(part(1 - core), 1)]
+            right2 = line(right, [(1, 2), (2, 3)])
+            left2 = line(left, [(2, 1), (1, 0)])
+            last = [line(right2, [(2, 3)]), line(left2, [(1, 0)])]
+            return [swap(x) if flip else x, right, left, right2, left2], last
+
+        (near, last), (crossed, crossed_last) = gather(part(core), 0), gather(part(1 - core), 1)
 
     with jax.named_scope("products"):
         where = jnp.stack([chip, core])
-        total = multiply_near(where, halves[0][:-1] + halves[1][:-1], weights)
-        filled = multiply_last(where, chips, total, [halves[0][-1], halves[1][-1]], weights)
+        total = multiply_near(where, near + crossed, weights)
+        filled = multiply_last(where, chips, total, last + crossed_last, weights)
 
     with jax.named_scope("return"):
         back = lax.all_to_all(filled, "expert", split_axis=0, concat_axis=0, tiled=True)
 
     with jax.named_scope("finish"):
-        target = target.reshape(tokens)
-        away = jnp.where(target % capacity // share == core, 0, 1)
-        local = away * (slots // CORES) + target // capacity * share + target % share
-        pick = (local[:, None] == jnp.arange(slots, dtype=jnp.int32)[None, :]).astype(bf16)
-        back = jnp.concatenate([back[:, :hidden], swap(back[:, hidden:])], axis=0)
-        returned = jnp.dot(pick, back, preferred_element_type=f32)
-        grad_hidden = (gate_prob[:, None] * returned).astype(bf16)
-        gate_part = jnp.sum(hidden_in.astype(f32) * returned, axis=1)
-        parts = jnp.broadcast_to(gate_part[None, :], (shards, tokens))
+        share_of = target % capacity // share
+        local = jnp.where(share_of == core, 0, slots // CORES) + target // capacity * share + target % share
+        across = swap(back[:, hidden:])
+        grad_hidden, parts = finish(local, gate_prob, back, across, hidden_in, shards)
         gate = jnp.sum(lax.all_to_all(parts, "tensor", split_axis=0, concat_axis=0, tiled=True), axis=0)
     return grad_hidden, gate
 

time: 208 us -> 207 us (level)
  blocking collectives: 59.1 us -> 68.2 us
  local copies, waits for them, and re-layouts: 5.37 us -> 2.02 us
  starting transfers between devices: 67.5 us -> 64.2 us
  other arithmetic: 3.13 us -> 0.72 us
  Pallas kernels: 11.2 us -> 13.6 us
  waiting for transfers between devices: 59.4 us -> 57.2 us
    all_to_all x0 -> x1, blocking collectives: none -> 9.15 us  [body(): lax.all_to_all(parts, 'tensor', split_axis=0, concat_axis=0, tiled=True)]
    all_to_all x1 -> x0, starting transfers between devices: 4.3 us -> none  [body(): lax.all_to_all(parts, 'tensor', split_axis=0, concat_axis=0, tiled=True)]
    ppermute x10 -> x12, starting transfers between devices: 30.6 us -> 34.6 us  [line(): lax.ppermute(array, 'tensor', [(a * CORES + c, b * CORES + (c ^ flip)) fo...]
    all_to_all x1 -> x0, waiting for transfers between devices: 3.92 us -> none  [body(): lax.all_to_all(parts, 'tensor', split_axis=0, concat_axis=0, tiled=True)]
    ppermute x3, starting transfers between devices: 10.6 us -> 7.55 us  [swap(): return lax.ppermute(array, 'tensor', core_pairs)]
    unnamed x16 -> x8, local copies, waits for them, and re-layouts: 2.74 us -> 0.03 us
    add x3 -> x1, other arithmetic: 2.44 us -> 0.04 us  [body(): jnp.where(share_of == core, 0, slots // CORES) + target // capacity * share]
    ppermute x10 -> x12, waiting for transfers between devices: 24.8 us -> 26.1 us  [line(): lax.ppermute(array, 'tensor', [(a * CORES + c, b * CORES + (c ^ flip)) fo...]
  transfers between devices with their start and end apart: 15 -> 16, of which waited for: 10 -> 8; matrix products, arithmetic and copies ran while one was open for 3% -> 1% of each run, Pallas kernels for 3% -> 3%
where the time goes in v5:
time: 207 us
  blocking collectives  68.2 us (33%)
  starting transfers between devices  64.2 us (31%)
  waiting for transfers between devices  57.2 us (28%)
  Pallas kernels  13.6 us (7%)
    all_to_all x1, blocking collectives, body(): lax.all_to_all(filled, 'expert', split_axis=0, concat_axis=0, tiled=True)  59.1 us
    ppermute x12, starting transfers between devices, line(): lax.ppermute(array, 'tensor', [(a * CORES + c, b * CORES + (c ^ flip)) fo...  34.6 us
    all_to_all x1, waiting for transfers between devices, body(): lax.all_to_all(send, 'expert', split_axis=0, concat_axis=0, tiled=True)  29.7 us
    ppermute x12, waiting for transfers between devices, line(): lax.ppermute(array, 'tensor', [(a * CORES + c, b * CORES + (c ^ flip)) fo...  26.1 us
    all_to_all x1, starting transfers between devices, body(): lax.all_to_all(send, 'expert', split_axis=0, concat_axis=0, tiled=True)  22 us
    all_to_all x1, blocking collectives, body(): lax.all_to_all(parts, 'tensor', split_axis=0, concat_axis=0, tiled=True)  9.15 us
    ppermute x3, starting transfers between devices, swap(): return lax.ppermute(array, 'tensor', core_pairs)  7.55 us
    pallas_call x1, Pallas kernels, multiply_near(): pl.pallas_call(near_kernel, out_shape=jax.ShapeDtypeStruct((rows, CORES *...  6.14 us
  transfers between devices with their start and end apart: 16, of which 8 were waited for; matrix products, arithmetic and copies ran while one was open for 1% of the time, Pallas kernels for 3%

profile of v5, /device:TPU:1, one launch (start us, length us, event | category | flops | bytes accessed | tf_op | source)
XLA Modules:
  0.0 206.8 jit_solution(8242953893899038538)
XLA Ops:
  0.6 0.0 copy-start
  0.6 3.0 %route.1 = (bf16[1024,384]{1,0:T(8,128)(2,1)}, s32[1,512]{1,0:T(1,128)}) custom-call(s32[1,512]{1,0:T(1,128)} %bitcast.23, bf16[512,384]{1,0:T(8,128)(2,1)} %rows_ref.1), custom_call_target="tpu_custom_call" | custom-call | tf_op jit(solution)/shard_map/route/pallas_call | solution.py:234
  3.6 22.0 %all-to-all-start = ((bf16[64,16,384]{2,1,0:T(8,128)(2,1)}), bf16[64,16,384]{2,1,0:T(8,128)(2,1)}, u32[]{:S(2)}, u32[]{:S(2)}) async-start(bf16[64,16,384]{2,1,0:T(8,128)(2,1)} %bitcast.22), calls=%async_computation | async-start | bytes 1572864 | tf_op jit(solution)/shard_map/dispatch/all_to_all | solution.py:240
  25.6 2.9 %collective-permute-start.9 = (bf16[512,3072]{1,0:T(8,128)(2,1)}, bf16[512,3072]{1,0:T(8,128)(2,1)}, u32[]{:S(2)}, u32[]{:S(2)}) collective-permute-start(bf16[512,3072]{1,0:T(8,128)(2,1)} %bitcast.14), channel_id=1, source_target_pairs={{0,1},{1,0},{2,3},{3,2},{4,5},{5,4},{6,7},{7,6},{8,9},{9,8},{10,11... | collective-permute-start | bytes 9437192 | tf_op jit(solution)/shard_map/gather/ppermute | solution.py:231
  28.5 29.7 %all-to-all-done = bf16[64,16,384]{2,1,0:T(8,128)(2,1)} async-done(((bf16[64,16,384]{2,1,0:T(8,128)(2,1)}), bf16[64,16,384]{2,1,0:T(8,128)(2,1)}, u32[]{:S(2)}, u32[]{:S(2)}) %all-to-all-start) | async-done | bytes 786464 | tf_op jit(solution)/shard_map/dispatch/all_to_all | solution.py:240
  58.2 1.9 dynamic-slice_bitcast_fusion
  60.1 15.2 %collective-permute-start = (bf16[512,384]{1,0:T(8,128)(2,1)S(1)}, bf16[512,384]{1,0:T(8,128)(2,1)}, u32[]{:S(2)}, u32[]{:S(2)}) collective-permute-start(bf16[512,384]{1,0:T(8,128)(2,1)S(1)} %get-tuple-element.11.refs_0_), channel_id=1, source_target_pairs={{0,2},{1,3},{2,4},{3,5},{4,6},{5,7},{8,10},{9,11},{10,12},{11,13},... | collective-permute-start | bytes 1179656 | tf_op jit(solution)/shard_map/gather/ppermute | solution.py:226
  75.3 1.3 collective-permute-start.1
  76.6 7.6 %collective-permute-start.5 = (bf16[512,384]{1,0:T(8,128)(2,1)}, bf16[512,384]{1,0:T(8,128)(2,1)}, u32[]{:S(2)}, u32[]{:S(2)}) collective-permute-start(bf16[512,384]{1,0:T(8,128)(2,1)} %get-tuple-element.10), channel_id=1, source_target_pairs={{0,3},{1,2},{2,5},{3,4},{4,7},{5,6},{8,11},{9,10},{10,13},{11,12},... | collective-permute-start | bytes 1179656 | tf_op jit(solution)/shard_map/gather/ppermute | solution.py:226
  84.2 1.3 collective-permute-start.6
  85.5 0.0 collective-permute-done.refs_1_
  85.5 1.4 collective-permute-start.2
  86.9 0.0 collective-permute-done.1.refs_2_
  86.9 1.3 collective-permute-start.3
  88.2 3.8 %collective-permute-done.5.refs_6_ = bf16[512,384]{1,0:T(8,128)(2,1)} collective-permute-done((bf16[512,384]{1,0:T(8,128)(2,1)}, bf16[512,384]{1,0:T(8,128)(2,1)}, u32[]{:S(2)}, u32[]{:S(2)}) %collective-permute-start.5) | collective-permute-done | bytes 393248 | tf_op jit(solution)/shard_map/gather/ppermute | solution.py:226
  92.0 1.4 collective-permute-start.7
  93.4 4.5 %collective-permute-done.6.refs_7_ = bf16[512,384]{1,0:T(8,128)(2,1)} collective-permute-done((bf16[512,384]{1,0:T(8,128)(2,1)}, bf16[512,384]{1,0:T(8,128)(2,1)}, u32[]{:S(2)}, u32[]{:S(2)}) %collective-permute-start.6) | collective-permute-done | bytes 393248 | tf_op jit(solution)/shard_map/gather/ppermute | solution.py:226
  97.9 1.3 collective-permute-start.8
  99.2 0.0 collective-permute-done.9.refs_11_.refs_5_
  99.2 1.9 collective-permute-start.4
  101.2 0.0 collective-permute-done.2.refs_3_
  101.2 0.7 collective-permute-start.10
  101.9 2.1 %collective-permute-done.3.refs_4_ = bf16[512,384]{1,0:T(8,128)(2,1)} collective-permute-done((bf16[512,384]{1,0:T(8,128)(2,1)}, bf16[512,384]{1,0:T(8,128)(2,1)}, u32[]{:S(2)}, u32[]{:S(2)}) %collective-permute-start.3) | collective-permute-done | bytes 393248 | tf_op jit(solution)/shard_map/gather/ppermute | solution.py:226
  103.9 1.3 collective-permute-start.11
  105.2 0.0 collective-permute-done.7.refs_8_
  105.2 0.7 collective-permute-start.12
  105.9 6.4 %collective-permute-done.8.refs_9_ = bf16[512,384]{1,0:T(8,128)(2,1)} collective-permute-done((bf16[512,384]{1,0:T(8,128)(2,1)}, bf16[512,384]{1,0:T(8,128)(2,1)}, u32[]{:S(2)}, u32[]{:S(2)}) %collective-permute-start.8) | collective-permute-done | bytes 393248 | tf_op jit(solution)/shard_map/gather/ppermute | solution.py:226
  112.4 1.3 collective-permute-start.13
  113.7 0.1 pad_add_fusion.place_ref
  113.7 0.0 collective-permute-done.4.refs_5_
  113.7 0.0 copy-done
  113.7 6.1 %products.2.total_ref = f32[512,1024]{1,0:T(8,128)S(1)} custom-call(s32[2]{0:T(128)S(1)} %pad_add_fusion.place_ref, bf16[512,384]{1,0:T(8,128)(2,1)S(1)} %get-tuple-element.11.refs_0_, bf16[512,384]{1,0:T(8,128)(2,1)} %collective-permute-done.refs_1_, bf16[512,384]{1,0:T(8,128)(2,1)} %collective-permute-done.1.refs_2_, ...), custom_call_target="tpu_custom_call" | custom-call | flops 3221225472 | bytes 9437184 | tf_op jit(solution)/shard_map/products/pallas_call | solution.py:108
  119.9 0.0 collective-permute-done.10.refs_0_
  119.9 0.8 collective-permute-done.11.refs_1_
  120.7 0.0 collective-permute-done.12.refs_2_
  120.7 8.4 %collective-permute-done.13.refs_3_ = bf16[512,384]{1,0:T(8,128)(2,1)S(1)} collective-permute-done((bf16[512,384]{1,0:T(8,128)(2,1)}, bf16[512,384]{1,0:T(8,128)(2,1)S(1)}, u32[]{:S(2)}, u32[]{:S(2)}) %collective-permute-start.13) | collective-permute-done | bytes 393248 | tf_op jit(solution)/shard_map/gather/ppermute | solution.py:226
  129.1 2.6 %products.3 = bf16[512,1024]{1,0:T(8,128)(2,1)S(1)} custom-call(s32[2]{0:T(128)S(1)} %pad_add_fusion.place_ref, f32[512,1024]{1,0:T(8,128)S(1)} %products.2.total_ref, bf16[512,384]{1,0:T(8,128)(2,1)S(1)} %collective-permute-done.10.refs_0_, bf16[512,384]{1,0:T(8,128)(2,1)S(1)} %collective-permute-done.11.refs_1_, ...), custom_call_target="tpu_custom_call" | custom-call | flops 805306368 | bytes 4194304 | tf_op jit(solution)/shard_map/products/pallas_call | solution.py:129
  131.8 0.0 copy-start.3
  131.8 0.0 copy-start.1
  131.8 0.0 copy-start.2
  131.8 59.1 %all_to_all.29 = bf16[64,8,1024]{2,1,0:T(8,128)(2,1)S(1)} all-to-all(bf16[64,8,1024]{2,1,0:T(8,128)(2,1)S(1)} %bitcast.19), channel_id=1, replica_groups=mesh['expert'=64,'tensor'=8] {'expert'}, dimensions={0} | all-to-all | bytes 2097152 | tf_op jit(solution)/shard_map/return/all_to_all | solution.py:264
  190.9 2.8 %collective-permute-start.14 = (bf16[512,512]{1,0:T(8,128)(2,1)S(1)}, bf16[512,512]{1,0:T(8,128)(2,1)S(1)}, u32[]{:S(2)}, u32[]{:S(2)}) collective-permute-start(bf16[512,512]{1,0:T(8,128)(2,1)S(1)} %slice.4), channel_id=1, source_target_pairs={{0,1},{1,0},{2,3},{3,2},{4,5},{5,4},{6,7},{7,6},{8,9},{9,8},{10,11... | collective-permute-start | bytes 1572872 | tf_op jit(solution)/shard_map/finish/ppermute | solution.py:231
  193.7 0.0 copy-done.3
  193.7 1.5 collective-permute-done.14.across_ref
  195.2 0.0 copy-done.1
  195.2 1.8 finish.1
  197.1 9.1 %all_to_all.30 = f32[8,1,512]{2,1,0:T(1,128)S(1)} all-to-all(f32[8,1,512]{2,1,0:T(1,128)S(1)} %copy.7), channel_id=1, replica_groups=mesh['expert'=64,'tensor'=8] {'tensor'}, dimensions={0} | all-to-all | bytes 32768 | tf_op jit(solution)/shard_map/finish/all_to_all | solution.py:271
  206.2 0.6 reduce_sum.9
  (4 shorter events, 0.1 us)
Async XLA Ops:
  0.6 113.1 %copy-start = (bf16[1,512,3072]{2,1,0:T(8,128)(2,1)S(1)}, bf16[1,512,3072]{2,1,0:T(8,128)(2,1)}, u32[]{:S(2)}) copy-start(bf16[1,512,3072]{2,1,0:T(8,128)(2,1)} %param.9) | copy-start | bytes 9437188
  3.6 54.6 %all-to-all-start = ((bf16[64,16,384]{2,1,0:T(8,128)(2,1)}), bf16[64,16,384]{2,1,0:T(8,128)(2,1)}, u32[]{:S(2)}, u32[]{:S(2)}) async-start(bf16[64,16,384]{2,1,0:T(8,128)(2,1)} %bitcast.22), calls=%async_computation | async-start | bytes 1572864 | tf_op jit(solution)/shard_map/dispatch/all_to_all | solution.py:240
  25.6 73.6 %collective-permute-start.9 = (bf16[512,3072]{1,0:T(8,128)(2,1)}, bf16[512,3072]{1,0:T(8,128)(2,1)}, u32[]{:S(2)}, u32[]{:S(2)}) collective-permute-start(bf16[512,3072]{1,0:T(8,128)(2,1)} %bitcast.14), channel_id=1, source_target_pairs={{0,1},{1,0},{2,3},{3,2},{4,5},{5,4},{6,7},{7,6},{8,9},{9,8},{10,11... | collective-permute-start | bytes 9437192 | tf_op jit(solution)/shard_map/gather/ppermute | solution.py:231
  60.1 25.3 %collective-permute-start = (bf16[512,384]{1,0:T(8,128)(2,1)S(1)}, bf16[512,384]{1,0:T(8,128)(2,1)}, u32[]{:S(2)}, u32[]{:S(2)}) collective-permute-start(bf16[512,384]{1,0:T(8,128)(2,1)S(1)} %get-tuple-element.11.refs_0_), channel_id=1, source_target_pairs={{0,2},{1,3},{2,4},{3,5},{4,6},{5,7},{8,10},{9,11},{10,12},{11,13},... | collective-permute-start | bytes 1179656 | tf_op jit(solution)/shard_map/gather/ppermute | solution.py:226
  75.3 11.6 %collective-permute-start.1 = (bf16[512,384]{1,0:T(8,128)(2,1)S(1)}, bf16[512,384]{1,0:T(8,128)(2,1)}, u32[]{:S(2)}, u32[]{:S(2)}) collective-permute-start(bf16[512,384]{1,0:T(8,128)(2,1)S(1)} %get-tuple-element.11.refs_0_), channel_id=1, source_target_pairs={{2,0},{3,1},{4,2},{5,3},{6,4},{7,5},{10,8},{11,9},{12,10},{13,11},... | collective-permute-start | bytes 1179656 | tf_op jit(solution)/shard_map/gather/ppermute | solution.py:226
  76.6 15.4 %collective-permute-start.5 = (bf16[512,384]{1,0:T(8,128)(2,1)}, bf16[512,384]{1,0:T(8,128)(2,1)}, u32[]{:S(2)}, u32[]{:S(2)}) collective-permute-start(bf16[512,384]{1,0:T(8,128)(2,1)} %get-tuple-element.10), channel_id=1, source_target_pairs={{0,3},{1,2},{2,5},{3,4},{4,7},{5,6},{8,11},{9,10},{10,13},{11,12},... | collective-permute-start | bytes 1179656 | tf_op jit(solution)/shard_map/gather/ppermute | solution.py:226
  84.2 13.7 %collective-permute-start.6 = (bf16[512,384]{1,0:T(8,128)(2,1)}, bf16[512,384]{1,0:T(8,128)(2,1)}, u32[]{:S(2)}, u32[]{:S(2)}) collective-permute-start(bf16[512,384]{1,0:T(8,128)(2,1)} %get-tuple-element.10), channel_id=1, source_target_pairs={{2,1},{3,0},{4,3},{5,2},{6,5},{7,4},{10,9},{11,8},{12,11},{13,10},... | collective-permute-start | bytes 1179656 | tf_op jit(solution)/shard_map/gather/ppermute | solution.py:226
  85.5 15.7 %collective-permute-start.2 = (bf16[512,384]{1,0:T(8,128)(2,1)}, bf16[512,384]{1,0:T(8,128)(2,1)}, u32[]{:S(2)}, u32[]{:S(2)}) collective-permute-start(bf16[512,384]{1,0:T(8,128)(2,1)} %collective-permute-done.refs_1_), channel_id=1, source_target_pairs={{2,4},{3,5},{4,6},{5,7},{10,12},{11,13},{12,14},{13,15},{18,20},{1... | collective-permute-start | bytes 1179656 | tf_op jit(solution)/shard_map/gather/ppermute | solution.py:226
  86.9 17.0 %collective-permute-start.3 = (bf16[512,384]{1,0:T(8,128)(2,1)}, bf16[512,384]{1,0:T(8,128)(2,1)}, u32[]{:S(2)}, u32[]{:S(2)}) collective-permute-start(bf16[512,384]{1,0:T(8,128)(2,1)} %collective-permute-done.1.refs_2_), channel_id=1, source_target_pairs={{4,2},{5,3},{2,0},{3,1},{12,10},{13,11},{10,8},{11,9},{20,18},{21,... | collective-permute-start | bytes 1179656 | tf_op jit(solution)/shard_map/gather/ppermute | solution.py:226
  92.0 13.2 %collective-permute-start.7 = (bf16[512,384]{1,0:T(8,128)(2,1)}, bf16[512,384]{1,0:T(8,128)(2,1)}, u32[]{:S(2)}, u32[]{:S(2)}) collective-permute-start(bf16[512,384]{1,0:T(8,128)(2,1)} %collective-permute-done.5.refs_6_), channel_id=1, source_target_pairs={{2,4},{3,5},{4,6},{5,7},{10,12},{11,13},{12,14},{13,15},{18,20},{1... | collective-permute-start | bytes 1179656 | tf_op jit(solution)/shard_map/gather/ppermute | solution.py:226
  97.9 14.5 %collective-permute-start.8 = (bf16[512,384]{1,0:T(8,128)(2,1)}, bf16[512,384]{1,0:T(8,128)(2,1)}, u32[]{:S(2)}, u32[]{:S(2)}) collective-permute-start(bf16[512,384]{1,0:T(8,128)(2,1)} %collective-permute-done.6.refs_7_), channel_id=1, source_target_pairs={{4,2},{5,3},{2,0},{3,1},{12,10},{13,11},{10,8},{11,9},{20,18},{21,... | collective-permute-start | bytes 1179656 | tf_op jit(solution)/shard_map/gather/ppermute | solution.py:226
  99.2 14.5 %collective-permute-start.4 = (bf16[512,384]{1,0:T(8,128)(2,1)}, bf16[512,384]{1,0:T(8,128)(2,1)}, u32[]{:S(2)}, u32[]{:S(2)}) collective-permute-start(bf16[512,384]{1,0:T(8,128)(2,1)} %get-tuple-element.10), channel_id=1, source_target_pairs={{0,1},{1,0},{2,3},{3,2},{4,5},{5,4},{6,7},{7,6},{8,9},{9,8},{10,11... | collective-permute-start | bytes 1179656 | tf_op jit(solution)/shard_map/gather/ppermute | solution.py:231
  101.2 18.7 %collective-permute-start.10 = (bf16[512,384]{1,0:T(8,128)(2,1)}, bf16[512,384]{1,0:T(8,128)(2,1)S(1)}, u32[]{:S(2)}, u32[]{:S(2)}) collective-permute-start(bf16[512,384]{1,0:T(8,128)(2,1)} %collective-permute-done.2.refs_3_), channel_id=1, source_target_pairs={{4,6},{5,7},{12,14},{13,15},{20,22},{21,23},{28,30},{29,31},{36,38... | collective-permute-start | bytes 1179656 | tf_op jit(solution)/shard_map/gather/ppermute | solution.py:226
  103.9 16.7 %collective-permute-start.11 = (bf16[512,384]{1,0:T(8,128)(2,1)}, bf16[512,384]{1,0:T(8,128)(2,1)S(1)}, u32[]{:S(2)}, u32[]{:S(2)}) collective-permute-start(bf16[512,384]{1,0:T(8,128)(2,1)} %collective-permute-done.3.refs_4_), channel_id=1, source_target_pairs={{2,0},{3,1},{10,8},{11,9},{18,16},{19,17},{26,24},{27,25},{34,32},... | collective-permute-start | bytes 1179656 | tf_op jit(solution)/shard_map/gather/ppermute | solution.py:226
  105.2 15.5 %collective-permute-start.12 = (bf16[512,384]{1,0:T(8,128)(2,1)}, bf16[512,384]{1,0:T(8,128)(2,1)S(1)}, u32[]{:S(2)}, u32[]{:S(2)}) collective-permute-start(bf16[512,384]{1,0:T(8,128)(2,1)} %collective-permute-done.7.refs_8_), channel_id=1, source_target_pairs={{4,6},{5,7},{12,14},{13,15},{20,22},{21,23},{28,30},{29,31},{36,38... | collective-permute-start | bytes 1179656 | tf_op jit(solution)/shard_map/gather/ppermute | solution.py:226
  112.4 16.7 %collective-permute-start.13 = (bf16[512,384]{1,0:T(8,128)(2,1)}, bf16[512,384]{1,0:T(8,128)(2,1)S(1)}, u32[]{:S(2)}, u32[]{:S(2)}) collective-permute-start(bf16[512,384]{1,0:T(8,128)(2,1)} %collective-permute-done.8.refs_9_), channel_id=1, source_target_pairs={{2,0},{3,1},{10,8},{11,9},{18,16},{19,17},{26,24},{27,25},{34,32},... | collective-permute-start | bytes 1179656 | tf_op jit(solution)/shard_map/gather/ppermute | solution.py:226
  131.8 61.9 %copy-start.3 = (s32[1,512]{1,0:T(1,128)S(1)}, s32[1,512]{1,0:T(1,128)}, u32[]{:S(2)}) copy-start(s32[1,512]{1,0:T(1,128)} %get-tuple-element.6) | copy-start | bytes 6148
  131.8 63.4 %copy-start.1 = (bf16[512,512]{1,0:T(8,128)(2,1)S(1)}, bf16[512,512]{1,0:T(8,128)(2,1)}, u32[]{:S(2)}) copy-start(bf16[512,512]{1,0:T(8,128)(2,1)} %hidden_ref.1) | copy-start | bytes 1572868
  131.8 63.4 %copy-start.2 = (f32[512]{0:T(512)S(1)}, f32[512]{0:T(512)}, u32[]{:S(2)}) copy-start(f32[512]{0:T(512)} %param.7) | copy-start | bytes 6148
  190.9 4.3 %collective-permute-start.14 = (bf16[512,512]{1,0:T(8,128)(2,1)S(1)}, bf16[512,512]{1,0:T(8,128)(2,1)S(1)}, u32[]{:S(2)}, u32[]{:S(2)}) collective-permute-start(bf16[512,512]{1,0:T(8,128)(2,1)S(1)} %slice.4), channel_id=1, source_target_pairs={{0,1},{1,0},{2,3},{3,2},{4,5},{5,4},{6,7},{7,6},{8,9},{9,8},{10,11... | collective-permute-start | bytes 1572872 | tf_op jit(solution)/shard_map/finish/ppermute | solution.py:231

commit v6 on v5

--- a/solution.py
+++ b/solution.py
@@ -142,19 +142,25 @@
     )(where, total, *pieces, *weights)
 
 
-def route_kernel(capacity, ids_ref, rows_ref, send_ref, target_ref):
+def route_kernel(capacity, ids_ref, rows_ref, send_ref, target_ref, slot_ref):
     tokens = rows_ref.shape[0]
-    slots = send_ref.shape[0]
-    ids = ids_ref[...]
-    chosen = (lax.broadcasted_iota(jnp.int32, (slots // capacity, tokens), 0) == ids).astype(jnp.float32)
-    before = (
-        lax.broadcasted_iota(jnp.int32, (tokens, tokens), 0) < lax.broadcasted_iota(jnp.int32, (tokens, tokens), 1)
-    ).astype(jnp.bfloat16)
-    counts = jnp.dot(chosen.astype(jnp.bfloat16), before, preferred_element_type=jnp.float32)
-    earlier = jnp.sum(chosen * counts, axis=0, keepdims=True)
-    target = ids * capacity + earlier.astype(jnp.int32)
-    target_ref[...] = target
-    place = (lax.broadcasted_iota(jnp.int32, (slots, tokens), 0) == target).astype(jnp.bfloat16)
+    block = send_ref.shape[0]
+    experts = block * HALVES // capacity
+
+    @pl.when(pl.program_id(0) == 0)
+    def _():
+        ids = ids_ref[...]
+        chosen = (lax.broadcasted_iota(jnp.int32, (experts, tokens), 0) == ids).astype(jnp.float32)
+        before = (
+            lax.broadcasted_iota(jnp.int32, (tokens, tokens), 0) < lax.broadcasted_iota(jnp.int32, (tokens, tokens), 1)
+        ).astype(jnp.bfloat16)
+        counts = jnp.dot(chosen.astype(jnp.bfloat16), before, preferred_element_type=jnp.float32)
+        earlier = jnp.sum(chosen * counts, axis=0, keepdims=True)
+        slot_ref[...] = ids * capacity + earlier.astype(jnp.int32)
+        target_ref[...] = slot_ref[...]
+
+    first = pl.program_id(0) * block
+    place = (lax.broadcasted_iota(jnp.int32, (block, tokens), 0) == slot_ref[...] - first).astype(jnp.bfloat16)
     send_ref[...] = jnp.dot(place, rows_ref[...], preferred_element_type=jnp.float32).astype(send_ref.dtype)
 
 
@@ -233,7 +239,14 @@
     with jax.named_scope("route"):
         send, target = pl.pallas_call(
             functools.partial(route_kernel, capacity),
+            grid=(HALVES,),
             out_shape=[jax.ShapeDtypeStruct((slots, width), bf16), jax.ShapeDtypeStruct((1, tokens), jnp.int32)],
+            in_specs=[pl.BlockSpec((1, tokens), lambda i: (0, 0)), pl.BlockSpec((tokens, width), lambda i: (0, 0))],
+            out_specs=[
+                pl.BlockSpec((slots // HALVES, width), lambda i: (i, 0)),
+                pl.BlockSpec((1, tokens), lambda i: (0, 0)),
+            ],
+            scratch_shapes=[pltpu.VMEM((1, tokens), jnp.int32)],
         )(expert_ids.reshape(1, tokens), grad_out)
 
     with jax.named_scope("dispatch"):

time: 207 us -> 208 us (level)
  no operation moved by 1% of the time
where the time goes in v6:
time: 208 us; the launch traced here: 207 us
  blocking collectives  68.2 us (33%)
  starting transfers between devices  64.2 us (31%)
  waiting for transfers between devices  57.2 us (28%)
  Pallas kernels  13.7 us (7%)
    all_to_all x1, blocking collectives, body(): lax.all_to_all(filled, 'expert', split_axis=0, concat_axis=0, tiled=True)  59.1 us
    ppermute x12, starting transfers between devices, line(): lax.ppermute(array, 'tensor', [(a * CORES + c, b * CORES + (c ^ flip)) fo...  34.6 us
    all_to_all x1, waiting for transfers between devices, body(): lax.all_to_all(send, 'expert', split_axis=0, concat_axis=0, tiled=True)  29.7 us
    ppermute x12, waiting for transfers between devices, line(): lax.ppermute(array, 'tensor', [(a * CORES + c, b * CORES + (c ^ flip)) fo...  26.1 us
    all_to_all x1, starting transfers between devices, body(): lax.all_to_all(send, 'expert', split_axis=0, concat_axis=0, tiled=True)  22 us
    all_to_all x1, blocking collectives, body(): lax.all_to_all(parts, 'tensor', split_axis=0, concat_axis=0, tiled=True)  9.15 us
    ppermute x3, starting transfers between devices, swap(): return lax.ppermute(array, 'tensor', core_pairs)  7.55 us
    pallas_call x1, Pallas kernels, multiply_near(): pl.pallas_call(near_kernel, out_shape=jax.ShapeDtypeStruct((rows, CORES *...  6.14 us
  transfers between devices with their start and end apart: 16, of which 8 were waited for; matrix products, arithmetic and copies ran while one was open for 1% of the time, Pallas kernels for 3%

profile of v6, /device:TPU:1, one launch (start us, length us, event | category | flops | bytes accessed | tf_op | source)
XLA Modules:
  0.0 206.9 jit_solution(2151704885446160390)
XLA Ops:
  0.6 0.0 copy-start
  0.6 3.1 %route.1 = (bf16[1024,384]{1,0:T(8,128)(2,1)}, s32[1,512]{1,0:T(1,128)}) custom-call(s32[1,512]{1,0:T(1,128)} %bitcast.23, bf16[512,384]{1,0:T(8,128)(2,1)} %rows_ref.1), custom_call_target="tpu_custom_call" | custom-call | tf_op jit(solution)/shard_map/route/pallas_call | solution.py:240
  3.7 22.0 %all-to-all-start = ((bf16[64,16,384]{2,1,0:T(8,128)(2,1)}), bf16[64,16,384]{2,1,0:T(8,128)(2,1)}, u32[]{:S(2)}, u32[]{:S(2)}) async-start(bf16[64,16,384]{2,1,0:T(8,128)(2,1)} %bitcast.22), calls=%async_computation | async-start | bytes 1572864 | tf_op jit(solution)/shard_map/dispatch/all_to_all | solution.py:253
  25.7 2.9 %collective-permute-start.9 = (bf16[512,3072]{1,0:T(8,128)(2,1)}, bf16[512,3072]{1,0:T(8,128)(2,1)}, u32[]{:S(2)}, u32[]{:S(2)}) collective-permute-start(bf16[512,3072]{1,0:T(8,128)(2,1)} %bitcast.14), channel_id=1, source_target_pairs={{0,1},{1,0},{2,3},{3,2},{4,5},{5,4},{6,7},{7,6},{8,9},{9,8},{10,11... | collective-permute-start | bytes 9437192 | tf_op jit(solution)/shard_map/gather/ppermute | solution.py:237
  28.6 29.7 %all-to-all-done = bf16[64,16,384]{2,1,0:T(8,128)(2,1)} async-done(((bf16[64,16,384]{2,1,0:T(8,128)(2,1)}), bf16[64,16,384]{2,1,0:T(8,128)(2,1)}, u32[]{:S(2)}, u32[]{:S(2)}) %all-to-all-start) | async-done | bytes 786464 | tf_op jit(solution)/shard_map/dispatch/all_to_all | solution.py:253
  58.3 1.9 dynamic-slice_bitcast_fusion
  60.2 15.4 %collective-permute-start = (bf16[512,384]{1,0:T(8,128)(2,1)S(1)}, bf16[512,384]{1,0:T(8,128)(2,1)}, u32[]{:S(2)}, u32[]{:S(2)}) collective-permute-start(bf16[512,384]{1,0:T(8,128)(2,1)S(1)} %get-tuple-element.11.refs_0_), channel_id=1, source_target_pairs={{0,2},{1,3},{2,4},{3,5},{4,6},{5,7},{8,10},{9,11},{10,12},{11,13},... | collective-permute-start | bytes 1179656 | tf_op jit(solution)/shard_map/gather/ppermute | solution.py:232
  75.6 1.3 collective-permute-start.1
  76.9 7.3 %collective-permute-start.5 = (bf16[512,384]{1,0:T(8,128)(2,1)}, bf16[512,384]{1,0:T(8,128)(2,1)}, u32[]{:S(2)}, u32[]{:S(2)}) collective-permute-start(bf16[512,384]{1,0:T(8,128)(2,1)} %get-tuple-element.10), channel_id=1, source_target_pairs={{0,3},{1,2},{2,5},{3,4},{4,7},{5,6},{8,11},{9,10},{10,13},{11,12},... | collective-permute-start | bytes 1179656 | tf_op jit(solution)/shard_map/gather/ppermute | solution.py:232
  84.3 1.3 collective-permute-start.6
  85.6 0.0 collective-permute-done.refs_1_
  85.6 1.4 collective-permute-start.2
  87.0 0.0 collective-permute-done.1.refs_2_
  87.0 1.3 collective-permute-start.3
  88.3 4.0 %collective-permute-done.5.refs_6_ = bf16[512,384]{1,0:T(8,128)(2,1)} collective-permute-done((bf16[512,384]{1,0:T(8,128)(2,1)}, bf16[512,384]{1,0:T(8,128)(2,1)}, u32[]{:S(2)}, u32[]{:S(2)}) %collective-permute-start.5) | collective-permute-done | bytes 393248 | tf_op jit(solution)/shard_map/gather/ppermute | solution.py:232
  92.3 1.4 collective-permute-start.7
  93.7 4.7 %collective-permute-done.6.refs_7_ = bf16[512,384]{1,0:T(8,128)(2,1)} collective-permute-done((bf16[512,384]{1,0:T(8,128)(2,1)}, bf16[512,384]{1,0:T(8,128)(2,1)}, u32[]{:S(2)}, u32[]{:S(2)}) %collective-permute-start.6) | collective-permute-done | bytes 393248 | tf_op jit(solution)/shard_map/gather/ppermute | solution.py:232
  98.5 1.3 collective-permute-start.8
  99.8 0.0 collective-permute-done.9.refs_11_.refs_5_
  99.8 1.9 collective-permute-start.4
  101.7 0.0 collective-permute-done.2.refs_3_
  101.7 0.7 collective-permute-start.10
  102.4 1.6 collective-permute-done.3.refs_4_
  104.1 1.3 collective-permute-start.11
  105.3 0.0 collective-permute-done.7.refs_8_
  105.3 0.7 collective-permute-start.12
  106.0 6.4 %collective-permute-done.8.refs_9_ = bf16[512,384]{1,0:T(8,128)(2,1)} collective-permute-done((bf16[512,384]{1,0:T(8,128)(2,1)}, bf16[512,384]{1,0:T(8,128)(2,1)}, u32[]{:S(2)}, u32[]{:S(2)}) %collective-permute-start.8) | collective-permute-done | bytes 393248 | tf_op jit(solution)/shard_map/gather/ppermute | solution.py:232
  112.5 1.3 collective-permute-start.13
  113.8 0.1 pad_add_fusion.place_ref
  113.8 0.0 collective-permute-done.4.refs_5_
  113.8 0.0 copy-done
  113.8 6.1 %products.2.total_ref = f32[512,1024]{1,0:T(8,128)S(1)} custom-call(s32[2]{0:T(128)S(1)} %pad_add_fusion.place_ref, bf16[512,384]{1,0:T(8,128)(2,1)S(1)} %get-tuple-element.11.refs_0_, bf16[512,384]{1,0:T(8,128)(2,1)} %collective-permute-done.refs_1_, bf16[512,384]{1,0:T(8,128)(2,1)} %collective-permute-done.1.refs_2_, ...), custom_call_target="tpu_custom_call" | custom-call | flops 3221225472 | bytes 9437184 | tf_op jit(solution)/shard_map/products/pallas_call | solution.py:108
  120.0 0.0 collective-permute-done.10.refs_0_
  120.0 0.8 collective-permute-done.11.refs_1_
  120.8 0.0 collective-permute-done.12.refs_2_
  120.8 8.4 %collective-permute-done.13.refs_3_ = bf16[512,384]{1,0:T(8,128)(2,1)S(1)} collective-permute-done((bf16[512,384]{1,0:T(8,128)(2,1)}, bf16[512,384]{1,0:T(8,128)(2,1)S(1)}, u32[]{:S(2)}, u32[]{:S(2)}) %collective-permute-start.13) | collective-permute-done | bytes 393248 | tf_op jit(solution)/shard_map/gather/ppermute | solution.py:232
  129.2 2.6 %products.3 = bf16[512,1024]{1,0:T(8,128)(2,1)S(1)} custom-call(s32[2]{0:T(128)S(1)} %pad_add_fusion.place_ref, f32[512,1024]{1,0:T(8,128)S(1)} %products.2.total_ref, bf16[512,384]{1,0:T(8,128)(2,1)S(1)} %collective-permute-done.10.refs_0_, bf16[512,384]{1,0:T(8,128)(2,1)S(1)} %collective-permute-done.11.refs_1_, ...), custom_call_target="tpu_custom_call" | custom-call | flops 805306368 | bytes 4194304 | tf_op jit(solution)/shard_map/products/pallas_call | solution.py:129
  131.9 0.0 copy-start.3
  131.9 0.0 copy-start.1
  131.9 0.0 copy-start.2
  131.9 59.1 %all_to_all.29 = bf16[64,8,1024]{2,1,0:T(8,128)(2,1)S(1)} all-to-all(bf16[64,8,1024]{2,1,0:T(8,128)(2,1)S(1)} %bitcast.19), channel_id=1, replica_groups=mesh['expert'=64,'tensor'=8] {'expert'}, dimensions={0} | all-to-all | bytes 2097152 | tf_op jit(solution)/shard_map/return/all_to_all | solution.py:277
  191.0 2.8 %collective-permute-start.14 = (bf16[512,512]{1,0:T(8,128)(2,1)S(1)}, bf16[512,512]{1,0:T(8,128)(2,1)S(1)}, u32[]{:S(2)}, u32[]{:S(2)}) collective-permute-start(bf16[512,512]{1,0:T(8,128)(2,1)S(1)} %slice.4), channel_id=1, source_target_pairs={{0,1},{1,0},{2,3},{3,2},{4,5},{5,4},{6,7},{7,6},{8,9},{9,8},{10,11... | collective-permute-start | bytes 1572872 | tf_op jit(solution)/shard_map/finish/ppermute | solution.py:237
  193.8 0.0 copy-done.3
  193.9 1.5 collective-permute-done.14.across_ref
  195.3 0.0 copy-done.1
  195.3 1.8 finish.1
  197.2 9.1 %all_to_all.30 = f32[8,1,512]{2,1,0:T(1,128)S(1)} all-to-all(f32[8,1,512]{2,1,0:T(1,128)S(1)} %copy.7), channel_id=1, replica_groups=mesh['expert'=64,'tensor'=8] {'tensor'}, dimensions={0} | all-to-all | bytes 32768 | tf_op jit(solution)/shard_map/finish/all_to_all | solution.py:284
  206.3 0.6 reduce_sum.9
  (4 shorter events, 0.1 us)
Async XLA Ops:
  0.6 113.2 %copy-start = (bf16[1,512,3072]{2,1,0:T(8,128)(2,1)S(1)}, bf16[1,512,3072]{2,1,0:T(8,128)(2,1)}, u32[]{:S(2)}) copy-start(bf16[1,512,3072]{2,1,0:T(8,128)(2,1)} %param.9) | copy-start | bytes 9437188
  3.7 54.6 %all-to-all-start = ((bf16[64,16,384]{2,1,0:T(8,128)(2,1)}), bf16[64,16,384]{2,1,0:T(8,128)(2,1)}, u32[]{:S(2)}, u32[]{:S(2)}) async-start(bf16[64,16,384]{2,1,0:T(8,128)(2,1)} %bitcast.22), calls=%async_computation | async-start | bytes 1572864 | tf_op jit(solution)/shard_map/dispatch/all_to_all | solution.py:253
  25.7 74.1 %collective-permute-start.9 = (bf16[512,3072]{1,0:T(8,128)(2,1)}, bf16[512,3072]{1,0:T(8,128)(2,1)}, u32[]{:S(2)}, u32[]{:S(2)}) collective-permute-start(bf16[512,3072]{1,0:T(8,128)(2,1)} %bitcast.14), channel_id=1, source_target_pairs={{0,1},{1,0},{2,3},{3,2},{4,5},{5,4},{6,7},{7,6},{8,9},{9,8},{10,11... | collective-permute-start | bytes 9437192 | tf_op jit(solution)/shard_map/gather/ppermute | solution.py:237
  60.2 25.3 %collective-permute-start = (bf16[512,384]{1,0:T(8,128)(2,1)S(1)}, bf16[512,384]{1,0:T(8,128)(2,1)}, u32[]{:S(2)}, u32[]{:S(2)}) collective-permute-start(bf16[512,384]{1,0:T(8,128)(2,1)S(1)} %get-tuple-element.11.refs_0_), channel_id=1, source_target_pairs={{0,2},{1,3},{2,4},{3,5},{4,6},{5,7},{8,10},{9,11},{10,12},{11,13},... | collective-permute-start | bytes 1179656 | tf_op jit(solution)/shard_map/gather/ppermute | solution.py:232
  75.6 11.4 %collective-permute-start.1 = (bf16[512,384]{1,0:T(8,128)(2,1)S(1)}, bf16[512,384]{1,0:T(8,128)(2,1)}, u32[]{:S(2)}, u32[]{:S(2)}) collective-permute-start(bf16[512,384]{1,0:T(8,128)(2,1)S(1)} %get-tuple-element.11.refs_0_), channel_id=1, source_target_pairs={{2,0},{3,1},{4,2},{5,3},{6,4},{7,5},{10,8},{11,9},{12,10},{13,11},... | collective-permute-start | bytes 1179656 | tf_op jit(solution)/shard_map/gather/ppermute | solution.py:232
  76.9 15.4 %collective-permute-start.5 = (bf16[512,384]{1,0:T(8,128)(2,1)}, bf16[512,384]{1,0:T(8,128)(2,1)}, u32[]{:S(2)}, u32[]{:S(2)}) collective-permute-start(bf16[512,384]{1,0:T(8,128)(2,1)} %get-tuple-element.10), channel_id=1, source_target_pairs={{0,3},{1,2},{2,5},{3,4},{4,7},{5,6},{8,11},{9,10},{10,13},{11,12},... | collective-permute-start | bytes 1179656 | tf_op jit(solution)/shard_map/gather/ppermute | solution.py:232
  84.3 14.2 %collective-permute-start.6 = (bf16[512,384]{1,0:T(8,128)(2,1)}, bf16[512,384]{1,0:T(8,128)(2,1)}, u32[]{:S(2)}, u32[]{:S(2)}) collective-permute-start(bf16[512,384]{1,0:T(8,128)(2,1)} %get-tuple-element.10), channel_id=1, source_target_pairs={{2,1},{3,0},{4,3},{5,2},{6,5},{7,4},{10,9},{11,8},{12,11},{13,10},... | collective-permute-start | bytes 1179656 | tf_op jit(solution)/shard_map/gather/ppermute | solution.py:232
  85.6 16.1 %collective-permute-start.2 = (bf16[512,384]{1,0:T(8,128)(2,1)}, bf16[512,384]{1,0:T(8,128)(2,1)}, u32[]{:S(2)}, u32[]{:S(2)}) collective-permute-start(bf16[512,384]{1,0:T(8,128)(2,1)} %collective-permute-done.refs_1_), channel_id=1, source_target_pairs={{2,4},{3,5},{4,6},{5,7},{10,12},{11,13},{12,14},{13,15},{18,20},{1... | collective-permute-start | bytes 1179656 | tf_op jit(solution)/shard_map/gather/ppermute | solution.py:232
  87.0 17.0 %collective-permute-start.3 = (bf16[512,384]{1,0:T(8,128)(2,1)}, bf16[512,384]{1,0:T(8,128)(2,1)}, u32[]{:S(2)}, u32[]{:S(2)}) collective-permute-start(bf16[512,384]{1,0:T(8,128)(2,1)} %collective-permute-done.1.refs_2_), channel_id=1, source_target_pairs={{4,2},{5,3},{2,0},{3,1},{12,10},{13,11},{10,8},{11,9},{20,18},{21,... | collective-permute-start | bytes 1179656 | tf_op jit(solution)/shard_map/gather/ppermute | solution.py:232
  92.3 13.0 %collective-permute-start.7 = (bf16[512,384]{1,0:T(8,128)(2,1)}, bf16[512,384]{1,0:T(8,128)(2,1)}, u32[]{:S(2)}, u32[]{:S(2)}) collective-permute-start(bf16[512,384]{1,0:T(8,128)(2,1)} %collective-permute-done.5.refs_6_), channel_id=1, source_target_pairs={{2,4},{3,5},{4,6},{5,7},{10,12},{11,13},{12,14},{13,15},{18,20},{1... | collective-permute-start | bytes 1179656 | tf_op jit(solution)/shard_map/gather/ppermute | solution.py:232
  98.5 14.0 %collective-permute-start.8 = (bf16[512,384]{1,0:T(8,128)(2,1)}, bf16[512,384]{1,0:T(8,128)(2,1)}, u32[]{:S(2)}, u32[]{:S(2)}) collective-permute-start(bf16[512,384]{1,0:T(8,128)(2,1)} %collective-permute-done.6.refs_7_), channel_id=1, source_target_pairs={{4,2},{5,3},{2,0},{3,1},{12,10},{13,11},{10,8},{11,9},{20,18},{21,... | collective-permute-start | bytes 1179656 | tf_op jit(solution)/shard_map/gather/ppermute | solution.py:232
  99.8 14.1 %collective-permute-start.4 = (bf16[512,384]{1,0:T(8,128)(2,1)}, bf16[512,384]{1,0:T(8,128)(2,1)}, u32[]{:S(2)}, u32[]{:S(2)}) collective-permute-start(bf16[512,384]{1,0:T(8,128)(2,1)} %get-tuple-element.10), channel_id=1, source_target_pairs={{0,1},{1,0},{2,3},{3,2},{4,5},{5,4},{6,7},{7,6},{8,9},{9,8},{10,11... | collective-permute-start | bytes 1179656 | tf_op jit(solution)/shard_map/gather/ppermute | solution.py:237
  101.7 18.3 %collective-permute-start.10 = (bf16[512,384]{1,0:T(8,128)(2,1)}, bf16[512,384]{1,0:T(8,128)(2,1)S(1)}, u32[]{:S(2)}, u32[]{:S(2)}) collective-permute-start(bf16[512,384]{1,0:T(8,128)(2,1)} %collective-permute-done.2.refs_3_), channel_id=1, source_target_pairs={{4,6},{5,7},{12,14},{13,15},{20,22},{21,23},{28,30},{29,31},{36,38... | collective-permute-start | bytes 1179656 | tf_op jit(solution)/shard_map/gather/ppermute | solution.py:232
  104.1 16.7 %collective-permute-start.11 = (bf16[512,384]{1,0:T(8,128)(2,1)}, bf16[512,384]{1,0:T(8,128)(2,1)S(1)}, u32[]{:S(2)}, u32[]{:S(2)}) collective-permute-start(bf16[512,384]{1,0:T(8,128)(2,1)} %collective-permute-done.3.refs_4_), channel_id=1, source_target_pairs={{2,0},{3,1},{10,8},{11,9},{18,16},{19,17},{26,24},{27,25},{34,32},... | collective-permute-start | bytes 1179656 | tf_op jit(solution)/shard_map/gather/ppermute | solution.py:232
  105.3 15.5 %collective-permute-start.12 = (bf16[512,384]{1,0:T(8,128)(2,1)}, bf16[512,384]{1,0:T(8,128)(2,1)S(1)}, u32[]{:S(2)}, u32[]{:S(2)}) collective-permute-start(bf16[512,384]{1,0:T(8,128)(2,1)} %collective-permute-done.7.refs_8_), channel_id=1, source_target_pairs={{4,6},{5,7},{12,14},{13,15},{20,22},{21,23},{28,30},{29,31},{36,38... | collective-permute-start | bytes 1179656 | tf_op jit(solution)/shard_map/gather/ppermute | solution.py:232
  112.5 16.7 %collective-permute-start.13 = (bf16[512,384]{1,0:T(8,128)(2,1)}, bf16[512,384]{1,0:T(8,128)(2,1)S(1)}, u32[]{:S(2)}, u32[]{:S(2)}) collective-permute-start(bf16[512,384]{1,0:T(8,128)(2,1)} %collective-permute-done.8.refs_9_), channel_id=1, source_target_pairs={{2,0},{3,1},{10,8},{11,9},{18,16},{19,17},{26,24},{27,25},{34,32},... | collective-permute-start | bytes 1179656 | tf_op jit(solution)/shard_map/gather/ppermute | solution.py:232
  131.9 61.9 %copy-start.3 = (s32[1,512]{1,0:T(1,128)S(1)}, s32[1,512]{1,0:T(1,128)}, u32[]{:S(2)}) copy-start(s32[1,512]{1,0:T(1,128)} %get-tuple-element.6) | copy-start | bytes 6148
  131.9 63.4 %copy-start.1 = (bf16[512,512]{1,0:T(8,128)(2,1)S(1)}, bf16[512,512]{1,0:T(8,128)(2,1)}, u32[]{:S(2)}) copy-start(bf16[512,512]{1,0:T(8,128)(2,1)} %hidden_ref.1) | copy-start | bytes 1572868
  131.9 63.4 %copy-start.2 = (f32[512]{0:T(512)S(1)}, f32[512]{0:T(512)}, u32[]{:S(2)}) copy-start(f32[512]{0:T(512)} %param.7) | copy-start | bytes 6148
  191.0 4.3 %collective-permute-start.14 = (bf16[512,512]{1,0:T(8,128)(2,1)S(1)}, bf16[512,512]{1,0:T(8,128)(2,1)S(1)}, u32[]{:S(2)}, u32[]{:S(2)}) collective-permute-start(bf16[512,512]{1,0:T(8,128)(2,1)S(1)} %slice.4), channel_id=1, source_target_pairs={{0,1},{1,0},{2,3},{3,2},{4,5},{5,4},{6,7},{7,6},{8,9},{9,8},{10,11... | collective-permute-start | bytes 1572872 | tf_op jit(solution)/shard_map/finish/ppermute | solution.py:237

commit v7 on v5

--- a/solution.py
+++ b/solution.py
@@ -76,21 +76,26 @@
         part = sources[n].at[:, pl.ds(pl.multiple_of(block * width, 128), width)]
         return pltpu.make_async_copy(part, weights.at[h, n], sems.at[h, n])
 
-    @pl.when(end)
+    step = pl.program_id(0)
+
+    @pl.when(end & (step == 0))
     def _():
-        last = [jnp.where(chip == 0, pieces[2 * h + 1][...], pieces[2 * h][...]) for h in range(HALVES)]
         for n in range(CORES):
             for h in range(HALVES):
                 weight_copy(h, n).start()
-        for n in range(CORES):
-            here = slice(n * hidden, (n + 1) * hidden)
-            more = total_ref[:, here]
+
+    for n in range(CORES):
+
+        @pl.when(end & (step == n))
+        def _():
+            more = total_ref[...]
             for h in range(HALVES):
+                last = jnp.where(chip == 0, pieces[2 * h + 1][...], pieces[2 * h][...])
                 weight_copy(h, n).wait()
                 more = more + lax.dot_general(
-                    last[h], weights[h, n], (((1,), (1,)), ((), ())), preferred_element_type=jnp.float32
+                    last, weights[h, n], (((1,), (1,)), ((), ())), preferred_element_type=jnp.float32
                 )
-            out[:, here] = more.astype(out.dtype)
+            out[...] = more.astype(out.dtype)
 
     @pl.when(jnp.logical_not(end))
     def _():
@@ -124,13 +129,16 @@
 
 
 def multiply_last(where, chips, total, pieces, weights):
-    width = pieces[0].shape[1]
+    rows, width = pieces[0].shape
     hidden = weights[0].shape[0]
     return pl.pallas_call(
         functools.partial(last_kernel, chips),
         out_shape=jax.ShapeDtypeStruct(total.shape, jnp.bfloat16),
-        in_specs=[SMEM] + [VMEM] * (1 + 2 * HALVES) + [HBM] * CORES,
-        out_specs=VMEM,
+        grid=(CORES,),
+        in_specs=[SMEM, pl.BlockSpec((rows, hidden), lambda n: (0, n))]
+        + [pl.BlockSpec((rows, width), lambda n: (0, 0))] * (2 * HALVES)
+        + [HBM] * CORES,
+        out_specs=pl.BlockSpec((rows, hidden), lambda n: (0, n)),
         scratch_shapes=[
             pltpu.VMEM((HALVES, CORES, hidden, width), jnp.bfloat16),
             pltpu.SemaphoreType.DMA((HALVES, CORES)),

time: 207 us -> 208 us (level)
  no operation moved by 1% of the time
where the time goes in v7:
time: 208 us; the launch traced here: 207 us
  blocking collectives  68.2 us (33%)
  starting transfers between devices  64.2 us (31%)
  waiting for transfers between devices  57.2 us (28%)
  Pallas kernels  13.8 us (7%)
    all_to_all x1, blocking collectives, body(): lax.all_to_all(filled, 'expert', split_axis=0, concat_axis=0, tiled=True)  59 us
    ppermute x12, starting transfers between devices, line(): lax.ppermute(array, 'tensor', [(a * CORES + c, b * CORES + (c ^ flip)) fo...  34.6 us
    all_to_all x1, waiting for transfers between devices, body(): lax.all_to_all(send, 'expert', split_axis=0, concat_axis=0, tiled=True)  29.7 us
    ppermute x12, waiting for transfers between devices, line(): lax.ppermute(array, 'tensor', [(a * CORES + c, b * CORES + (c ^ flip)) fo...  26.1 us
    all_to_all x1, starting transfers between devices, body(): lax.all_to_all(send, 'expert', split_axis=0, concat_axis=0, tiled=True)  22 us
    all_to_all x1, blocking collectives, body(): lax.all_to_all(parts, 'tensor', split_axis=0, concat_axis=0, tiled=True)  9.2 us
    ppermute x3, starting transfers between devices, swap(): return lax.ppermute(array, 'tensor', core_pairs)  7.55 us
    pallas_call x1, Pallas kernels, multiply_near(): pl.pallas_call(near_kernel, out_shape=jax.ShapeDtypeStruct((rows, CORES *...  6.14 us
  transfers between devices with their start and end apart: 16, of which 8 were waited for; matrix products, arithmetic and copies ran while one was open for 1% of the time, Pallas kernels for 3%

profile of v7, /device:TPU:1, one launch (start us, length us, event | category | flops | bytes accessed | tf_op | source)
XLA Modules:
  0.0 207.1 jit_solution(8579452924471838779)
XLA Ops:
  0.6 0.0 copy-start
  0.6 3.0 %route.1 = (bf16[1024,384]{1,0:T(8,128)(2,1)}, s32[1,512]{1,0:T(1,128)}) custom-call(s32[1,512]{1,0:T(1,128)} %bitcast.23, bf16[512,384]{1,0:T(8,128)(2,1)} %rows_ref.1), custom_call_target="tpu_custom_call" | custom-call | tf_op jit(solution)/shard_map/route/pallas_call | solution.py:242
  3.6 22.0 %all-to-all-start = ((bf16[64,16,384]{2,1,0:T(8,128)(2,1)}), bf16[64,16,384]{2,1,0:T(8,128)(2,1)}, u32[]{:S(2)}, u32[]{:S(2)}) async-start(bf16[64,16,384]{2,1,0:T(8,128)(2,1)} %bitcast.22), calls=%async_computation | async-start | bytes 1572864 | tf_op jit(solution)/shard_map/dispatch/all_to_all | solution.py:248
  25.6 2.9 %collective-permute-start.9 = (bf16[512,3072]{1,0:T(8,128)(2,1)}, bf16[512,3072]{1,0:T(8,128)(2,1)}, u32[]{:S(2)}, u32[]{:S(2)}) collective-permute-start(bf16[512,3072]{1,0:T(8,128)(2,1)} %bitcast.14), channel_id=1, source_target_pairs={{0,1},{1,0},{2,3},{3,2},{4,5},{5,4},{6,7},{7,6},{8,9},{9,8},{10,11... | collective-permute-start | bytes 9437192 | tf_op jit(solution)/shard_map/gather/ppermute | solution.py:239
  28.5 29.7 %all-to-all-done = bf16[64,16,384]{2,1,0:T(8,128)(2,1)} async-done(((bf16[64,16,384]{2,1,0:T(8,128)(2,1)}), bf16[64,16,384]{2,1,0:T(8,128)(2,1)}, u32[]{:S(2)}, u32[]{:S(2)}) %all-to-all-start) | async-done | bytes 786464 | tf_op jit(solution)/shard_map/dispatch/all_to_all | solution.py:248
  58.2 1.9 dynamic-slice_bitcast_fusion
  60.1 15.2 %collective-permute-start = (bf16[512,384]{1,0:T(8,128)(2,1)S(1)}, bf16[512,384]{1,0:T(8,128)(2,1)}, u32[]{:S(2)}, u32[]{:S(2)}) collective-permute-start(bf16[512,384]{1,0:T(8,128)(2,1)S(1)} %get-tuple-element.11.refs_0_), channel_id=1, source_target_pairs={{0,2},{1,3},{2,4},{3,5},{4,6},{5,7},{8,10},{9,11},{10,12},{11,13},... | collective-permute-start | bytes 1179656 | tf_op jit(solution)/shard_map/gather/ppermute | solution.py:234
  75.3 1.3 collective-permute-start.1
  76.6 7.6 %collective-permute-start.5 = (bf16[512,384]{1,0:T(8,128)(2,1)}, bf16[512,384]{1,0:T(8,128)(2,1)}, u32[]{:S(2)}, u32[]{:S(2)}) collective-permute-start(bf16[512,384]{1,0:T(8,128)(2,1)} %get-tuple-element.10), channel_id=1, source_target_pairs={{0,3},{1,2},{2,5},{3,4},{4,7},{5,6},{8,11},{9,10},{10,13},{11,12},... | collective-permute-start | bytes 1179656 | tf_op jit(solution)/shard_map/gather/ppermute | solution.py:234
  84.2 1.3 collective-permute-start.6
  85.5 0.0 collective-permute-done.refs_1_
  85.5 1.4 collective-permute-start.2
  86.9 0.0 collective-permute-done.1.refs_2_
  86.9 1.3 collective-permute-start.3
  88.2 3.8 %collective-permute-done.5.refs_6_ = bf16[512,384]{1,0:T(8,128)(2,1)} collective-permute-done((bf16[512,384]{1,0:T(8,128)(2,1)}, bf16[512,384]{1,0:T(8,128)(2,1)}, u32[]{:S(2)}, u32[]{:S(2)}) %collective-permute-start.5) | collective-permute-done | bytes 393248 | tf_op jit(solution)/shard_map/gather/ppermute | solution.py:234
  92.0 1.4 collective-permute-start.7
  93.4 4.5 %collective-permute-done.6.refs_7_ = bf16[512,384]{1,0:T(8,128)(2,1)} collective-permute-done((bf16[512,384]{1,0:T(8,128)(2,1)}, bf16[512,384]{1,0:T(8,128)(2,1)}, u32[]{:S(2)}, u32[]{:S(2)}) %collective-permute-start.6) | collective-permute-done | bytes 393248 | tf_op jit(solution)/shard_map/gather/ppermute | solution.py:234
  97.9 1.3 collective-permute-start.8
  99.2 0.0 collective-permute-done.9.refs_11_.refs_5_
  99.2 1.9 collective-permute-start.4
  101.2 0.0 collective-permute-done.2.refs_3_
  101.2 0.7 collective-permute-start.10
  101.9 2.1 %collective-permute-done.3.refs_4_ = bf16[512,384]{1,0:T(8,128)(2,1)} collective-permute-done((bf16[512,384]{1,0:T(8,128)(2,1)}, bf16[512,384]{1,0:T(8,128)(2,1)}, u32[]{:S(2)}, u32[]{:S(2)}) %collective-permute-start.3) | collective-permute-done | bytes 393248 | tf_op jit(solution)/shard_map/gather/ppermute | solution.py:234
  103.9 1.3 collective-permute-start.11
  105.2 0.0 collective-permute-done.7.refs_8_
  105.2 0.7 collective-permute-start.12
  105.9 6.4 %collective-permute-done.8.refs_9_ = bf16[512,384]{1,0:T(8,128)(2,1)} collective-permute-done((bf16[512,384]{1,0:T(8,128)(2,1)}, bf16[512,384]{1,0:T(8,128)(2,1)}, u32[]{:S(2)}, u32[]{:S(2)}) %collective-permute-start.8) | collective-permute-done | bytes 393248 | tf_op jit(solution)/shard_map/gather/ppermute | solution.py:234
  112.4 1.3 collective-permute-start.13
  113.7 0.1 pad_add_fusion.place_ref
  113.7 0.0 collective-permute-done.4.refs_5_
  113.7 0.0 copy-done
  113.7 6.1 %products.2.total_ref = f32[512,1024]{1,0:T(8,128)S(1)} custom-call(s32[2]{0:T(128)S(1)} %pad_add_fusion.place_ref, bf16[512,384]{1,0:T(8,128)(2,1)S(1)} %get-tuple-element.11.refs_0_, bf16[512,384]{1,0:T(8,128)(2,1)} %collective-permute-done.refs_1_, bf16[512,384]{1,0:T(8,128)(2,1)} %collective-permute-done.1.refs_2_, ...), custom_call_target="tpu_custom_call" | custom-call | flops 3221225472 | bytes 9437184 | tf_op jit(solution)/shard_map/products/pallas_call | solution.py:113
  119.9 0.0 collective-permute-done.10.refs_0_
  119.9 0.8 collective-permute-done.11.refs_1_
  120.7 0.0 collective-permute-done.12.refs_2_
  120.7 8.4 %collective-permute-done.13.refs_3_ = bf16[512,384]{1,0:T(8,128)(2,1)S(1)} collective-permute-done((bf16[512,384]{1,0:T(8,128)(2,1)}, bf16[512,384]{1,0:T(8,128)(2,1)S(1)}, u32[]{:S(2)}, u32[]{:S(2)}) %collective-permute-start.13) | collective-permute-done | bytes 393248 | tf_op jit(solution)/shard_map/gather/ppermute | solution.py:234
  129.1 2.9 %products.3 = bf16[512,1024]{1,0:T(8,128)(2,1)S(1)} custom-call(s32[2]{0:T(128)S(1)} %pad_add_fusion.place_ref, f32[512,1024]{1,0:T(8,128)S(1)} %products.2.total_ref, bf16[512,384]{1,0:T(8,128)(2,1)S(1)} %collective-permute-done.10.refs_0_, bf16[512,384]{1,0:T(8,128)(2,1)S(1)} %collective-permute-done.11.refs_1_, ...), custom_call_target="tpu_custom_call" | custom-call | flops 805306368 | bytes 4194304 | tf_op jit(solution)/shard_map/products/pallas_call | solution.py:134
  132.0 0.0 copy-start.3
  132.0 0.0 copy-start.1
  132.1 0.0 copy-start.2
  132.1 59.0 %all_to_all.29 = bf16[64,8,1024]{2,1,0:T(8,128)(2,1)S(1)} all-to-all(bf16[64,8,1024]{2,1,0:T(8,128)(2,1)S(1)} %bitcast.19), channel_id=1, replica_groups=mesh['expert'=64,'tensor'=8] {'expert'}, dimensions={0} | all-to-all | bytes 2097152 | tf_op jit(solution)/shard_map/return/all_to_all | solution.py:272
  191.1 2.8 %collective-permute-start.14 = (bf16[512,512]{1,0:T(8,128)(2,1)S(1)}, bf16[512,512]{1,0:T(8,128)(2,1)S(1)}, u32[]{:S(2)}, u32[]{:S(2)}) collective-permute-start(bf16[512,512]{1,0:T(8,128)(2,1)S(1)} %slice.4), channel_id=1, source_target_pairs={{0,1},{1,0},{2,3},{3,2},{4,5},{5,4},{6,7},{7,6},{8,9},{9,8},{10,11... | collective-permute-start | bytes 1572872 | tf_op jit(solution)/shard_map/finish/ppermute | solution.py:239
  193.9 0.0 copy-done.3
  193.9 1.5 collective-permute-done.14.across_ref
  195.4 0.0 copy-done.1
  195.4 1.8 finish.1
  197.3 9.2 %all_to_all.30 = f32[8,1,512]{2,1,0:T(1,128)S(1)} all-to-all(f32[8,1,512]{2,1,0:T(1,128)S(1)} %copy.7), channel_id=1, replica_groups=mesh['expert'=64,'tensor'=8] {'tensor'}, dimensions={0} | all-to-all | bytes 32768 | tf_op jit(solution)/shard_map/finish/all_to_all | solution.py:279
  206.5 0.6 reduce_sum.9
  (4 shorter events, 0.1 us)
Async XLA Ops:
  0.6 113.1 %copy-start = (bf16[1,512,3072]{2,1,0:T(8,128)(2,1)S(1)}, bf16[1,512,3072]{2,1,0:T(8,128)(2,1)}, u32[]{:S(2)}) copy-start(bf16[1,512,3072]{2,1,0:T(8,128)(2,1)} %param.9) | copy-start | bytes 9437188
  3.6 54.6 %all-to-all-start = ((bf16[64,16,384]{2,1,0:T(8,128)(2,1)}), bf16[64,16,384]{2,1,0:T(8,128)(2,1)}, u32[]{:S(2)}, u32[]{:S(2)}) async-start(bf16[64,16,384]{2,1,0:T(8,128)(2,1)} %bitcast.22), calls=%async_computation | async-start | bytes 1572864 | tf_op jit(solution)/shard_map/dispatch/all_to_all | solution.py:248
  25.6 73.6 %collective-permute-start.9 = (bf16[512,3072]{1,0:T(8,128)(2,1)}, bf16[512,3072]{1,0:T(8,128)(2,1)}, u32[]{:S(2)}, u32[]{:S(2)}) collective-permute-start(bf16[512,3072]{1,0:T(8,128)(2,1)} %bitcast.14), channel_id=1, source_target_pairs={{0,1},{1,0},{2,3},{3,2},{4,5},{5,4},{6,7},{7,6},{8,9},{9,8},{10,11... | collective-permute-start | bytes 9437192 | tf_op jit(solution)/shard_map/gather/ppermute | solution.py:239
  60.1 25.3 %collective-permute-start = (bf16[512,384]{1,0:T(8,128)(2,1)S(1)}, bf16[512,384]{1,0:T(8,128)(2,1)}, u32[]{:S(2)}, u32[]{:S(2)}) collective-permute-start(bf16[512,384]{1,0:T(8,128)(2,1)S(1)} %get-tuple-element.11.refs_0_), channel_id=1, source_target_pairs={{0,2},{1,3},{2,4},{3,5},{4,6},{5,7},{8,10},{9,11},{10,12},{11,13},... | collective-permute-start | bytes 1179656 | tf_op jit(solution)/shard_map/gather/ppermute | solution.py:234
  75.3 11.6 %collective-permute-start.1 = (bf16[512,384]{1,0:T(8,128)(2,1)S(1)}, bf16[512,384]{1,0:T(8,128)(2,1)}, u32[]{:S(2)}, u32[]{:S(2)}) collective-permute-start(bf16[512,384]{1,0:T(8,128)(2,1)S(1)} %get-tuple-element.11.refs_0_), channel_id=1, source_target_pairs={{2,0},{3,1},{4,2},{5,3},{6,4},{7,5},{10,8},{11,9},{12,10},{13,11},... | collective-permute-start | bytes 1179656 | tf_op jit(solution)/shard_map/gather/ppermute | solution.py:234
  76.6 15.4 %collective-permute-start.5 = (bf16[512,384]{1,0:T(8,128)(2,1)}, bf16[512,384]{1,0:T(8,128)(2,1)}, u32[]{:S(2)}, u32[]{:S(2)}) collective-permute-start(bf16[512,384]{1,0:T(8,128)(2,1)} %get-tuple-element.10), channel_id=1, source_target_pairs={{0,3},{1,2},{2,5},{3,4},{4,7},{5,6},{8,11},{9,10},{10,13},{11,12},... | collective-permute-start | bytes 1179656 | tf_op jit(solution)/shard_map/gather/ppermute | solution.py:234
  84.2 13.7 %collective-permute-start.6 = (bf16[512,384]{1,0:T(8,128)(2,1)}, bf16[512,384]{1,0:T(8,128)(2,1)}, u32[]{:S(2)}, u32[]{:S(2)}) collective-permute-start(bf16[512,384]{1,0:T(8,128)(2,1)} %get-tuple-element.10), channel_id=1, source_target_pairs={{2,1},{3,0},{4,3},{5,2},{6,5},{7,4},{10,9},{11,8},{12,11},{13,10},... | collective-permute-start | bytes 1179656 | tf_op jit(solution)/shard_map/gather/ppermute | solution.py:234
  85.5 15.7 %collective-permute-start.2 = (bf16[512,384]{1,0:T(8,128)(2,1)}, bf16[512,384]{1,0:T(8,128)(2,1)}, u32[]{:S(2)}, u32[]{:S(2)}) collective-permute-start(bf16[512,384]{1,0:T(8,128)(2,1)} %collective-permute-done.refs_1_), channel_id=1, source_target_pairs={{2,4},{3,5},{4,6},{5,7},{10,12},{11,13},{12,14},{13,15},{18,20},{1... | collective-permute-start | bytes 1179656 | tf_op jit(solution)/shard_map/gather/ppermute | solution.py:234
  86.9 17.0 %collective-permute-start.3 = (bf16[512,384]{1,0:T(8,128)(2,1)}, bf16[512,384]{1,0:T(8,128)(2,1)}, u32[]{:S(2)}, u32[]{:S(2)}) collective-permute-start(bf16[512,384]{1,0:T(8,128)(2,1)} %collective-permute-done.1.refs_2_), channel_id=1, source_target_pairs={{4,2},{5,3},{2,0},{3,1},{12,10},{13,11},{10,8},{11,9},{20,18},{21,... | collective-permute-start | bytes 1179656 | tf_op jit(solution)/shard_map/gather/ppermute | solution.py:234
  92.0 13.2 %collective-permute-start.7 = (bf16[512,384]{1,0:T(8,128)(2,1)}, bf16[512,384]{1,0:T(8,128)(2,1)}, u32[]{:S(2)}, u32[]{:S(2)}) collective-permute-start(bf16[512,384]{1,0:T(8,128)(2,1)} %collective-permute-done.5.refs_6_), channel_id=1, source_target_pairs={{2,4},{3,5},{4,6},{5,7},{10,12},{11,13},{12,14},{13,15},{18,20},{1... | collective-permute-start | bytes 1179656 | tf_op jit(solution)/shard_map/gather/ppermute | solution.py:234
  97.9 14.5 %collective-permute-start.8 = (bf16[512,384]{1,0:T(8,128)(2,1)}, bf16[512,384]{1,0:T(8,128)(2,1)}, u32[]{:S(2)}, u32[]{:S(2)}) collective-permute-start(bf16[512,384]{1,0:T(8,128)(2,1)} %collective-permute-done.6.refs_7_), channel_id=1, source_target_pairs={{4,2},{5,3},{2,0},{3,1},{12,10},{13,11},{10,8},{11,9},{20,18},{21,... | collective-permute-start | bytes 1179656 | tf_op jit(solution)/shard_map/gather/ppermute | solution.py:234
  99.2 14.5 %collective-permute-start.4 = (bf16[512,384]{1,0:T(8,128)(2,1)}, bf16[512,384]{1,0:T(8,128)(2,1)}, u32[]{:S(2)}, u32[]{:S(2)}) collective-permute-start(bf16[512,384]{1,0:T(8,128)(2,1)} %get-tuple-element.10), channel_id=1, source_target_pairs={{0,1},{1,0},{2,3},{3,2},{4,5},{5,4},{6,7},{7,6},{8,9},{9,8},{10,11... | collective-permute-start | bytes 1179656 | tf_op jit(solution)/shard_map/gather/ppermute | solution.py:239
  101.2 18.7 %collective-permute-start.10 = (bf16[512,384]{1,0:T(8,128)(2,1)}, bf16[512,384]{1,0:T(8,128)(2,1)S(1)}, u32[]{:S(2)}, u32[]{:S(2)}) collective-permute-start(bf16[512,384]{1,0:T(8,128)(2,1)} %collective-permute-done.2.refs_3_), channel_id=1, source_target_pairs={{4,6},{5,7},{12,14},{13,15},{20,22},{21,23},{28,30},{29,31},{36,38... | collective-permute-start | bytes 1179656 | tf_op jit(solution)/shard_map/gather/ppermute | solution.py:234
  103.9 16.7 %collective-permute-start.11 = (bf16[512,384]{1,0:T(8,128)(2,1)}, bf16[512,384]{1,0:T(8,128)(2,1)S(1)}, u32[]{:S(2)}, u32[]{:S(2)}) collective-permute-start(bf16[512,384]{1,0:T(8,128)(2,1)} %collective-permute-done.3.refs_4_), channel_id=1, source_target_pairs={{2,0},{3,1},{10,8},{11,9},{18,16},{19,17},{26,24},{27,25},{34,32},... | collective-permute-start | bytes 1179656 | tf_op jit(solution)/shard_map/gather/ppermute | solution.py:234
  105.2 15.5 %collective-permute-start.12 = (bf16[512,384]{1,0:T(8,128)(2,1)}, bf16[512,384]{1,0:T(8,128)(2,1)S(1)}, u32[]{:S(2)}, u32[]{:S(2)}) collective-permute-start(bf16[512,384]{1,0:T(8,128)(2,1)} %collective-permute-done.7.refs_8_), channel_id=1, source_target_pairs={{4,6},{5,7},{12,14},{13,15},{20,22},{21,23},{28,30},{29,31},{36,38... | collective-permute-start | bytes 1179656 | tf_op jit(solution)/shard_map/gather/ppermute | solution.py:234
  112.4 16.7 %collective-permute-start.13 = (bf16[512,384]{1,0:T(8,128)(2,1)}, bf16[512,384]{1,0:T(8,128)(2,1)S(1)}, u32[]{:S(2)}, u32[]{:S(2)}) collective-permute-start(bf16[512,384]{1,0:T(8,128)(2,1)} %collective-permute-done.8.refs_9_), channel_id=1, source_target_pairs={{2,0},{3,1},{10,8},{11,9},{18,16},{19,17},{26,24},{27,25},{34,32},... | collective-permute-start | bytes 1179656 | tf_op jit(solution)/shard_map/gather/ppermute | solution.py:234
  132.0 61.9 %copy-start.3 = (s32[1,512]{1,0:T(1,128)S(1)}, s32[1,512]{1,0:T(1,128)}, u32[]{:S(2)}) copy-start(s32[1,512]{1,0:T(1,128)} %get-tuple-element.6) | copy-start | bytes 6148
  132.0 63.4 %copy-start.1 = (bf16[512,512]{1,0:T(8,128)(2,1)S(1)}, bf16[512,512]{1,0:T(8,128)(2,1)}, u32[]{:S(2)}) copy-start(bf16[512,512]{1,0:T(8,128)(2,1)} %hidden_ref.1) | copy-start | bytes 1572868
  132.1 63.4 %copy-start.2 = (f32[512]{0:T(512)S(1)}, f32[512]{0:T(512)}, u32[]{:S(2)}) copy-start(f32[512]{0:T(512)} %param.7) | copy-start | bytes 6148
  191.1 4.3 %collective-permute-start.14 = (bf16[512,512]{1,0:T(8,128)(2,1)S(1)}, bf16[512,512]{1,0:T(8,128)(2,1)S(1)}, u32[]{:S(2)}, u32[]{:S(2)}) collective-permute-start(bf16[512,512]{1,0:T(8,128)(2,1)S(1)} %slice.4), channel_id=1, source_target_pairs={{0,1},{1,0},{2,3},{3,2},{4,5},{5,4},{6,7},{7,6},{8,9},{9,8},{10,11... | collective-permute-start | bytes 1572872 | tf_op jit(solution)/shard_map/finish/ppermute | solution.py:239
